TPU v7x, 32 devices: a whole 2x2x4 slice. The times are simulated.
32 devices in a mesh: seq: 8 (over z, y), fsdp: 4 (over x, core).
Axes of the slice: x: 2, y: 2, z: 4, core: 2. Of those that a mesh axis runs over, the one named last changes fastest.
Arguments:
- incoming_symbols: bfloat16 [4, 2048, 1024], P('fsdp', 'seq'), may hold values from -6 to 6
- downstream_slope: bfloat16 [4, 2048, 1024], P('fsdp', 'seq'), may hold values from -6 to 6
- sequence_extents: int32 [4, 8], P('fsdp'), may hold values from 0 to 2046, as said below
- mixer_lookup_map: bfloat16 [1024, 1024], P('fsdp'), may hold values from -0.1875 to 0.1875
- mixer_payload_map: bfloat16 [1024, 1024], P('fsdp'), may hold values from -0.1875 to 0.1875
- mixer_accepting_map: bfloat16 [1024, 1024], P('fsdp'), may hold values from -0.1875 to 0.1875
- mixer_emitted_map: bfloat16 [1024, 1024], P('fsdp'), may hold values from -0.375 to 0.375
- feedforward_lookup_map: bfloat16 [1024, 4096], P('fsdp'), may hold values from -0.1875 to 0.1875
- feedforward_payload_map: bfloat16 [4096, 1024], P('fsdp'), may hold values from -0.09375 to 0.09375
- feedforward_accepting_map: bfloat16 [1024, 1024], P('fsdp'), may hold values from -0.1875 to 0.1875
- prime_normalize_gain: float32 [1024], replicated, may hold values from 0.5 to 1.5
- prime_normalize_bias: float32 [1024], replicated, may hold values from -1.5 to 1.5
- later_normalize_gain: float32 [1024], replicated, may hold values from 0.5 to 1.5
- later_normalize_bias: float32 [1024], replicated, may hold values from -1.5 to 1.5
- mixer_lookup_shiftmix: float32 [1024], replicated, may hold values from 0.1 to 0.9
- mixer_payload_shiftmix: float32 [1024], replicated, may hold values from 0.1 to 0.9
- mixer_accepting_shiftmix: float32 [1024], replicated, may hold values from 0.1 to 0.9
- feedforward_lookup_shiftmix: float32 [1024], replicated, may hold values from 0.1 to 0.9
- feedforward_accepting_shiftmix: float32 [1024], replicated, may hold values from 0.1 to 0.9
- channel_shrink_rate: float32 [1024], replicated, may hold values from -7 to -3
- newest_boost: float32 [1024], replicated, may hold values from -1 to 1
Outputs:
- mixed: bfloat16 [4, 2048, 1024], P('fsdp', 'seq')
- tokens_grad: bfloat16 [4, 2048, 1024], P('fsdp', 'seq')
- att_key_grad: float32 [1024, 1024], P(('seq', 'fsdp'))
- att_value_grad: float32 [1024, 1024], P(('seq', 'fsdp'))
- att_recept_grad: float32 [1024, 1024], P(('seq', 'fsdp'))
- att_output_grad: float32 [1024, 1024], P(('seq', 'fsdp'))
- ffn_key_grad: float32 [1024, 4096], P(('seq', 'fsdp'))
- ffn_value_grad: float32 [4096, 1024], P(('seq', 'fsdp'))
- ffn_recept_grad: float32 [1024, 1024], P(('seq', 'fsdp'))
- first_gain_grad: float32 [1024], P(('seq', 'fsdp'))
- first_bias_grad: float32 [1024], P(('seq', 'fsdp'))
- derivative_post_scale_amplitude: float32 [1024], P(('seq', 'fsdp'))
- second_bias_grad: float32 [1024], P(('seq', 'fsdp'))
- mix_key_grad: float32 [1024], P(('seq', 'fsdp'))
- mix_value_grad: float32 [1024], P(('seq', 'fsdp'))
- mix_recept_grad: float32 [1024], P(('seq', 'fsdp'))
- ffn_mix_key_grad: float32 [1024], P(('seq', 'fsdp'))
- ffn_mix_recept_grad: float32 [1024], P(('seq', 'fsdp'))
- time_decay_grad: float32 [1024], P(('seq', 'fsdp'))
- time_first_grad: float32 [1024], P(('seq', 'fsdp'))
Inputs may be any that keep to these rules, and one draw needn't show every extreme that they name: `sequence_extents`: row g lists three positive sequence lengths summing to 2048, then zeros; two of them are under 256 / 2. In some group both of these are 1.
All inputs are finite; a program needn't handle non-finite values.
Results may differ from a plain program's by a relative error of at most 0.02.
Values may be sent and summed in bfloat16 or wider, within the bound.
No kernel may reach another device: no remote copies, remote signals or barrier semaphores. Data moves between devices by JAX's collectives and lax.ppermute only.
A program may use at most 256 MiB of HBM per device.

v0:
```python
from functools import partial

import jax
import jax.numpy as jnp
from jax import lax
from jax.sharding import PartitionSpec as P

WKV_BLOCK = 128


norm_eps = 1e-05


def passed_along(value, axis, steps):
    count = lax.axis_size(axis)
    initial, last = (max(0, -steps), min(count, count - steps))
    return lax.ppermute(value, axis, [(source, source + steps) for source in range(initial, last)])


def layer_norm(hidden_track, gain_vec, bias_vec):
    centred = hidden_track - jnp.mean(hidden_track, axis=-1, keepdims=True)
    spread = jnp.mean(centred * centred, axis=-1, keepdims=True)
    return centred * lax.rsqrt(spread + norm_eps) * gain_vec + bias_vec


def shift_mix(current, previous, indicator_records, weights):
    retain = 1.0 - indicator_records.astype(jnp.float32)[:, None]
    shifted = jnp.concatenate([previous, current[:-1]], axis=0) * retain
    return tuple((current * weight + shifted * (1.0 - weight) for weight in weights))


def token_starts(sequence_extents, positions):
    begins = jnp.cumsum(sequence_extents, axis=-1) - sequence_extents
    start_marks = (begins[..., :, None] == positions) & (sequence_extents[..., :, None] > 0)
    return jnp.any(start_marks, axis=-2)


def link_states(earlier, later):
    return (earlier[0] * later[0], later[0] * earlier[1] + later[1])


def recurrent_mean_here_device(
    lookup_records,
    payload_records,
    shrink_learned,
    extra_learned,
    handed_forward,
    indicator_records,
):
    row_count, col_count = lookup_records.shape
    span_rows = min(WKV_BLOCK, row_count)
    block_count = row_count // span_rows
    decay_rate = jnp.exp(jnp.concatenate([shrink_learned, shrink_learned]))
    additional_first_reinforcement = jnp.exp(jnp.concatenate([extra_learned, extra_learned]))
    powered_couplings = jnp.exp(lookup_records)
    supplied_tokens_stream = jnp.concatenate(
        [powered_couplings * payload_records, powered_couplings], axis=1
    ).reshape(block_count, span_rows, 2 * col_count)
    labels = jnp.cumsum(indicator_records.reshape(block_count, span_rows).astype(jnp.int32), axis=1)
    places = jnp.arange(span_rows)
    before = places[:, None] > places[None, :]
    linked = ((labels[:, :, None] == labels[:, None, :]) & before[None]).astype(jnp.float32)
    opened = (labels == 0).astype(jnp.float32)
    closing = (labels == labels[:, -1:]).astype(jnp.float32)
    offsets = places.astype(jnp.float32)[:, None]
    middle = 0.5 * span_rows
    rising = jnp.exp((offsets - middle) * decay_rate)
    descending = jnp.exp((middle + 1.0 - offsets) * decay_rate)
    inside_partial_additions = descending * jnp.einsum(
        "nts,nsc->ntc", linked, supplied_tokens_stream * rising, precision=lax.Precision.HIGHEST
    )
    tail_decay = jnp.exp((offsets + 1.0 - span_rows) * decay_rate)
    block_ends = jnp.einsum(
        "ns,nsc->nc", closing, supplied_tokens_stream * tail_decay, precision=lax.Precision.HIGHEST
    )
    block_gates = opened[:, -1:] * jnp.exp(-span_rows * decay_rate)[None, :]
    first_end = block_ends[:1] + block_gates[:1] * handed_forward[None, :]
    block_ends = jnp.concatenate([first_end, block_ends[1:]], axis=0)
    gate_run, state_run = lax.associative_scan(link_states, (block_gates, block_ends), axis=0)
    entering = jnp.concatenate([handed_forward[None, :], state_run[:-1]], axis=0)
    passed_onward_segment = (
        opened[:, :, None] * jnp.exp(-offsets * decay_rate)[None] * entering[:, None, :]
    )
    finished_running_additions = (
        inside_partial_additions
        + passed_onward_segment
        + additional_first_reinforcement * supplied_tokens_stream
    )
    quotient = (
        finished_running_additions[:, :, :col_count] / finished_running_additions[:, :, col_count:]
    )
    return (quotient.reshape(row_count, col_count), gate_run[-1], state_run[-1])


def on_device(
    incoming_symbols,
    downstream_slope,
    sequence_extents,
    mixer_lookup_map,
    mixer_payload_map,
    mixer_accepting_map,
    mixer_emitted_map,
    feedforward_lookup_map,
    feedforward_payload_map,
    feedforward_accepting_map,
    prime_normalize_gain,
    prime_normalize_bias,
    later_normalize_gain,
    later_normalize_bias,
    mixer_lookup_shiftmix,
    mixer_payload_shiftmix,
    mixer_accepting_shiftmix,
    feedforward_lookup_shiftmix,
    feedforward_accepting_shiftmix,
    channel_shrink_rate,
    newest_boost,
):
    hidden_track = incoming_symbols[0].astype(jnp.float32)
    tok_count, model_width = hidden_track.shape
    seq_count = lax.axis_size("seq")
    sequence_number = lax.axis_index("seq")
    apportioned_extent = model_width // seq_count
    group_positions = jnp.arange(tok_count * seq_count, dtype=jnp.int32)
    group_flags = token_starts(sequence_extents[0], group_positions)
    local_flags = lax.dynamic_slice_in_dim(group_flags, sequence_number * tok_count, tok_count)
    lookup_map, payload_map, accepting_map, emitted_map = (
        lax.all_gather(mixer_lookup_map, "fsdp", axis=0, tiled=True),
        lax.all_gather(mixer_payload_map, "fsdp", axis=0, tiled=True),
        lax.all_gather(mixer_accepting_map, "fsdp", axis=0, tiled=True),
        lax.all_gather(mixer_emitted_map, "fsdp", axis=0, tiled=True),
    )
    normed, first_back = jax.vjp(
        layer_norm, hidden_track, prime_normalize_gain, prime_normalize_bias
    )
    prior_row = passed_along(normed[-1:], "seq", 1)

    def mix_attention(current, previous, weights):
        return shift_mix(current, previous, local_flags, weights)

    (key_in, value_in, recept_in), mix_one_back = jax.vjp(
        mix_attention,
        normed,
        prior_row,
        (mixer_lookup_shiftmix, mixer_payload_shiftmix, mixer_accepting_shiftmix),
    )
    key_low = key_in.astype(jnp.bfloat16)
    value_low = value_in.astype(jnp.bfloat16)
    recept_low = recept_in.astype(jnp.bfloat16)
    lookup_records = jnp.dot(key_low, lookup_map, preferred_element_type=jnp.float32).astype(
        jnp.bfloat16
    )
    payload_records = jnp.dot(value_low, payload_map, preferred_element_type=jnp.float32).astype(
        jnp.bfloat16
    )
    recept = jax.nn.sigmoid(jnp.dot(recept_low, accepting_map, preferred_element_type=jnp.float32))
    key_cols, value_cols = (
        lax.all_to_all(lookup_records, "seq", split_axis=1, concat_axis=0, tiled=True),
        lax.all_to_all(payload_records, "seq", split_axis=1, concat_axis=0, tiled=True),
    )
    decay_cols = lax.dynamic_slice_in_dim(
        channel_shrink_rate, sequence_number * apportioned_extent, apportioned_extent
    )
    leading_fields = lax.dynamic_slice_in_dim(
        newest_boost, sequence_number * apportioned_extent, apportioned_extent
    )
    wkv_apply = partial(recurrent_mean_here_device, indicator_records=group_flags)
    (wkv_vals, gate_end, state_end), wkv_back = jax.vjp(
        wkv_apply,
        key_cols.astype(jnp.float32),
        value_cols.astype(jnp.float32),
        decay_cols,
        leading_fields,
        jnp.zeros((2 * apportioned_extent,), jnp.float32),
    )
    wkv_low = lax.all_to_all(
        wkv_vals.astype(jnp.bfloat16), "seq", split_axis=0, concat_axis=1, tiled=True
    )
    wkv_float = wkv_low.astype(jnp.float32)
    attended = (recept * wkv_float).astype(jnp.bfloat16)
    resid = hidden_track + jnp.dot(attended, emitted_map, preferred_element_type=jnp.float32)
    second, second_back = jax.vjp(layer_norm, resid, later_normalize_gain, later_normalize_bias)
    prior_second = passed_along(second[-1:], "seq", 1)

    def mix_channel(current, previous, weights):
        return shift_mix(current, previous, local_flags, weights)

    (up_in, gate_in), mix_two_back = jax.vjp(
        mix_channel,
        second,
        prior_second,
        (feedforward_lookup_shiftmix, feedforward_accepting_shiftmix),
    )
    expanding_map, contracting_map, sigmoid_switch_map = (
        lax.all_gather(feedforward_lookup_map, "fsdp", axis=0, tiled=True),
        lax.all_gather(feedforward_payload_map, "fsdp", axis=0, tiled=True),
        lax.all_gather(feedforward_accepting_map, "fsdp", axis=0, tiled=True),
    )
    up_low = up_in.astype(jnp.bfloat16)
    gate_low = gate_in.astype(jnp.bfloat16)
    pre_up = jnp.dot(up_low, expanding_map, preferred_element_type=jnp.float32)
    positive = jnp.maximum(pre_up, 0.0)
    squared = (positive * positive).astype(jnp.bfloat16)
    ffn_vals = jnp.dot(squared, contracting_map, preferred_element_type=jnp.float32)
    gating = jax.nn.sigmoid(
        jnp.dot(gate_low, sigmoid_switch_map, preferred_element_type=jnp.float32)
    )
    mixed = (resid + gating * ffn_vals).astype(jnp.bfloat16)
    (
        lookup_map,
        payload_map,
        accepting_map,
        emitted_map,
        expanding_map,
        contracting_map,
        sigmoid_switch_map,
    ) = (
        lax.all_gather(mixer_lookup_map, "fsdp", axis=0, tiled=True),
        lax.all_gather(mixer_payload_map, "fsdp", axis=0, tiled=True),
        lax.all_gather(mixer_accepting_map, "fsdp", axis=0, tiled=True),
        lax.all_gather(mixer_emitted_map, "fsdp", axis=0, tiled=True),
        lax.all_gather(feedforward_lookup_map, "fsdp", axis=0, tiled=True),
        lax.all_gather(feedforward_payload_map, "fsdp", axis=0, tiled=True),
        lax.all_gather(feedforward_accepting_map, "fsdp", axis=0, tiled=True),
    )
    upstream = downstream_slope[0].astype(jnp.float32)
    d_vals = (upstream * gating).astype(jnp.bfloat16)
    derivative_receptance_preactivation = (upstream * ffn_vals * gating * (1.0 - gating)).astype(
        jnp.bfloat16
    )
    grad_down = jnp.dot(squared.T, d_vals, preferred_element_type=jnp.float32)
    grad_gate = jnp.dot(
        gate_low.T, derivative_receptance_preactivation, preferred_element_type=jnp.float32
    )
    d_squared = jnp.dot(d_vals, contracting_map.T, preferred_element_type=jnp.float32)
    d_pre_up = (d_squared * 2.0 * positive).astype(jnp.bfloat16)
    grad_up = jnp.dot(up_low.T, d_pre_up, preferred_element_type=jnp.float32)
    d_up_in = jnp.dot(d_pre_up, expanding_map.T, preferred_element_type=jnp.float32)
    d_gate_in = jnp.dot(
        derivative_receptance_preactivation,
        sigmoid_switch_map.T,
        preferred_element_type=jnp.float32,
    )
    d_second, d_prior_second, (grad_ffn_mix_key, grad_ffn_mix_recept) = mix_two_back(
        (d_up_in, d_gate_in)
    )
    returned_second = passed_along(d_prior_second, "seq", -1)
    d_second = jnp.concatenate([d_second[:-1], d_second[-1:] + returned_second], axis=0)
    d_resid_norm, grad_second_gain, grad_second_bias = second_back(d_second)
    d_resid = upstream + d_resid_norm
    d_att = d_resid.astype(jnp.bfloat16)
    grad_output = jnp.dot(attended.T, d_att, preferred_element_type=jnp.float32)
    d_attended = jnp.dot(d_att, emitted_map.T, preferred_element_type=jnp.float32)
    d_wkv = (d_attended * recept).astype(jnp.bfloat16)
    d_recept_pre = (d_attended * wkv_float * recept * (1.0 - recept)).astype(jnp.bfloat16)
    d_wkv_cols = lax.all_to_all(d_wkv, "seq", split_axis=1, concat_axis=0, tiled=True)
    d_key_cols, d_value_cols, d_decay_cols, d_first_cols, unused_state = wkv_back(
        (d_wkv_cols.astype(jnp.float32), jnp.zeros_like(gate_end), jnp.zeros_like(state_end))
    )
    d_key_low, d_value_low = (
        lax.all_to_all(
            d_key_cols.astype(jnp.bfloat16), "seq", split_axis=0, concat_axis=1, tiled=True
        ),
        lax.all_to_all(
            d_value_cols.astype(jnp.bfloat16), "seq", split_axis=0, concat_axis=1, tiled=True
        ),
    )
    grad_decay = lax.dynamic_update_slice_in_dim(
        jnp.zeros((model_width,), jnp.float32),
        d_decay_cols,
        sequence_number * apportioned_extent,
        0,
    )
    grad_first = lax.dynamic_update_slice_in_dim(
        jnp.zeros((model_width,), jnp.float32),
        d_first_cols,
        sequence_number * apportioned_extent,
        0,
    )
    grad_key = jnp.dot(key_low.T, d_key_low, preferred_element_type=jnp.float32)
    grad_value = jnp.dot(value_low.T, d_value_low, preferred_element_type=jnp.float32)
    grad_recept = jnp.dot(recept_low.T, d_recept_pre, preferred_element_type=jnp.float32)
    d_key_in = jnp.dot(d_key_low, lookup_map.T, preferred_element_type=jnp.float32)
    d_value_in = jnp.dot(d_value_low, payload_map.T, preferred_element_type=jnp.float32)
    d_recept_in = jnp.dot(d_recept_pre, accepting_map.T, preferred_element_type=jnp.float32)
    d_normed, d_prior, (grad_mix_key, grad_mix_value, grad_mix_recept) = mix_one_back(
        (d_key_in, d_value_in, d_recept_in)
    )
    returned_first = passed_along(d_prior, "seq", -1)
    d_normed = jnp.concatenate([d_normed[:-1], d_normed[-1:] + returned_first], axis=0)
    d_stream_norm, grad_first_gain, grad_first_bias = first_back(d_normed)
    tokens_grad = (d_resid + d_stream_norm).astype(jnp.bfloat16)[None]
    partials = (
        grad_key,
        grad_value,
        grad_recept,
        grad_output,
        grad_up,
        grad_down,
        grad_gate,
        grad_first_gain,
        grad_first_bias,
        grad_second_gain,
        grad_second_bias,
        grad_mix_key,
        grad_mix_value,
        grad_mix_recept,
        grad_ffn_mix_key,
        grad_ffn_mix_recept,
        grad_decay,
        grad_first,
    )
    grads = (
        lax.psum_scatter(partials[0], ("seq", "fsdp"), scatter_dimension=0, tiled=True),
        lax.psum_scatter(partials[1], ("seq", "fsdp"), scatter_dimension=0, tiled=True),
        lax.psum_scatter(partials[2], ("seq", "fsdp"), scatter_dimension=0, tiled=True),
        lax.psum_scatter(partials[3], ("seq", "fsdp"), scatter_dimension=0, tiled=True),
        lax.psum_scatter(partials[4], ("seq", "fsdp"), scatter_dimension=0, tiled=True),
        lax.psum_scatter(partials[5], ("seq", "fsdp"), scatter_dimension=0, tiled=True),
        lax.psum_scatter(partials[6], ("seq", "fsdp"), scatter_dimension=0, tiled=True),
        lax.psum_scatter(partials[7], ("seq", "fsdp"), scatter_dimension=0, tiled=True),
        lax.psum_scatter(partials[8], ("seq", "fsdp"), scatter_dimension=0, tiled=True),
        lax.psum_scatter(partials[9], ("seq", "fsdp"), scatter_dimension=0, tiled=True),
        lax.psum_scatter(partials[10], ("seq", "fsdp"), scatter_dimension=0, tiled=True),
        lax.psum_scatter(partials[11], ("seq", "fsdp"), scatter_dimension=0, tiled=True),
        lax.psum_scatter(partials[12], ("seq", "fsdp"), scatter_dimension=0, tiled=True),
        lax.psum_scatter(partials[13], ("seq", "fsdp"), scatter_dimension=0, tiled=True),
        lax.psum_scatter(partials[14], ("seq", "fsdp"), scatter_dimension=0, tiled=True),
        lax.psum_scatter(partials[15], ("seq", "fsdp"), scatter_dimension=0, tiled=True),
        lax.psum_scatter(partials[16], ("seq", "fsdp"), scatter_dimension=0, tiled=True),
        lax.psum_scatter(partials[17], ("seq", "fsdp"), scatter_dimension=0, tiled=True),
    )
    return (
        mixed[None],
        tokens_grad,
        grads[0],
        grads[1],
        grads[2],
        grads[3],
        grads[4],
        grads[5],
        grads[6],
        grads[7],
        grads[8],
        grads[9],
        grads[10],
        grads[11],
        grads[12],
        grads[13],
        grads[14],
        grads[15],
        grads[16],
        grads[17],
    )


def solution(mesh):
    placed = (
        P("fsdp", "seq", None),
        P("fsdp", "seq", None),
        P("fsdp", None),
        P("fsdp", None),
        P("fsdp", None),
        P("fsdp", None),
        P("fsdp", None),
        P("fsdp", None),
        P("fsdp", None),
        P("fsdp", None),
        P(),
        P(),
        P(),
        P(),
        P(),
        P(),
        P(),
        P(),
        P(),
        P(),
        P(),
    )
    return jax.shard_map(
        on_device,
        mesh=mesh,
        in_specs=placed,
        out_specs=(
            P("fsdp", "seq", None),
            P("fsdp", "seq", None),
            P(("seq", "fsdp"), None),
            P(("seq", "fsdp"), None),
            P(("seq", "fsdp"), None),
            P(("seq", "fsdp"), None),
            P(("seq", "fsdp"), None),
            P(("seq", "fsdp"), None),
            P(("seq", "fsdp"), None),
            P(("seq", "fsdp")),
            P(("seq", "fsdp")),
            P(("seq", "fsdp")),
            P(("seq", "fsdp")),
            P(("seq", "fsdp")),
            P(("seq", "fsdp")),
            P(("seq", "fsdp")),
            P(("seq", "fsdp")),
            P(("seq", "fsdp")),
            P(("seq", "fsdp")),
            P(("seq", "fsdp")),
        ),
        check_vma=False,
    )
```

profile of v0, /device:TPU:0, one launch (start us, length us, event | category | flops | bytes accessed | tf_op | source)
XLA Modules:
  0.0 1342.0 jit_solution(4513496870963493083)
XLA Ops:
  19.6 15.4 %all-gather.12.cloned.1.call-done = bf16[1024,1024]{1,0:T(8,128)(2,1)} async-done(((bf16[256,1024]{1,0:T(8,128)(2,1)}), bf16[1024,1024]{1,0:T(8,128)(2,1)}) %all-gather.12.cloned.1.call-update) | async-done | bytes 2097168 | tf_op jit(solution)/shard_map/all_gather | solution.py:128
  45.9 13.2 all-gather.10.cloned.1.call-done
  73.9 9.1 all-to-all-done
  98.3 13.6 %all-to-all-done.2 = bf16[8,256,128]{2,1,0:T(8,128)(2,1)} async-done(((bf16[8,256,128]{2,1,0:T(8,128)(2,1)}), bf16[8,256,128]{2,1,0:T(8,128)(2,1)}, u32[]{:S(2)}, u32[]{:S(2)}) %all-to-all-start.2) | async-done | bytes 524320 | tf_op jit(solution)/shard_map/all_to_all | solution.py:175
  134.7 56.4 %all-gather.18.cloned.1.call-done = bf16[1024,4096]{1,0:T(8,128)(2,1)} async-done(((bf16[256,4096]{1,0:T(8,128)(2,1)}), bf16[1024,4096]{1,0:T(8,128)(2,1)}) %all-gather.18.cloned.1.call-update) | async-done | bytes 8388624 | tf_op jit(solution)/shard_map/all_gather | solution.py:194
  191.1 7.9 convolution_maximum_fusion
  199.0 52.0 %all-gather.20.cloned.1.call-done = bf16[4096,1024]{1,0:T(8,128)(2,1)} async-done(((bf16[1024,1024]{1,0:T(8,128)(2,1)}), bf16[4096,1024]{1,0:T(8,128)(2,1)}) %all-gather.20.cloned.1.call-update) | async-done | bytes 8388624 | tf_op jit(solution)/shard_map/all_gather | solution.py:195
  251.0 8.2 fusion.44
  262.7 7.3 fusion.1
  270.1 6.5 fusion.134
  295.1 5.5 all-to-all-start.3
  308.7 8.0 all-to-all-done.3
  332.2 5.8 multiply_reduce_fusion
  339.3 18.1 %all_to_all.87 = bf16[8,256,128]{1,2,0:T(8,128)(2,1)S(1)} all-to-all(bf16[8,256,128]{1,2,0:T(8,128)(2,1)} %copy.65), channel_id=1, replica_groups=mesh['seq'=8,'fsdp'=4] {'seq'}, dimensions={0} | all-to-all | bytes 1048576 | tf_op jit(solution)/shard_map/all_to_all | solution.py:263
  361.5 16.9 %all_to_all.88 = bf16[8,256,128]{1,2,0:T(8,128)(2,1)S(1)} all-to-all(bf16[8,256,128]{1,2,0:T(8,128)(2,1)S(1)} %copy.66), channel_id=1, replica_groups=mesh['seq'=8,'fsdp'=4] {'seq'}, dimensions={0} | all-to-all | bytes 1048576 | tf_op jit(solution)/shard_map/all_to_all | solution.py:260
  383.8 9.3 fusion.139
  394.3 10.3 fusion.56
  426.9 44.0 %all-reduce.67 = (f32[1024]{0:T(1024)S(1)}, f32[1024]{0:T(1024)S(1)}, f32[1024]{0:T(1024)S(1)}, f32[1024]{0:T(1024)S(1)}, f32[1024]{0:T(1024)S(1)}, /*index=5*/f...) all-reduce(f32[1024]{0:T(1024)S(1)} %get-tuple-element.28, ...), channel_id=9, replica_groups=mesh['seq'=8,'fsdp'=4] {'seq','fsdp'}, use_global_device_ids=true, to_apply=%region_20.21.clone | all-reduce | flops 11264 | bytes 90112
  478.6 68.6 %reduce-scatter.14.cloned.1.call-done = f32[32,1024]{1,0:T(8,128)} async-done(((f32[1024,1024]{1,0:T(8,128)}), f32[32,1024]{1,0:T(8,128)}) %reduce-scatter.14.cloned.1.call-update) | async-done | bytes 131088 | tf_op jit(solution)/shard_map/reduce_scatter | solution.py:316
  547.2 139.8 %reduce-scatter.12.cloned.1.call-done = f32[32,1024]{1,0:T(8,128)} async-done(((f32[1024,1024]{1,0:T(8,128)}), f32[32,1024]{1,0:T(8,128)}) %reduce-scatter.12.cloned.1.call-update) | async-done | bytes 131088 | tf_op jit(solution)/shard_map/reduce_scatter | solution.py:315
  686.9 139.6 %reduce-scatter.10.cloned.1.call-done = f32[32,1024]{1,0:T(8,128)} async-done(((f32[1024,1024]{1,0:T(8,128)}), f32[32,1024]{1,0:T(8,128)}) %reduce-scatter.10.cloned.1.call-update) | async-done | bytes 131088 | tf_op jit(solution)/shard_map/reduce_scatter | solution.py:314
  826.6 139.5 %reduce-scatter.8.cloned.1.call-done = f32[32,1024]{1,0:T(8,128)} async-done(((f32[1024,1024]{1,0:T(8,128)}), f32[32,1024]{1,0:T(8,128)}) %reduce-scatter.8.cloned.1.call-update) | async-done | bytes 131088 | tf_op jit(solution)/shard_map/reduce_scatter | solution.py:313
  966.1 182.3 %reduce-scatter.16.cloned.1.call-done = f32[32,4096]{1,0:T(8,128)} async-done(((f32[1024,4096]{1,0:T(8,128)}), f32[32,4096]{1,0:T(8,128)}) %reduce-scatter.16.cloned.1.call-update) | async-done | bytes 524304 | tf_op jit(solution)/shard_map/reduce_scatter | solution.py:317
  1148.4 186.6 %reduce-scatter.18.cloned.1.call-done = f32[128,1024]{1,0:T(8,128)} async-done(((f32[4096,1024]{1,0:T(8,128)}), f32[128,1024]{1,0:T(8,128)}) %reduce-scatter.18.cloned.1.call-update) | async-done | bytes 524304 | tf_op jit(solution)/shard_map/reduce_scatter | solution.py:318
  (566 shorter events, 161.8 us)
Async XLA Ops:
  7.2 27.7 %all-gather.12.cloned.1.call-start = ((), (), s32[]{:S(2)}) async-start(), calls=%async_computation.15 | async-start | bytes 2621440 | tf_op jit(solution)/shard_map/all_gather | solution.py:128
  7.9 51.2 %all-gather.10.cloned.1.call-start = ((), (), s32[]{:S(2)}) async-start(), calls=%async_computation.14 | async-start | bytes 2621440 | tf_op jit(solution)/shard_map/all_gather | solution.py:127
  8.7 89.6 %all-gather.8.cloned.1.call-start = ((), (), s32[]{:S(2)}) async-start(), calls=%async_computation.13 | async-start | bytes 2621440 | tf_op jit(solution)/shard_map/all_gather | solution.py:129
  9.4 106.3 %all-gather.14.cloned.1.call-start = ((), (), s32[]{:S(2)}) async-start(), calls=%async_computation.16 | async-start | bytes 2621440 | tf_op jit(solution)/shard_map/all_gather | solution.py:130
  10.0 121.4 %all-gather.16.cloned.1.call-start = ((), (), s32[]{:S(2)}) async-start(), calls=%async_computation.17 | async-start | bytes 2621440 | tf_op jit(solution)/shard_map/all_gather | solution.py:196
  10.6 180.5 %all-gather.18.cloned.1.call-start = ((), (), s32[]{:S(2)}) async-start(), calls=%async_computation.18 | async-start | bytes 10485760 | tf_op jit(solution)/shard_map/all_gather | solution.py:194
  11.2 239.8 %all-gather.20.cloned.1.call-start = ((), (), s32[]{:S(2)}) async-start(), calls=%async_computation.19 | async-start | bytes 10485760 | tf_op jit(solution)/shard_map/all_gather | solution.py:195
  13.0 6.6 collective-permute-start
  38.4 24.2 %all-to-all-start.1 = ((bf16[256,8,128]{2,0,1:T(8,128)(2,1)}), bf16[256,8,128]{2,0,1:T(8,128)(2,1)S(1)}, u32[]{:S(2)}, u32[]{:S(2)}) async-start(bf16[256,8,128]{2,0,1:T(8,128)(2,1)} %bitcast.175), calls=%async_computation.1 | async-start | bytes 1048576 | tf_op jit(solution)/shard_map/all_to_all | solution.py:158
  62.6 20.4 %all-to-all-start = ((bf16[256,8,128]{2,0,1:T(8,128)(2,1)}), bf16[256,8,128]{2,0,1:T(8,128)(2,1)S(1)}, u32[]{:S(2)}, u32[]{:S(2)}) async-start(bf16[256,8,128]{2,0,1:T(8,128)(2,1)} %bitcast.176), calls=%async_computation | async-start | bytes 1048576 | tf_op jit(solution)/shard_map/all_to_all | solution.py:157
  93.5 18.5 %all-to-all-start.2 = ((bf16[8,256,128]{2,1,0:T(8,128)(2,1)}), bf16[8,256,128]{2,1,0:T(8,128)(2,1)}, u32[]{:S(2)}, u32[]{:S(2)}) async-start(bf16[8,256,128]{2,1,0:T(8,128)(2,1)} %bitcast.11), calls=%async_computation.2 | async-start | bytes 1048576 | tf_op jit(solution)/shard_map/all_to_all | solution.py:175
  97.6 380.9 %reduce-scatter.20.cloned.1.call-start = ((), (), s32[]{:S(2)}) async-start(), calls=%async_computation.26 | async-start | bytes 4325376 | tf_op jit(solution)/shard_map/reduce_scatter | solution.py:319
  119.5 4.5 collective-permute-start.1
  191.1 59.9 %copy-start.13 = (bf16[1,256,1024]{2,1,0:T(8,128)(2,1)S(1)}, bf16[1,256,1024]{2,1,0:T(8,128)(2,1)}, u32[]{:S(2)}) copy-start(bf16[1,256,1024]{2,1,0:T(8,128)(2,1)} %param.22) | copy-start | bytes 1572868
  262.7 284.5 %reduce-scatter.14.cloned.1.call-start = ((), (), s32[]{:S(2)}) async-start(), calls=%async_computation.23 | async-start | bytes 4325376 | tf_op jit(solution)/shard_map/reduce_scatter | solution.py:316
  278.6 5.5 collective-permute-start.2
  295.1 21.6 %all-to-all-start.3 = ((bf16[256,8,128]{2,0,1:T(8,128)(2,1)}), bf16[256,8,128]{2,0,1:T(8,128)(2,1)}, u32[]{:S(2)}, u32[]{:S(2)}) async-start(bf16[256,8,128]{2,0,1:T(8,128)(2,1)} %bitcast.194), calls=%async_computation.3 | async-start | bytes 1048576 | tf_op jit(solution)/shard_map/all_to_all | solution.py:255
  300.6 386.3 %reduce-scatter.12.cloned.1.call-start = ((), (), s32[]{:S(2)}) async-start(), calls=%async_computation.22 | async-start | bytes 4325376 | tf_op jit(solution)/shard_map/reduce_scatter | solution.py:315
  305.0 521.6 %reduce-scatter.10.cloned.1.call-start = ((), (), s32[]{:S(2)}) async-start(), calls=%async_computation.21 | async-start | bytes 4325376 | tf_op jit(solution)/shard_map/reduce_scatter | solution.py:314
  361.2 604.9 %reduce-scatter.8.cloned.1.call-start = ((), (), s32[]{:S(2)}) async-start(), calls=%async_computation.20 | async-start | bytes 4325376 | tf_op jit(solution)/shard_map/reduce_scatter | solution.py:313
  382.2 766.3 %reduce-scatter.16.cloned.1.call-start = ((), (), s32[]{:S(2)}) async-start(), calls=%async_computation.24 | async-start | bytes 17301504 | tf_op jit(solution)/shard_map/reduce_scatter | solution.py:317
  393.1 942.0 %reduce-scatter.18.cloned.1.call-start = ((), (), s32[]{:S(2)}) async-start(), calls=%async_computation.25 | async-start | bytes 17301504 | tf_op jit(solution)/shard_map/reduce_scatter | solution.py:318
  419.5 5.5 collective-permute-start.3
  425.1 52.2 %copy-start.137 = (f32[256]{0:T(256)S(1)}, f32[256]{0:T(256)}, u32[]{:S(2)}) copy-start(f32[256]{0:T(256)} %copy-done.136) | copy-start | bytes 3076
  (149 other events, 1021.7 us)
Sparse Core Ops, SparseCore 0:
  9.6 25.3 all-gather.11
  36.5 22.5 all-gather.9
  60.7 22.5 all-gather.7
  84.7 22.5 all-gather.13
  108.7 22.5 all-gather.15
  132.8 58.2 all-gather.17
  192.6 58.2 all-gather.19
  262.8 143.9 reduce-scatter.19
  409.7 137.4 reduce-scatter.13
  549.9 137.0 reduce-scatter.11
  689.8 136.7 reduce-scatter.9
  829.3 136.7 reduce-scatter.7
  969.0 179.4 reduce-scatter.15
  1151.2 183.8 reduce-scatter.17
where the time goes:
time: 1350 us; the launch traced here: 1340 us
  waiting for transfers between devices  1040 us (77%)
  matrix products  99.7 us (7%)
  blocking collectives  78.9 us (6%)
  other arithmetic  39.2 us (3%)
  local copies, waits for them, and re-layouts  33.9 us (3%)
  starting transfers between devices  32.5 us (2%)
  between operations  16.6 us (1%)
    reduce_scatter x1, waiting for transfers between devices, on_device(): lax.psum_scatter(partials[5], ('seq', 'fsdp'), scatter_dimension=0, tiled...  187 us
    reduce_scatter x1, waiting for transfers between devices, on_device(): lax.psum_scatter(partials[4], ('seq', 'fsdp'), scatter_dimension=0, tiled...  182 us
    reduce_scatter x1, waiting for transfers between devices, on_device(): lax.psum_scatter(partials[2], ('seq', 'fsdp'), scatter_dimension=0, tiled...  140 us
    reduce_scatter x1, waiting for transfers between devices, on_device(): lax.psum_scatter(partials[1], ('seq', 'fsdp'), scatter_dimension=0, tiled...  140 us
    reduce_scatter x1, waiting for transfers between devices, on_device(): lax.psum_scatter(partials[0], ('seq', 'fsdp'), scatter_dimension=0, tiled...  140 us
    reduce_scatter x1, waiting for transfers between devices, on_device(): lax.psum_scatter(partials[3], ('seq', 'fsdp'), scatter_dimension=0, tiled...  68.6 us
    all_gather x1, waiting for transfers between devices, on_device(): lax.all_gather(feedforward_lookup_map, 'fsdp', axis=0, tiled=True)  56.4 us
    all_gather x1, waiting for transfers between devices, on_device(): lax.all_gather(feedforward_payload_map, 'fsdp', axis=0, tiled=True)  52 us
  transfers between devices with their start and end apart: 22, of which 17 were waited for; matrix products, arithmetic and copies ran while one was open for 11% of the time, Pallas kernels for 0%

commit v1 on v0

v1 whole, which is shorter than its diff:
```python
from functools import partial

import jax
import jax.numpy as jnp
from jax import lax
from jax.experimental import pallas as pl
from jax.experimental.pallas import tpu as pltpu
from jax.sharding import PartitionSpec as P

norm_eps = 1e-05
F32 = jnp.float32
BF16 = jnp.bfloat16
FAR = 1 << 20
BOTH = ("seq", "fsdp")


def flipped(value, axis, bit):
    count = lax.axis_size(axis)
    return lax.ppermute(value, axis, [(i, i ^ (1 << bit)) for i in range(count)])


def passed_along(value, axis, steps):
    count = lax.axis_size(axis)
    initial, last = (max(0, -steps), min(count, count - steps))
    return lax.ppermute(value, axis, [(source, source + steps) for source in range(initial, last)])


def layer_norm(hidden_track, gain_vec, bias_vec):
    centred = hidden_track - jnp.mean(hidden_track, axis=-1, keepdims=True)
    spread = jnp.mean(centred * centred, axis=-1, keepdims=True)
    return centred * lax.rsqrt(spread + norm_eps) * gain_vec + bias_vec


def shift_mix(current, previous, indicator_records, weights):
    retain = 1.0 - indicator_records.astype(F32)[:, None]
    shifted = jnp.concatenate([previous, current[:-1]], axis=0) * retain
    return tuple((current * weight + shifted * (1.0 - weight) for weight in weights))


def token_starts(sequence_extents, positions):
    begins = jnp.cumsum(sequence_extents, axis=-1) - sequence_extents
    start_marks = (begins[..., :, None] == positions) & (sequence_extents[..., :, None] > 0)
    return jnp.any(start_marks, axis=-2)


def scan_forward_body(rate_ref, k_ref, v_ref, since_ref, a_ref, b_ref, end_ref):
    rows, cols = k_ref.shape
    place = lax.broadcasted_iota(jnp.int32, (8, cols), 0)
    rate = rate_ref[...]
    fades = [jnp.exp(-rate * float(d)) for d in (1, 2, 4)]
    carry_fade = jnp.exp(-rate * (place + 1).astype(F32))

    def sub(k, v, since, state):
        lift = jnp.exp(k)
        near = jnp.minimum(since, place)
        out = []
        for run, last in zip((lift * v, lift), state):
            for d, fade in zip((1, 2, 4), fades):
                run = run + jnp.where(near >= d, fade * pltpu.roll(run, d, 0), 0.0)
            run = run + jnp.where(since > place, carry_fade * last, 0.0)
            before = jnp.where(place == 0, last, pltpu.roll(run, 1, 0))
            before = jnp.where(since >= 1, before, 0.0)
            out.append((before, run[7:8, :]))
        return out

    def step(i, state):
        base = pl.multiple_of(i * 16, 16)
        k = k_ref[pl.ds(base, 16), :].astype(F32)
        v = v_ref[pl.ds(base, 16), :].astype(F32)
        for h in range(2):
            at = pl.multiple_of(base + 8 * h, 8)
            since = jnp.tile(since_ref[pl.ds(at, 8), :], (1, cols // 128))
            (ua, sa), (ub, sb) = sub(k[8 * h : 8 * h + 8], v[8 * h : 8 * h + 8], since, state)
            a_ref[pl.ds(at, 8), :] = ua
            b_ref[pl.ds(at, 8), :] = ub
            state = (sa, sb)
        return state

    zero = jnp.zeros((1, cols), F32)
    sa, sb = lax.fori_loop(0, rows // 16, step, (zero, zero))
    end_ref[...] = jnp.where(place == 0, sa, jnp.where(place == 1, sb, 0.0))


def scan_backward_body(
    rate_ref, bonus_ref, k_ref, v_ref, d_ref, a_in_ref, b_in_ref, until_ref, a_ref, b_ref, end_ref
):
    rows, cols = k_ref.shape
    place = lax.broadcasted_iota(jnp.int32, (8, cols), 0)
    rate = rate_ref[...]
    fades = [jnp.exp(-rate * float(d)) for d in (1, 2, 4)]
    carry_fade = jnp.exp(-rate * (8 - place).astype(F32))

    def step(j, state):
        i = rows // 16 - 1 - j
        base = pl.multiple_of(i * 16, 16)
        k = k_ref[pl.ds(base, 16), :].astype(F32)
        v = v_ref[pl.ds(base, 16), :].astype(F32)
        d = d_ref[pl.ds(base, 16), :].astype(F32)
        for h in (1, 0):
            at = pl.multiple_of(base + 8 * h, 8)
            part = slice(8 * h, 8 * h + 8)
            until = jnp.tile(until_ref[pl.ds(at, 8), :], (1, cols // 128))
            near = jnp.minimum(until, 7 - place)
            bonus = jnp.exp(bonus_ref[...] + k[part])
            inverse = 1.0 / (b_in_ref[pl.ds(at, 8), :] + bonus)
            wkv = (a_in_ref[pl.ds(at, 8), :] + bonus * v[part]) * inverse
            first = d[part] * inverse
            new = []
            for run, last, ref in zip((first, -first * wkv), state, (a_ref, b_ref)):
                for q, fade in zip((1, 2, 4), fades):
                    run = run + jnp.where(near >= q, fade * pltpu.roll(run, 8 - q, 0), 0.0)
                run = run + jnp.where(until >= 8 - place, carry_fade * last, 0.0)
                after = jnp.where(place == 7, last, pltpu.roll(run, 7, 0))
                ref[pl.ds(at, 8), :] = jnp.where(until >= 1, after, 0.0)
                new.append(run[0:1, :])
            state = tuple(new)
        return state

    zero = jnp.zeros((1, cols), F32)
    sa, sb = lax.fori_loop(0, rows // 16, step, (zero, zero))
    end_ref[...] = jnp.where(place == 0, sa, jnp.where(place == 1, sb, 0.0))


def scan_call(body, vectors, arrays, marks):
    rows, cols = arrays[0].shape
    wide = min(256, cols)
    vec = pl.BlockSpec((1, wide), lambda i: (0, i))
    arr = pl.BlockSpec((rows, wide), lambda i: (0, i))
    return pl.pallas_call(
        body,
        grid=(cols // wide,),
        in_specs=[vec] * len(vectors)
        + [arr] * len(arrays)
        + [pl.BlockSpec((rows, 128), lambda i: (0, 0))],
        out_specs=[arr, arr, pl.BlockSpec((8, wide), lambda i: (0, i))],
        out_shape=[
            jax.ShapeDtypeStruct((rows, cols), F32),
            jax.ShapeDtypeStruct((rows, cols), F32),
            jax.ShapeDtypeStruct((8, cols), F32),
        ],
        cost_estimate=pl.CostEstimate(
            flops=60 * rows * cols, bytes_accessed=16 * rows * cols, transcendentals=rows * cols
        ),
    )(*[v[None, :] for v in vectors], *arrays, marks)


def gathered_ends(ends):
    count = lax.axis_size("seq")
    copies = jnp.broadcast_to(ends[None], (count, *ends.shape))
    return lax.all_to_all(copies, "seq", split_axis=0, concat_axis=0, tiled=True)


def scattered_sum(grad, order, here):
    rows, cols = grad.shape
    seq_count, fsdp_count = lax.axis_size("seq"), lax.axis_size("fsdp")
    line = seq_count // 2
    block = rows // (seq_count * fsdp_count)
    value = grad.reshape(line, 2, 2, 2, block, cols)
    dims = ["z", "y", "x", "c"]
    links = {"y": ("seq", 0), "x": ("fsdp", 1), "c": ("fsdp", 0)}
    for name in order:
        dim = dims.index(name)
        dims.pop(dim)
        if name == "z":
            value = line_sum(value, dim, here["z"], line)
            continue
        axis, bit = links[name]
        away = lax.dynamic_index_in_dim(value, 1 - here[name], dim, keepdims=False)
        got = flipped(away.astype(BF16), axis, bit)
        mine = lax.dynamic_index_in_dim(value, here[name], dim, keepdims=False)
        value = mine.astype(F32) + got.astype(F32)
    return value


def line_sum(value, dim, place, line):
    if line > 4:
        groups = [[2 * i + y for i in range(line)] for y in range(2)]
        whole = jnp.moveaxis(value, dim, 0)
        return lax.psum_scatter(whole, "seq", scatter_dimension=0, axis_index_groups=groups)
    up = down = None
    for step in range(1, line):
        sent_up = lax.dynamic_index_in_dim(
            value, jnp.minimum(place + line - step, line - 1), dim, keepdims=False
        ).astype(F32)
        sent_down = lax.dynamic_index_in_dim(
            value, jnp.maximum(place - line + step, 0), dim, keepdims=False
        ).astype(F32)
        if up is not None:
            sent_up = sent_up + up.astype(F32)
            sent_down = sent_down + down.astype(F32)
        up = lax.ppermute(
            sent_up.astype(BF16),
            "seq",
            [(2 * z + y, 2 * z + 2 + y) for z in range(step) for y in range(2)],
        )
        down = lax.ppermute(
            sent_down.astype(BF16),
            "seq",
            [(2 * z + y, 2 * z - 2 + y) for z in range(line - step, line) for y in range(2)],
        )
    mine = lax.dynamic_index_in_dim(value, place, dim, keepdims=False)
    return mine.astype(F32) + up.astype(F32) + down.astype(F32)


def on_device(
    incoming_symbols,
    downstream_slope,
    sequence_extents,
    mixer_lookup_map,
    mixer_payload_map,
    mixer_accepting_map,
    mixer_emitted_map,
    feedforward_lookup_map,
    feedforward_payload_map,
    feedforward_accepting_map,
    prime_normalize_gain,
    prime_normalize_bias,
    later_normalize_gain,
    later_normalize_bias,
    mixer_lookup_shiftmix,
    mixer_payload_shiftmix,
    mixer_accepting_shiftmix,
    feedforward_lookup_shiftmix,
    feedforward_accepting_shiftmix,
    channel_shrink_rate,
    newest_boost,
):
    hidden_track = incoming_symbols[0].astype(F32)
    tok_count, model_width = hidden_track.shape
    seq_count, fsdp_count = lax.axis_size("seq"), lax.axis_size("fsdp")
    sequence_number, fsdp_number = lax.axis_index("seq"), lax.axis_index("fsdp")
    here = {
        "z": sequence_number // 2,
        "y": sequence_number % 2,
        "x": fsdp_number // 2,
        "c": fsdp_number % 2,
    }

    group_positions = jnp.arange(tok_count * seq_count, dtype=jnp.int32)
    group_flags = token_starts(sequence_extents[0], group_positions)
    chunk_flags = group_flags.reshape(seq_count, tok_count)
    local_flags = lax.dynamic_index_in_dim(chunk_flags, sequence_number, 0, keepdims=False)
    chunk_has = jnp.any(chunk_flags, axis=1)
    chunk_first = chunk_flags[:, 0]
    places = jnp.arange(tok_count, dtype=jnp.int32)
    later = places[None, :] > places[:, None]
    last_start = jnp.max(
        jnp.where(local_flags[None, :] & ~later, places[None, :], -FAR), axis=1
    )
    next_start = jnp.min(jnp.where(local_flags[None, :] & later, places[None, :], FAR), axis=1)
    since = places - last_start
    until = next_start - 1 - places
    since_wide = jnp.broadcast_to(since[:, None], (tok_count, 128))
    until_wide = jnp.broadcast_to(until[:, None], (tok_count, 128))

    def whole(weight):
        return lax.all_gather(weight, "fsdp", axis=0, tiled=True)

    lookup_map = whole(mixer_lookup_map)
    payload_map = whole(mixer_payload_map)
    accepting_map = whole(mixer_accepting_map)
    emitted_map = whole(mixer_emitted_map)
    sigmoid_switch_map = whole(feedforward_accepting_map)
    expanding_map = whole(feedforward_lookup_map)
    contracting_map = whole(feedforward_payload_map)

    normed, first_back = jax.vjp(
        layer_norm, hidden_track, prime_normalize_gain, prime_normalize_bias
    )
    prior_row = passed_along(normed[-1:], "seq", 1)

    def mix(current, previous, weights):
        return shift_mix(current, previous, local_flags, weights)

    (key_in, value_in, recept_in), mix_one_back = jax.vjp(
        mix,
        normed,
        prior_row,
        (mixer_lookup_shiftmix, mixer_payload_shiftmix, mixer_accepting_shiftmix),
    )
    key_low = key_in.astype(BF16)
    value_low = value_in.astype(BF16)
    recept_low = recept_in.astype(BF16)
    key_rows = jnp.dot(key_low, lookup_map, preferred_element_type=F32).astype(BF16)
    value_rows = jnp.dot(value_low, payload_map, preferred_element_type=F32).astype(BF16)
    rate = jnp.exp(channel_shrink_rate)
    part_a, part_b, ends = scan_call(
        scan_forward_body, (rate,), (key_rows, value_rows), since_wide
    )
    all_ends = gathered_ends(ends[:2])
    recept = jax.nn.sigmoid(jnp.dot(recept_low, accepting_map, preferred_element_type=F32))
    order = jnp.arange(seq_count, dtype=jnp.int32)
    between = (order[None, :] > order[:, None]) & (order[None, :] < sequence_number)
    reaches = (order < sequence_number) & ~jnp.any(between & chunk_has[None, :], axis=1)
    gap = ((sequence_number - 1 - order) * tok_count).astype(F32)
    weigh = jnp.where(reaches[:, None], jnp.exp(-rate[None, :] * gap[:, None]), 0.0)
    entering = jnp.sum(weigh[:, None, :] * all_ends, axis=0)
    into = jnp.where(
        (since > places)[:, None], jnp.exp(-rate[None, :] * places.astype(F32)[:, None]), 0.0
    )
    key_float, value_float = key_rows.astype(F32), value_rows.astype(F32)
    state_a = part_a + into * entering[0:1]
    state_b = part_b + into * entering[1:2]
    bonus = jnp.exp(newest_boost + key_float)
    divisor = state_b + bonus
    wkv = (state_a + bonus * value_float) / divisor
    wkv_float = wkv.astype(BF16).astype(F32)
    attended = (recept * wkv_float).astype(BF16)
    resid = hidden_track + jnp.dot(attended, emitted_map, preferred_element_type=F32)

    second, second_back = jax.vjp(layer_norm, resid, later_normalize_gain, later_normalize_bias)
    prior_second = passed_along(second[-1:], "seq", 1)
    (up_in, gate_in), mix_two_back = jax.vjp(
        mix,
        second,
        prior_second,
        (feedforward_lookup_shiftmix, feedforward_accepting_shiftmix),
    )
    up_low = up_in.astype(BF16)
    gate_low = gate_in.astype(BF16)
    gating = jax.nn.sigmoid(jnp.dot(gate_low, sigmoid_switch_map, preferred_element_type=F32))
    pre_up = jnp.dot(up_low, expanding_map, preferred_element_type=F32)
    positive = jnp.maximum(pre_up, 0.0)
    squared = (positive * positive).astype(BF16)
    ffn_vals = jnp.dot(squared, contracting_map, preferred_element_type=F32)
    mixed = (resid + gating * ffn_vals).astype(BF16)

    upstream = downstream_slope[0].astype(F32)
    d_vals = (upstream * gating).astype(BF16)
    d_gate_pre = (upstream * ffn_vals * gating * (1.0 - gating)).astype(BF16)
    d_squared = jnp.dot(d_vals, contracting_map.T, preferred_element_type=F32)
    d_pre_up = (d_squared * 2.0 * positive).astype(BF16)
    grad_down = scattered_sum(
        jnp.dot(squared.T, d_vals, preferred_element_type=F32), "cxyz", here
    )
    d_up_in = jnp.dot(d_pre_up, expanding_map.T, preferred_element_type=F32)
    d_gate_in = jnp.dot(d_gate_pre, sigmoid_switch_map.T, preferred_element_type=F32)
    grad_up = scattered_sum(jnp.dot(up_low.T, d_pre_up, preferred_element_type=F32), "cyxz", here)
    grad_gate = scattered_sum(
        jnp.dot(gate_low.T, d_gate_pre, preferred_element_type=F32), "czxy", here
    )
    d_second, d_prior_second, (grad_ffn_mix_key, grad_ffn_mix_recept) = mix_two_back(
        (d_up_in, d_gate_in)
    )
    returned_second = passed_along(d_prior_second, "seq", -1)
    d_second = jnp.concatenate([d_second[:-1], d_second[-1:] + returned_second], axis=0)
    d_resid_norm, grad_second_gain, grad_second_bias = second_back(d_second)
    d_resid = upstream + d_resid_norm

    d_att = d_resid.astype(BF16)
    d_attended = jnp.dot(d_att, emitted_map.T, preferred_element_type=F32)
    d_wkv_low = (d_attended * recept).astype(BF16)
    d_recept_pre = (d_attended * wkv_float * recept * (1.0 - recept)).astype(BF16)
    back_a, back_b, heads = scan_call(
        scan_backward_body,
        (rate, newest_boost),
        (key_rows, value_rows, d_wkv_low, state_a, state_b),
        until_wide,
    )
    all_heads = gathered_ends(heads[:2])
    grad_output = scattered_sum(
        jnp.dot(attended.T, d_att, preferred_element_type=F32), "czyx", here
    )
    grad_recept = scattered_sum(
        jnp.dot(recept_low.T, d_recept_pre, preferred_element_type=F32), "czxy", here
    )
    d_recept_in = jnp.dot(d_recept_pre, accepting_map.T, preferred_element_type=F32)
    blocked = chunk_first[None, :] & (order[None, :] <= order[:, None])
    blocked = blocked & (order[None, :] > sequence_number)
    inner = chunk_has[None, :] & (order[None, :] > sequence_number)
    inner = inner & (order[None, :] < order[:, None])
    comes = (order > sequence_number) & ~jnp.any(blocked | inner, axis=1)
    gap_back = ((order - 1 - sequence_number) * tok_count).astype(F32)
    weigh_back = jnp.where(comes[:, None], jnp.exp(-rate[None, :] * gap_back[:, None]), 0.0)
    returning = jnp.sum(weigh_back[:, None, :] * all_heads, axis=0)
    rest = (tok_count - 1 - places).astype(F32)
    out_of = jnp.where(
        (until > tok_count)[:, None], jnp.exp(-rate[None, :] * rest[:, None]), 0.0
    )
    next_a = back_a + out_of * returning[0:1]
    next_b = back_b + out_of * returning[1:2]
    lift = jnp.exp(key_float)
    d_wkv = d_wkv_low.astype(F32)
    ratio = bonus * d_wkv / divisor
    gap_value = ratio * (value_float - wkv)
    d_key_low = (gap_value + lift * (value_float * next_a + next_b)).astype(BF16)
    d_value_low = (ratio + lift * next_a).astype(BF16)
    grad_first = jnp.sum(gap_value, axis=0)
    grad_decay = -rate * jnp.exp(-rate) * jnp.sum(next_a * state_a + next_b * state_b, axis=0)

    grad_key = scattered_sum(
        jnp.dot(key_low.T, d_key_low, preferred_element_type=F32), "cxyz", here
    )
    grad_value = scattered_sum(
        jnp.dot(value_low.T, d_value_low, preferred_element_type=F32), "cyxz", here
    )
    d_key_in = jnp.dot(d_key_low, lookup_map.T, preferred_element_type=F32)
    d_value_in = jnp.dot(d_value_low, payload_map.T, preferred_element_type=F32)
    d_normed, d_prior, (grad_mix_key, grad_mix_value, grad_mix_recept) = mix_one_back(
        (d_key_in, d_value_in, d_recept_in)
    )
    returned_first = passed_along(d_prior, "seq", -1)
    d_normed = jnp.concatenate([d_normed[:-1], d_normed[-1:] + returned_first], axis=0)
    d_stream_norm, grad_first_gain, grad_first_bias = first_back(d_normed)
    tokens_grad = (d_resid + d_stream_norm).astype(BF16)[None]

    small = jnp.stack(
        [
            grad_first_gain,
            grad_first_bias,
            grad_second_gain,
            grad_second_bias,
            grad_mix_key,
            grad_mix_value,
            grad_mix_recept,
            grad_ffn_mix_key,
            grad_ffn_mix_recept,
            grad_decay,
            grad_first,
        ]
    )
    owners = seq_count * fsdp_count
    share = model_width // owners
    small = small.reshape(-1, owners, share).transpose(1, 0, 2).reshape(owners, -1)
    small = lax.all_to_all(small, BOTH, split_axis=0, concat_axis=0, tiled=True)
    small = jnp.sum(small, axis=0).reshape(-1, share)
    large = (grad_key, grad_value, grad_recept, grad_output, grad_up, grad_down, grad_gate)
    return (mixed[None], tokens_grad, *large, *[small[i] for i in range(11)])


def solution(mesh):
    rows = P("fsdp", None)
    tokens = P("fsdp", "seq", None)
    return jax.shard_map(
        on_device,
        mesh=mesh,
        in_specs=(tokens, tokens, *[rows] * 8, *[P()] * 11),
        out_specs=(tokens, tokens, *[P(BOTH, None)] * 7, *[P(BOTH)] * 11),
        check_vma=False,
    )
```

time: 1350 us -> 621 us (0.46)
  waiting for transfers between devices: 1040 us -> 274 us
  starting transfers between devices: 32.5 us -> 136 us
  blocking collectives: 78.9 us -> 0 us
  matrix products: 99.7 us -> 62 us
  other arithmetic: 39.2 us -> 67.5 us
    reduce_scatter x7 -> x0, waiting for transfers between devices: 856 us -> none  [the longest x1 187 us: on_device(): lax.psum_scatter(partials[5], ('seq', 'fsdp'), scatter_dimension=0, tiled...]
    ppermute x0 -> x63, starting transfers between devices: none -> 107 us  [the longest x21 71.6 us: line_sum(): lax.ppermute(sent_up.astype(BF16), 'seq', [(2 * z + y, 2 * z + 2 + y) for...]
    ppermute x0 -> x63, waiting for transfers between devices: none -> 85.2 us  [the longest x21 43.1 us: flipped(): return lax.ppermute(value, axis, [(i, i ^ 1 << bit) for i in range(count)])]
    unnamed x1 -> x0, blocking collectives: 44 us -> none
    dot_general x24 -> x21, matrix products: 99.7 us -> 62 us  [the longest x1 8.34 us: on_device(): jnp.dot(squared.T, d_vals, preferred_element_type=F32)]
    add x8 -> x28, other arithmetic: 0.75 us -> 37.8 us  [the longest x21 33.2 us: scattered_sum(): value = mine.astype(F32) + got.astype(F32)]
    all_gather x7, waiting for transfers between devices: 142 us -> 179 us  [whole(): return lax.all_gather(weight, 'fsdp', axis=0, tiled=True)]
    all_to_all x2 -> x0, blocking collectives: 34.9 us -> none  [the longest x1 18.1 us: on_device(): lax.all_to_all(d_value_cols.astype(jnp.bfloat16), 'seq', split_axis=0, co...]
  transfers between devices with their start and end apart: 22 -> 77, of which waited for: 17 -> 30; matrix products, arithmetic and copies ran while one was open for 11% -> 22% of each run, Pallas kernels for 0% -> 2%
where the time goes in v1:
time: 621 us; the launch traced here: 613 us
  waiting for transfers between devices  274 us (44%)
  starting transfers between devices  136 us (22%)
  other arithmetic  67.5 us (11%)
  matrix products  62 us (10%)
  local copies, waits for them, and re-layouts  46.5 us (7%)
  between operations  16.8 us (3%)
  Pallas kernels  11.2 us (2%)
    all_gather x7, waiting for transfers between devices, whole(): return lax.all_gather(weight, 'fsdp', axis=0, tiled=True)  179 us
    ppermute x21, starting transfers between devices, line_sum(): lax.ppermute(sent_up.astype(BF16), 'seq', [(2 * z + y, 2 * z + 2 + y) for...  71.6 us
    ppermute x21, waiting for transfers between devices, flipped(): return lax.ppermute(value, axis, [(i, i ^ 1 << bit) for i in range(count)])  43.1 us
    add x21, other arithmetic, scattered_sum(): value = mine.astype(F32) + got.astype(F32)  33.2 us
    ppermute x21, waiting for transfers between devices, line_sum(): lax.ppermute(sent_up.astype(BF16), 'seq', [(2 * z + y, 2 * z + 2 + y) for...  22.3 us
    convert_element_type x21, local copies, waits for them, and re-layouts, scattered_sum(): got = flipped(away.astype(BF16), axis, bit)  21.6 us
    ppermute x21, waiting for transfers between devices, line_sum(): lax.ppermute(sent_down.astype(BF16), 'seq', [(2 * z + y, 2 * z - 2 + y) f...  19.8 us
    ppermute x21, starting transfers between devices, line_sum(): lax.ppermute(sent_down.astype(BF16), 'seq', [(2 * z + y, 2 * z - 2 + y) f...  18.9 us
  transfers between devices with their start and end apart: 77, of which 30 were waited for; matrix products, arithmetic and copies ran while one was open for 22% of the time, Pallas kernels for 2%

profile of v1, /device:TPU:0, one launch (start us, length us, event | category | flops | bytes accessed | tf_op | source)
XLA Modules:
  0.0 613.5 jit_solution(7093111086528040412)
XLA Ops:
  21.2 13.7 %all-gather.12.cloned.1.call-done = bf16[1024,1024]{1,0:T(8,128)(2,1)} async-done(((bf16[256,1024]{1,0:T(8,128)(2,1)}), bf16[1024,1024]{1,0:T(8,128)(2,1)}) %all-gather.12.cloned.1.call-update) | async-done | bytes 2097168 | tf_op jit(solution)/shard_map/all_gather | solution.py:257
  38.0 21.0 %all-gather.10.cloned.1.call-done = bf16[1024,1024]{1,0:T(8,128)(2,1)} async-done(((bf16[256,1024]{1,0:T(8,128)(2,1)}), bf16[1024,1024]{1,0:T(8,128)(2,1)}) %all-gather.10.cloned.1.call-update) | async-done | bytes 2097168 | tf_op jit(solution)/shard_map/all_gather | solution.py:257
  69.4 5.5 all-to-all-start
  74.9 8.4 %all-gather.8.cloned.1.call-done = bf16[1024,1024]{1,0:T(8,128)(2,1)} async-done(((bf16[256,1024]{1,0:T(8,128)(2,1)}), bf16[1024,1024]{1,0:T(8,128)(2,1)}) %all-gather.8.cloned.1.call-update) | async-done | bytes 2097168 | tf_op jit(solution)/shard_map/all_gather | solution.py:257
  90.3 17.0 %all-gather.14.cloned.1.call-done = bf16[1024,1024]{1,0:T(8,128)(2,1)} async-done(((bf16[256,1024]{1,0:T(8,128)(2,1)}), bf16[1024,1024]{1,0:T(8,128)(2,1)}) %all-gather.14.cloned.1.call-update) | async-done | bytes 2097168 | tf_op jit(solution)/shard_map/all_gather | solution.py:257
  120.9 10.4 %all-gather.16.cloned.1.call-done = bf16[1024,1024]{1,0:T(8,128)(2,1)} async-done(((bf16[256,1024]{1,0:T(8,128)(2,1)}), bf16[1024,1024]{1,0:T(8,128)(2,1)}) %all-gather.16.cloned.1.call-update) | async-done | bytes 2097168 | tf_op jit(solution)/shard_map/all_gather | solution.py:257
  134.7 56.4 %all-gather.18.cloned.1.call-done = bf16[1024,4096]{1,0:T(8,128)(2,1)} async-done(((bf16[256,4096]{1,0:T(8,128)(2,1)}), bf16[1024,4096]{1,0:T(8,128)(2,1)}) %all-gather.18.cloned.1.call-update) | async-done | bytes 8388624 | tf_op jit(solution)/shard_map/all_gather | solution.py:257
  191.1 8.0 %convolution_maximum_fusion = f32[256,4096]{1,0:T(8,128)} fusion(bf16[256,1024]{1,0:T(8,128)(2,1)} %get-tuple-element.63, bf16[1024,4096]{1,0:T(8,128)(2,1)} %all-gather.18.cloned.1.call-done), kind=kOutput, calls=%fused_computation.5 | convolution fusion | flops 2148532224 | bytes 13107200 | tf_op jit(solution)/shard_map/dot_general | solution.py:322
  199.1 51.9 %all-gather.20.cloned.1.call-done = bf16[4096,1024]{1,0:T(8,128)(2,1)} async-done(((bf16[1024,1024]{1,0:T(8,128)(2,1)}), bf16[4096,1024]{1,0:T(8,128)(2,1)}) %all-gather.20.cloned.1.call-update) | async-done | bytes 8388624 | tf_op jit(solution)/shard_map/all_gather | solution.py:257
  251.0 7.4 %fusion.1 = bf16[256,4096]{1,0:T(8,128)(2,1)S(1)} fusion(f32[256,4096]{1,0:T(8,128)} %convolution_maximum_fusion, bf16[4096,1024]{1,0:T(8,128)(2,1)} %all-gather.20.cloned.1.call-done, f32[256,1024]{1,0:T(8,128)} %fusion.11, bf16[1,256,1024]{2,1,0:T(8,128)(2,1)S(1)} %copy-done.17), kind=kOutput, calls=%fused_computation.7 | convolution fusion | flops 2151415808 | bytes 16252928 | tf_op jit(solution)/shard_map/dot_general | solution.py:331
  264.1 5.9 fusion.152
  273.4 8.3 %fusion.52 = f32[4096,1024]{1,0:T(8,128)} fusion(f32[256,4096]{1,0:T(8,128)S(1)} %copy-done.4, f32[256,1024]{1,0:T(8,128)S(1)} %copy-done.28, bf16[1,256,1024]{2,1,0:T(8,128)(2,1)S(1)} %copy-done.17), kind=kOutput, calls=%fused_computation.137 | convolution fusion | flops 2150367232 | bytes 22544384 | tf_op jit(solution)/shard_map/dot_general | solution.py:334
  291.9 6.0 fusion.3
  307.4 6.2 %shard_map.357 = (f32[256,1024]{1,0:T(8,128)}, f32[256,1024]{1,0:T(8,128)}, f32[8,1024]{1,0:T(8,128)}) custom-call(f32[1,1024]{1,0:T(1,128)} %bitcast.414, f32[1,1024]{1,0:T(1,128)} %bitcast.412, bf16[256,1024]{1,0:T(8,128)(2,1)} %convolution_convert_fusion.1.k_ref, bf16[256,1024]{1,0:T(8,128)(2,1)} %convolution_convert_fusion.v_ref, ...), custom_call_target="tpu_custom_call" | custom-call | flops 15728640 | bytes 4194304 | tf_op jit(solution)/shard_map/pallas_call | solution.py:129
  315.1 5.8 all-to-all-start.1
  354.0 5.7 all-to-all-start.2
  408.4 6.3 %collective-permute-done.5 = bf16[4,2,32,1024]{3,2,1,0:T(8,128)(2,1)S(1)} collective-permute-done((bf16[4,2,32,1024]{3,2,1,0:T(8,128)(2,1)S(1)}, bf16[4,2,32,1024]{3,2,1,0:T(8,128)(2,1)S(1)}, u32[]{:S(2)}, u32[]{:S(2)}) %collective-permute-start.5) | collective-permute-done | bytes 524320 | tf_op jit(solution)/shard_map/ppermute | solution.py:19
  422.7 8.5 %collective-permute-start.16 = (bf16[32,1024]{1,0:T(8,128)(2,1)S(1)}, bf16[32,1024]{1,0:T(8,128)(2,1)S(1)}, u32[]{:S(2)}, u32[]{:S(2)}) collective-permute-start(bf16[32,1024]{1,0:T(8,128)(2,1)S(1)} %get-tuple-element.99), channel_id=1, source_target_pairs={{0,8},{4,12},{1,9},{5,13},{2,10},{6,14},{3,11},{7,15}} | collective-permute-start | bytes 196616 | tf_op jit(solution)/shard_map/ppermute | solution.py:191
  460.1 6.1 collective-permute-done.37
  467.0 6.0 bitcast_add_fusion
  475.8 9.7 %bitcast_add_fusion.1 = f32[4,2,2,32,4096]{4,3,0,2,1:T(8,128)} fusion(bf16[4,2,2,32,4096]{4,3,0,2,1:T(8,128)(2,1)} %collective-permute-done.40, f32[4,2,2,2,32,4096]{5,4,3,2,1,0:T(8,128)} %bitcast.390, s32[]{:T(128)S(6)} %select_n.187), kind=kLoop, calls=%fused_computation.3 | loop fusion | flops 4194304 | bytes 20971524 | tf_op jit(solution)/shard_map/add | solution.py:171
  514.0 6.0 collective-permute-done.65
  524.6 12.2 %collective-permute-done.41 = bf16[4,2,32,4096]{3,2,0,1:T(8,128)(2,1)} collective-permute-done((bf16[4,2,32,4096]{3,2,0,1:T(8,128)(2,1)S(1)}, bf16[4,2,32,4096]{3,2,0,1:T(8,128)(2,1)}, u32[]{:S(2)}, u32[]{:S(2)}) %collective-permute-start.41) | collective-permute-done | bytes 2097184 | tf_op jit(solution)/shard_map/ppermute | solution.py:19
  542.4 13.3 %collective-permute-done.51 = bf16[4,128,1024]{2,1,0:T(8,128)(2,1)S(1)} collective-permute-done((bf16[4,128,1024]{2,1,0:T(8,128)(2,1)S(1)}, bf16[4,128,1024]{2,1,0:T(8,128)(2,1)S(1)}, u32[]{:S(2)}, u32[]{:S(2)}) %collective-permute-start.51) | collective-permute-done | bytes 1048608 | tf_op jit(solution)/shard_map/ppermute | solution.py:19
  (474 shorter events, 290.9 us)
Async XLA Ops:
  7.2 27.8 %all-gather.12.cloned.1.call-start = ((), (), s32[]{:S(2)}) async-start(), calls=%async_computation.5 | async-start | bytes 2621440 | tf_op jit(solution)/shard_map/all_gather | solution.py:257
  7.9 51.2 %all-gather.10.cloned.1.call-start = ((), (), s32[]{:S(2)}) async-start(), calls=%async_computation.4 | async-start | bytes 2621440 | tf_op jit(solution)/shard_map/all_gather | solution.py:257
  8.7 74.6 %all-gather.8.cloned.1.call-start = ((), (), s32[]{:S(2)}) async-start(), calls=%async_computation.3 | async-start | bytes 2621440 | tf_op jit(solution)/shard_map/all_gather | solution.py:257
  9.4 97.9 %all-gather.14.cloned.1.call-start = ((), (), s32[]{:S(2)}) async-start(), calls=%async_computation.6 | async-start | bytes 2621440 | tf_op jit(solution)/shard_map/all_gather | solution.py:257
  10.0 121.4 %all-gather.16.cloned.1.call-start = ((), (), s32[]{:S(2)}) async-start(), calls=%async_computation.7 | async-start | bytes 2621440 | tf_op jit(solution)/shard_map/all_gather | solution.py:257
  10.6 180.5 %all-gather.18.cloned.1.call-start = ((), (), s32[]{:S(2)}) async-start(), calls=%async_computation.8 | async-start | bytes 10485760 | tf_op jit(solution)/shard_map/all_gather | solution.py:257
  11.3 239.7 %all-gather.20.cloned.1.call-start = ((), (), s32[]{:S(2)}) async-start(), calls=%async_computation.9 | async-start | bytes 10485760 | tf_op jit(solution)/shard_map/all_gather | solution.py:257
  287.8 79.9 %collective-permute-start.58 = (bf16[4,2,2,32,1024]{4,3,1,2,0:T(8,128)(2,1)}, bf16[4,2,2,32,1024]{4,3,1,2,0:T(8,128)(2,1)}, u32[]{:S(2)}, u32[]{:S(2)}) collective-permute-start(bf16[4,2,2,32,1024]{4,3,1,2,0:T(8,128)(2,1)} %fusion.50), channel_id=1, source_target_pairs={{0,1},{1,0},{2,3},{3,2},{4,5},{5,4},{6,7},{7,6},{8,9},{9,8},{10,11... | collective-permute-start | bytes 3145736 | tf_op jit(solution)/shard_map/ppermute | solution.py:19
  323.8 48.9 %collective-permute-start.31 = (bf16[4,2,2,32,1024]{4,3,2,1,0:T(8,128)(2,1)}, bf16[4,2,2,32,1024]{4,3,2,1,0:T(8,128)(2,1)}, u32[]{:S(2)}, u32[]{:S(2)}) collective-permute-start(bf16[4,2,2,32,1024]{4,3,2,1,0:T(8,128)(2,1)} %fusion.51), channel_id=1, source_target_pairs={{0,1},{1,0},{2,3},{3,2},{4,5},{5,4},{6,7},{7,6},{8,9},{9,8},{10,11... | collective-permute-start | bytes 3145736 | tf_op jit(solution)/shard_map/ppermute | solution.py:19
  325.7 50.0 %collective-permute-start.22 = (bf16[4,2,2,32,1024]{4,3,2,1,0:T(8,128)(2,1)}, bf16[4,2,2,32,1024]{4,3,2,1,0:T(8,128)(2,1)}, u32[]{:S(2)}, u32[]{:S(2)}) collective-permute-start(bf16[4,2,2,32,1024]{4,3,2,1,0:T(8,128)(2,1)} %fusion.47), channel_id=1, source_target_pairs={{0,1},{1,0},{2,3},{3,2},{4,5},{5,4},{6,7},{7,6},{8,9},{9,8},{10,11... | collective-permute-start | bytes 3145736 | tf_op jit(solution)/shard_map/ppermute | solution.py:19
  339.0 40.1 %collective-permute-start.13 = (bf16[4,2,2,32,1024]{4,3,2,1,0:T(8,128)(2,1)}, bf16[4,2,2,32,1024]{4,3,2,1,0:T(8,128)(2,1)}, u32[]{:S(2)}, u32[]{:S(2)}) collective-permute-start(bf16[4,2,2,32,1024]{4,3,2,1,0:T(8,128)(2,1)} %fusion.46), channel_id=1, source_target_pairs={{0,1},{1,0},{2,3},{3,2},{4,5},{5,4},{6,7},{7,6},{8,9},{9,8},{10,11... | collective-permute-start | bytes 3145736 | tf_op jit(solution)/shard_map/ppermute | solution.py:19
  344.3 37.8 %collective-permute-start.4 = (bf16[4,2,2,32,1024]{4,3,2,1,0:T(8,128)(2,1)}, bf16[4,2,2,32,1024]{4,3,2,1,0:T(8,128)(2,1)}, u32[]{:S(2)}, u32[]{:S(2)}) collective-permute-start(bf16[4,2,2,32,1024]{4,3,2,1,0:T(8,128)(2,1)} %fusion.45), channel_id=1, source_target_pairs={{0,1},{1,0},{2,3},{3,2},{4,5},{5,4},{6,7},{7,6},{8,9},{9,8},{10,11... | collective-permute-start | bytes 3145736 | tf_op jit(solution)/shard_map/ppermute | solution.py:19
  400.3 66.7 %collective-permute-start.49 = (bf16[4,2,2,128,1024]{4,3,0,1,2:T(8,128)(2,1)S(1)}, bf16[4,2,2,128,1024]{4,3,0,1,2:T(8,128)(2,1)}, u32[]{:S(2)}, u32[]{:S(2)}) collective-permute-start(bf16[4,2,2,128,1024]{4,3,0,1,2:T(8,128)(2,1)S(1)} %copy-done.29), channel_id=1, source_target_pairs={{0,1},{1,0},{2,3},{3,2},{4,5},{5,4},{6,7},{7,6},{8,9},{9,8},{10,11... | collective-permute-start | bytes 12582920 | tf_op jit(solution)/shard_map/ppermute | solution.py:19
  402.1 73.8 %collective-permute-start.40 = (bf16[4,2,2,32,4096]{4,3,0,2,1:T(8,128)(2,1)}, bf16[4,2,2,32,4096]{4,3,0,2,1:T(8,128)(2,1)}, u32[]{:S(2)}, u32[]{:S(2)}) collective-permute-start(bf16[4,2,2,32,4096]{4,3,0,2,1:T(8,128)(2,1)} %fusion.2), channel_id=1, source_target_pairs={{0,1},{1,0},{2,3},{3,2},{4,5},{5,4},{6,7},{7,6},{8,9},{9,8},{10,11... | collective-permute-start | bytes 12582920 | tf_op jit(solution)/shard_map/ppermute | solution.py:19
  454.5 35.0 %collective-permute-start.25 = (bf16[2,2,32,1024]{3,2,1,0:T(8,128)(2,1)}, bf16[2,2,32,1024]{3,2,1,0:T(8,128)(2,1)}, u32[]{:S(2)}, u32[]{:S(2)}) collective-permute-start(bf16[2,2,32,1024]{3,2,1,0:T(8,128)(2,1)} %get-tuple-element.82), channel_id=1, source_target_pairs={{0,8},{4,12},{8,16},{12,20},{16,24},{20,28},{1,9},{5,13},{9,17},{1... | collective-permute-start | bytes 786440 | tf_op jit(solution)/shard_map/ppermute | solution.py:191
  458.8 32.8 %collective-permute-start.28 = (bf16[2,2,32,1024]{3,2,1,0:T(8,128)(2,1)S(1)}, bf16[2,2,32,1024]{3,2,1,0:T(8,128)(2,1)}, u32[]{:S(2)}, u32[]{:S(2)}) collective-permute-start(bf16[2,2,32,1024]{3,2,1,0:T(8,128)(2,1)S(1)} %fusion.86), channel_id=1, source_target_pairs={{8,0},{12,4},{16,8},{20,12},{24,16},{28,20},{9,1},{13,5},{17,9},{2... | collective-permute-start | bytes 786440 | tf_op jit(solution)/shard_map/ppermute | solution.py:196
  466.2 27.4 %collective-permute-start.20 = (bf16[32,1024]{1,0:T(8,128)(2,1)}, bf16[32,1024]{1,0:T(8,128)(2,1)S(1)}, u32[]{:S(2)}, u32[]{:S(2)}) collective-permute-start(bf16[32,1024]{1,0:T(8,128)(2,1)} %get-tuple-element.98), channel_id=1, source_target_pairs={{16,8},{20,12},{24,16},{28,20},{17,9},{21,13},{25,17},{29,21},{18,... | collective-permute-start | bytes 196616 | tf_op jit(solution)/shard_map/ppermute | solution.py:196
  473.4 46.7 %collective-permute-start.50 = (bf16[4,2,128,1024]{3,2,0,1:T(8,128)(2,1)S(1)}, bf16[4,2,128,1024]{3,2,0,1:T(8,128)(2,1)}, u32[]{:S(2)}, u32[]{:S(2)}) collective-permute-start(bf16[4,2,128,1024]{3,2,0,1:T(8,128)(2,1)S(1)} %fusion.5), channel_id=1, source_target_pairs={{0,2},{1,3},{2,0},{3,1},{4,6},{5,7},{6,4},{7,5},{8,10},{9,11},{10,... | collective-permute-start | bytes 6291464 | tf_op jit(solution)/shard_map/ppermute | solution.py:19
  488.1 48.7 %collective-permute-start.41 = (bf16[4,2,32,4096]{3,2,0,1:T(8,128)(2,1)S(1)}, bf16[4,2,32,4096]{3,2,0,1:T(8,128)(2,1)}, u32[]{:S(2)}, u32[]{:S(2)}) collective-permute-start(bf16[4,2,32,4096]{3,2,0,1:T(8,128)(2,1)S(1)} %fusion.4), channel_id=1, source_target_pairs={{0,4},{4,0},{8,12},{12,8},{16,20},{20,16},{24,28},{28,24},{1,5},{5... | collective-permute-start | bytes 6291464 | tf_op jit(solution)/shard_map/ppermute | solution.py:19
  507.8 33.8 %collective-permute-start.38 = (bf16[2,32,1024]{2,1,0:T(8,128)(2,1)}, bf16[2,32,1024]{2,1,0:T(8,128)(2,1)S(1)}, u32[]{:S(2)}, u32[]{:S(2)}) collective-permute-start(bf16[2,32,1024]{2,1,0:T(8,128)(2,1)} %fusion.107), channel_id=1, source_target_pairs={{0,4},{4,0},{8,12},{12,8},{16,20},{20,16},{24,28},{28,24},{1,5},{5... | collective-permute-start | bytes 393224 | tf_op jit(solution)/shard_map/ppermute | solution.py:19
  512.0 30.4 %collective-permute-start.29 = (bf16[2,32,1024]{2,1,0:T(8,128)(2,1)S(1)}, bf16[2,32,1024]{2,1,0:T(8,128)(2,1)S(1)}, u32[]{:S(2)}, u32[]{:S(2)}) collective-permute-start(bf16[2,32,1024]{2,1,0:T(8,128)(2,1)S(1)} %fusion.106), channel_id=1, source_target_pairs={{0,2},{1,3},{2,0},{3,1},{4,6},{5,7},{6,4},{7,5},{8,10},{9,11},{10,... | collective-permute-start | bytes 393224 | tf_op jit(solution)/shard_map/ppermute | solution.py:19
  522.7 32.9 %collective-permute-start.51 = (bf16[4,128,1024]{2,1,0:T(8,128)(2,1)S(1)}, bf16[4,128,1024]{2,1,0:T(8,128)(2,1)S(1)}, u32[]{:S(2)}, u32[]{:S(2)}) collective-permute-start(bf16[4,128,1024]{2,1,0:T(8,128)(2,1)S(1)} %fusion.49), channel_id=1, source_target_pairs={{0,4},{4,0},{8,12},{12,8},{16,20},{20,16},{24,28},{28,24},{1,5},{5... | collective-permute-start | bytes 3145736 | tf_op jit(solution)/shard_map/ppermute | solution.py:19
  539.5 34.1 %collective-permute-start.66 = (bf16[32,1024]{1,0:T(8,128)(2,1)S(1)}, bf16[32,1024]{1,0:T(8,128)(2,1)S(1)}, u32[]{:S(2)}, u32[]{:S(2)}) collective-permute-start(bf16[32,1024]{1,0:T(8,128)(2,1)S(1)} %fusion.125), channel_id=1, source_target_pairs={{0,4},{4,0},{8,12},{12,8},{16,20},{20,16},{24,28},{28,24},{1,5},{5... | collective-permute-start | bytes 196616 | tf_op jit(solution)/shard_map/ppermute | solution.py:19
  541.6 42.3 %collective-permute-start.39 = (bf16[32,1024]{1,0:T(8,128)(2,1)S(1)}, bf16[32,1024]{1,0:T(8,128)(2,1)S(1)}, u32[]{:S(2)}, u32[]{:S(2)}) collective-permute-start(bf16[32,1024]{1,0:T(8,128)(2,1)S(1)} %fusion.124), channel_id=1, source_target_pairs={{0,2},{1,3},{2,0},{3,1},{4,6},{5,7},{6,4},{7,5},{8,10},{9,11},{10,... | collective-permute-start | bytes 196616 | tf_op jit(solution)/shard_map/ppermute | solution.py:19
  (120 other events, 1195.5 us)
Sparse Core Ops, SparseCore 0:
  9.6 25.3 all-gather.11
  36.5 22.5 all-gather.9
  60.7 22.5 all-gather.7
  84.7 22.5 all-gather.13
  108.7 22.5 all-gather.15
  132.8 58.2 all-gather.17
  192.7 58.2 all-gather.19

commit v2 on v1

v2 whole, which is shorter than its diff:
```python
from functools import partial

import jax
import jax.numpy as jnp
from jax import lax
from jax.experimental import pallas as pl
from jax.experimental.pallas import tpu as pltpu
from jax.sharding import PartitionSpec as P

norm_eps = 1e-05
F32 = jnp.float32
BF16 = jnp.bfloat16
FAR = 1 << 20
SLIGHT = pl.CostEstimate(flops=1, bytes_accessed=1, transcendentals=0)
NEVER = 1e30
BOTH = ("seq", "fsdp")
LINKS = {"c": ("fsdp", 0), "x": ("fsdp", 1), "y": ("seq", 0), "z0": ("seq", 1)}
VMEM = pl.BlockSpec(memory_space=pltpu.VMEM)
SMEM = pl.BlockSpec(memory_space=pltpu.SMEM)
HBM = pl.BlockSpec(memory_space=pl.ANY)
WIDE = 512
STEP = 32


def after(value, *others):
    return lax.optimization_barrier((value, others))[0]


def flipped(value, axis, bit):
    count = lax.axis_size(axis)
    return lax.ppermute(value, axis, [(i, i ^ (1 << bit)) for i in range(count)])


def passed_along(value, axis, steps):
    count = lax.axis_size(axis)
    initial, last = (max(0, -steps), min(count, count - steps))
    return lax.ppermute(value, axis, [(source, source + steps) for source in range(initial, last)])


def token_starts(sequence_extents, positions):
    begins = jnp.cumsum(sequence_extents, axis=-1) - sequence_extents
    start_marks = (begins[..., :, None] == positions) & (sequence_extents[..., :, None] > 0)
    return jnp.any(start_marks, axis=-2)


def gathered_ends(ends):
    count = lax.axis_size("seq")
    copies = jnp.broadcast_to(ends[None], (count, *ends.shape))
    return lax.all_to_all(copies, "seq", split_axis=0, concat_axis=0, tiled=True)


def across(left, right):
    return lax.dot_general(left, right, (((1,), (1,)), ((), ())), preferred_element_type=F32)


def spread(mark, cols):
    return jnp.tile(mark, (1, cols // 128))


def normal(z):
    centred = z - jnp.mean(z, axis=-1, keepdims=True)
    return centred, lax.rsqrt(jnp.mean(centred * centred, axis=-1, keepdims=True) + norm_eps)


def normal_back(z, d, gain):
    centred, scale = normal(z)
    n = centred * scale
    e = d * gain
    inner = e - jnp.mean(e, axis=-1, keepdims=True) - n * jnp.mean(e * n, axis=-1, keepdims=True)
    return n, scale * inner


def one_later(block, previous):
    place = lax.broadcasted_iota(jnp.int32, block.shape, 0)
    return jnp.where(place == 0, previous, pltpu.roll(block, 1, 0))


def one_earlier(block, following):
    rows = block.shape[0]
    place = lax.broadcasted_iota(jnp.int32, block.shape, 0)
    return jnp.where(place == rows - 1, following, pltpu.roll(block, rows - 1, 0))


def folded(block):
    return sum(block[n : n + 8] for n in range(0, block.shape[0], 8))


def turn_blocks(index_ref, n, source, whole, away, mine):
    owners = index_ref.shape[1]
    block = source.shape[1] // owners
    whole[...] = source[...].T
    for r in range(owners):
        base = pl.multiple_of(index_ref[n, r] * block, block)
        out, at = (away, r) if r < owners // 2 else (mine, r - owners // 2)
        out[n, at * block : (at + 1) * block, :] = whole[pl.ds(base, block), :]


def turns_in_kernel(rows, streams):
    return (rows // streams[0].blocks.shape[0]) % 16 == 0


def turned_outside(acts, streams):
    rows = acts[0].shape[1]
    out = []
    for act, stream in zip(acts, streams):
        block = rows // stream.blocks.shape[0]
        index = stream.blocks[:, None] * block + jnp.arange(block)[None, :]
        out.append(jnp.take(act.T, index.reshape(-1), axis=0))
    out = jnp.stack(out)
    return out[:, : rows // 2], out[:, rows // 2 :]


class Piece:
    def __init__(self, part, offset, lead=(), rows=None, column=None):
        self.part, self.offset, self.lead = part, offset, lead
        self.rows, self.column = rows, column


def listed(plans):
    parts, offsets, copies = [], [], []
    for plan in plans:
        copies.append([])
        for piece in plan:
            known = [n for n, p in enumerate(parts) if p is piece.part]
            if not known:
                parts.append(piece.part)
                known = [len(parts) - 1]
            copies[-1].append((known[0], piece, len(offsets)))
            offsets.append(piece.offset)
    return parts, jnp.stack(offsets).astype(jnp.int32), copies


def copied(copies, ins, offset_ref, whole, sems, columns=None):
    started = []
    for n, (part, piece, which) in enumerate(copies):
        source = ins[part].at[piece.lead] if piece.lead else ins[part]
        if piece.rows is not None:
            source = source.at[piece.rows, :]
        base = pl.multiple_of(offset_ref[which], 16)
        target = pl.ds(base, source.shape[0])
        if piece.column is not None:
            taken = slice(piece.column, piece.column + source.shape[1])
            if columns is not None and taken.start != columns.start:
                continue
        elif columns is not None:
            taken = columns
            source = source.at[:, columns]
        else:
            taken = slice(0, source.shape[1])
        copy = pltpu.make_async_copy(source, whole.at[target, taken], sems.at[n])
        copy.start()
        started.append(copy)
    return started


def packed(entries):
    parts = []
    places = []
    for array, _, _, _ in entries:
        known = [n for n, p in enumerate(parts) if p is array]
        if not known:
            parts.append(array)
            known = [len(parts) - 1]
        places.append(known[0])
    wide = entries[0][3].stop - entries[0][3].start
    total_rows = sum(e[2] for e in entries)

    def body(offset_ref, *refs):
        ins, out, sems = refs[: len(parts)], refs[-2], refs[-1]
        started, at = [], 0
        for n, (_, _, rows, columns) in enumerate(entries):
            base = pl.multiple_of(offset_ref[n], 16)
            copy = pltpu.make_async_copy(
                ins[places[n]].at[pl.ds(base, rows), columns],
                out.at[at : at + rows, :],
                sems.at[n],
            )
            copy.start()
            started.append(copy)
            at += rows
        wait_all(started)

    return pl.pallas_call(
        body,
        grid_spec=pltpu.PrefetchScalarGridSpec(
            num_scalar_prefetch=1,
            grid=(),
            in_specs=[HBM] * len(parts),
            out_specs=VMEM,
            scratch_shapes=[pltpu.SemaphoreType.DMA((len(entries),))],
        ),
        out_shape=jax.ShapeDtypeStruct((total_rows, wide), BF16),
        cost_estimate=SLIGHT,
        compiler_params=pltpu.CompilerParams(vmem_limit_bytes=60 << 20),
    )(jnp.stack([e[1] for e in entries]).astype(jnp.int32), *parts)


def wait_all(copies):
    for copy in copies:
        copy.wait()


def by_columns(count, body):
    def step(j, carry):
        body(pl.ds(pl.multiple_of(j * WIDE, WIDE), WIDE))
        return carry

    lax.fori_loop(0, count // WIDE, step, 0)


def shapes_of(*pairs):
    return [jax.ShapeDtypeStruct(shape, dtype) for shape, dtype in pairs]


def scan_forward(rate_ref, k_ref, v_ref, since_ref, a_ref, b_ref, end_ref, cols):
    rows, wide = k_ref.shape[0], cols.stop - cols.start
    place = lax.broadcasted_iota(jnp.int32, (8, wide), 0)
    rate = rate_ref[:, cols]
    fades = [jnp.exp(-rate * float(d)) for d in (1, 2, 4)]
    carry_fade = jnp.exp(-rate * (place + 1).astype(F32))

    def step(i, state):
        base = pl.multiple_of(i * 16, 16)
        k = k_ref[pl.ds(base, 16), cols].astype(F32)
        v = v_ref[pl.ds(base, 16), cols].astype(F32)
        for h in range(2):
            at = pl.multiple_of(base + 8 * h, 8)
            part = slice(8 * h, 8 * h + 8)
            since = spread(since_ref[pl.ds(at, 8), :], wide)
            near = jnp.minimum(since, place)
            lift = jnp.exp(k[part])
            new = []
            for run, last, ref in zip((lift * v[part], lift), state, (a_ref, b_ref)):
                for d, fade in zip((1, 2, 4), fades):
                    run = run + jnp.where(near >= d, fade * pltpu.roll(run, d, 0), 0.0)
                run = run + jnp.where(since > place, carry_fade * last, 0.0)
                before = one_later(run, last)
                ref[pl.ds(at, 8), cols] = jnp.where(since >= 1, before, 0.0)
                new.append(run[7:8, :])
            state = tuple(new)
        return state

    zero = jnp.zeros((1, wide), F32)
    sa, sb = lax.fori_loop(0, rows // 16, step, (zero, zero))
    end_ref[0:1, cols] = sa
    end_ref[1:2, cols] = sb


def scan_backward(
    rate_ref,
    boost_ref,
    k_ref,
    v_ref,
    d_ref,
    a_in_ref,
    b_in_ref,
    until_ref,
    a_ref,
    b_ref,
    end_ref,
    cols,
):
    rows, wide = k_ref.shape[0], cols.stop - cols.start
    place = lax.broadcasted_iota(jnp.int32, (8, wide), 0)
    rate = rate_ref[:, cols]
    fades = [jnp.exp(-rate * float(d)) for d in (1, 2, 4)]
    carry_fade = jnp.exp(-rate * (8 - place).astype(F32))

    def step(j, state):
        base = pl.multiple_of((rows // 16 - 1 - j) * 16, 16)
        k = k_ref[pl.ds(base, 16), cols].astype(F32)
        v = v_ref[pl.ds(base, 16), cols].astype(F32)
        d = d_ref[pl.ds(base, 16), cols].astype(F32)
        for h in (1, 0):
            at = pl.multiple_of(base + 8 * h, 8)
            part = slice(8 * h, 8 * h + 8)
            until = spread(until_ref[pl.ds(at, 8), :], wide)
            near = jnp.minimum(until, 7 - place)
            bonus = jnp.exp(boost_ref[:, cols] + k[part])
            inverse = 1.0 / (b_in_ref[pl.ds(at, 8), cols] + bonus)
            wkv = (a_in_ref[pl.ds(at, 8), cols] + bonus * v[part]) * inverse
            first = d[part] * inverse
            new = []
            for run, last, ref in zip((first, -first * wkv), state, (a_ref, b_ref)):
                for q, fade in zip((1, 2, 4), fades):
                    run = run + jnp.where(near >= q, fade * pltpu.roll(run, 8 - q, 0), 0.0)
                run = run + jnp.where(until >= 8 - place, carry_fade * last, 0.0)
                ref[pl.ds(at, 8), cols] = jnp.where(until >= 1, one_earlier(run, last), 0.0)
                new.append(run[0:1, :])
            state = tuple(new)
        return state

    zero = jnp.zeros((1, wide), F32)
    sa, sb = lax.fori_loop(0, rows // 16, step, (zero, zero))
    end_ref[0:1, cols] = sa
    end_ref[1:2, cols] = sb


def carried(gap_ref, ends_ref, rate):
    cols = rate.shape[1]
    a = b = jnp.zeros((1, cols), F32)
    for j in range(gap_ref.shape[0]):
        weigh = jnp.exp(-rate * spread(gap_ref[j : j + 1, :], cols))
        a = a + weigh * ends_ref[j, 0:1, :]
        b = b + weigh * ends_ref[j, 1:2, :]
    return a, b


def norm_and_mix(track, prior, gain, bias, weights, since, others, turns):
    tokens, cols = track.shape
    count, more = len(weights), len(others)
    streams = [stream for _, stream in turns]
    inside = turns_in_kernel(cols, streams)

    def body(*refs):
        index_ref, track_ref, prior_ref, gain_ref, bias_ref, since_ref = refs[:6]
        mix_refs, other_refs = refs[6 : 6 + count], refs[6 + count : 6 + count + more]
        outs = refs[6 + count + more :]
        mixed, rest = outs[:count], outs[count:]
        gain, bias = gain_ref[...], bias_ref[...]

        def norm(z):
            centred, scale = normal(z)
            return centred * scale * gain + bias

        def step(i, last):
            at = pl.ds(pl.multiple_of(i * STEP, STEP), STEP)
            now = norm(track_ref[at, :].astype(F32))
            then = one_later(now, last)
            then = jnp.where(spread(since_ref[at, :], cols) == 0, 0.0, then)
            for out, mix_ref in zip(mixed, mix_refs):
                weight = mix_ref[...]
                out[at, :] = (now * weight + then * (1.0 - weight)).astype(BF16)
            return now[STEP - 1 :, :]

        lax.fori_loop(0, tokens // STEP, step, norm(prior_ref[...].astype(F32)))
        if inside:
            away, mine, whole = rest
            sources = [*other_refs, *mixed]
            for n, (which, _) in enumerate(turns):
                turn_blocks(index_ref, n, sources[which], whole, away, mine)

    low = ((tokens, cols), BF16)
    half = ((len(streams), cols // 2, tokens), BF16)
    index = jnp.stack([s.blocks for s in streams])
    out = pl.pallas_call(
        body,
        in_specs=[SMEM] + [VMEM] * (5 + count + more),
        out_specs=[VMEM] * (count + 2 * inside),
        out_shape=shapes_of(*[low] * count, *[half, half] * inside),
        scratch_shapes=[pltpu.VMEM((cols, tokens), BF16)] * inside,
        cost_estimate=SLIGHT,
        compiler_params=pltpu.CompilerParams(vmem_limit_bytes=60 << 20),
    )(index, track, prior, gain, bias, since, *weights, *others)
    if inside:
        return out[:count], out[count], out[count + 1]
    sources = [*others, *out]
    return out, *turned_outside([sources[which] for which, _ in turns], streams)


def keys_and_values(key_low, value_low, plans, rate, since):
    tokens, cols = key_low.shape
    parts, offsets, copies = listed(plans)
    most = max(len(c) for c in copies)

    def body(offset_ref, key_ref, value_ref, rate_ref, since_ref, *refs):
        ins = refs[: len(parts)]
        k_ref, v_ref, a_ref, b_ref, end_ref, w_k, w_v, sems = refs[len(parts) :]
        started = [
            copied(copies[n], ins, offset_ref, w, sems.at[n]) for n, w in enumerate((w_k, w_v))
        ]
        for n, (low, w, out) in enumerate(((key_ref, w_k, k_ref), (value_ref, w_v, v_ref))):
            wait_all(started[n])

            def one(at, low=low, w=w, out=out):
                out[:, at] = jnp.dot(low[...], w[:, at], preferred_element_type=F32).astype(BF16)

            by_columns(cols, one)
        end_ref[...] = jnp.zeros_like(end_ref)
        for first in range(0, cols, 256):
            scan_forward(
                rate_ref, k_ref, v_ref, since_ref, a_ref, b_ref, end_ref, slice(first, first + 256)
            )

    low, full = ((tokens, cols), BF16), ((tokens, cols), F32)
    return pl.pallas_call(
        body,
        grid_spec=pltpu.PrefetchScalarGridSpec(
            num_scalar_prefetch=1,
            grid=(),
            in_specs=[VMEM] * 4 + [HBM] * len(parts),
            out_specs=[VMEM] * 5,
            scratch_shapes=[
                pltpu.VMEM((cols, cols), BF16),
                pltpu.VMEM((cols, cols), BF16),
                pltpu.SemaphoreType.DMA((2, most)),
            ],
        ),
        out_shape=shapes_of(low, low, full, full, ((8, cols), F32)),
        cost_estimate=SLIGHT,
        compiler_params=pltpu.CompilerParams(vmem_limit_bytes=60 << 20),
    )(offsets, key_low, value_low, rate, since, *parts)


def attend(recept_low, k, v, part_a, part_b, ends, gap, rate, boost, since, track, plans):
    tokens, cols = recept_low.shape
    parts, offsets, copies = listed(plans)
    most = max(len(c) for c in copies)

    def body(offset_ref, *refs):
        low_ref, k_ref, v_ref, pa_ref, pb_ref, ends_ref, gap_ref = refs[:7]
        rate_ref, boost_ref, since_ref, track_ref = refs[7:11]
        ins = refs[11 : 11 + len(parts)]
        recept_ref, att_ref, resid_ref, a_ref, b_ref, last_ref, w_r, w_e, sems = refs[
            11 + len(parts) :
        ]
        started = [
            copied(copies[n], ins, offset_ref, w, sems.at[n]) for n, w in enumerate((w_r, w_e))
        ]
        rate, boost = rate_ref[...], boost_ref[...]
        enter_a, enter_b = carried(gap_ref, ends_ref, rate)
        wait_all(started[0])

        def gate(at):
            pre = jnp.dot(low_ref[...], w_r[:, at], preferred_element_type=F32)
            recept_ref[:, at] = jax.nn.sigmoid(pre)

        by_columns(cols, gate)

        def step(i, carry):
            at = pl.ds(pl.multiple_of(i * STEP, STEP), STEP)
            place = i * STEP + lax.broadcasted_iota(jnp.int32, (STEP, cols), 0)
            inside = spread(since_ref[at, :], cols) > place
            fade = jnp.where(inside, jnp.exp(-rate * place.astype(F32)), 0.0)
            a = pa_ref[at, :] + fade * enter_a
            b = pb_ref[at, :] + fade * enter_b
            a_ref[at, :] = a
            b_ref[at, :] = b
            bonus = jnp.exp(boost + k_ref[at, :].astype(F32))
            wkv = (a + bonus * v_ref[at, :].astype(F32)) / (b + bonus)
            low = wkv.astype(BF16).astype(F32)
            att_ref[at, :] = (recept_ref[at, :] * low).astype(BF16)
            return carry

        lax.fori_loop(0, tokens // STEP, step, 0)
        wait_all(started[1])

        def emit(at):
            out = jnp.dot(att_ref[...], w_e[:, at], preferred_element_type=F32)
            resid_ref[:, at] = track_ref[:, at].astype(F32) + out

        by_columns(cols, emit)
        last_ref[...] = resid_ref[tokens - 1 :, :]

    low, full = ((tokens, cols), BF16), ((tokens, cols), F32)
    return pl.pallas_call(
        body,
        grid_spec=pltpu.PrefetchScalarGridSpec(
            num_scalar_prefetch=1,
            grid=(),
            in_specs=[VMEM] * 11 + [HBM] * len(parts),
            out_specs=[VMEM] * 6,
            scratch_shapes=[
                pltpu.VMEM((cols, cols), BF16),
                pltpu.VMEM((cols, cols), BF16),
                pltpu.SemaphoreType.DMA((2, most)),
            ],
        ),
        out_shape=shapes_of(full, low, full, full, full, ((1, cols), F32)),
        cost_estimate=SLIGHT,
        compiler_params=pltpu.CompilerParams(vmem_limit_bytes=60 << 20),
    )(
        offsets,
        recept_low,
        k,
        v,
        part_a,
        part_b,
        ends,
        gap,
        rate,
        boost,
        since,
        track,
        *parts,
    )


def channel_mix(up_low, gate_low, resid, slope, up_weight, gate_weight, since, plans, stream):
    tokens, model = up_low.shape
    ff = plans[0][0].part.shape[-1]
    parts, offsets, copies = listed(plans)
    most = max(len(c) for c in copies)
    spans = 4
    span = ff // spans
    owners = stream.blocks.shape[0]
    block = ff // owners
    inside = block % 128 == 0

    def body(offset_ref, index_ref, up_ref, gate_ref, resid_ref, slope_ref, *refs):
        up_mix, gate_mix, since_ref = refs[:3]
        ins = refs[3 : 3 + len(parts)]
        outs = refs[3 + len(parts) :]
        mixed_ref, d_out_ref, squared_ref, d_pre_ref, d_up_ref, d_gate_ref, row_ref = outs[:7]
        w_up, w_down, w_gate, positive, sems = outs[-5:]
        gate_copies = copied(copies[2], ins, offset_ref, w_gate, sems.at[spans + 1])
        up_copies = [
            copied(
                copies[0], ins, offset_ref, w_up, sems.at[n], slice(n * span, (n + 1) * span)
            )
            for n in range(spans)
        ]
        down_copies = copied(copies[1], ins, offset_ref, w_down, sems.at[spans])
        wait_all(gate_copies)

        def gate_step(cols):
            gate = jnp.dot(gate_ref[...], w_gate[:, cols], preferred_element_type=F32)
            d_gate_ref[:, cols] = jax.nn.sigmoid(gate)

        by_columns(model, gate_step)

        def up_step(j, carry):
            cols = pl.ds(pl.multiple_of(j * WIDE, WIDE), WIDE)
            pre = jnp.dot(up_ref[...], w_up[:, cols], preferred_element_type=F32)
            pre = jnp.maximum(pre, 0.0)
            positive[:, cols] = pre
            squared_ref[:, cols] = (pre * pre).astype(BF16)
            return carry

        for n in range(spans):
            wait_all(up_copies[n])
            lax.fori_loop(n * span // WIDE, (n + 1) * span // WIDE, up_step, 0)
        wait_all(down_copies)

        def down_step(cols):
            values = jnp.dot(squared_ref[...], w_down[:, cols], preferred_element_type=F32)
            gating = d_gate_ref[:, cols]
            upstream = slope_ref[:, cols].astype(F32)
            mixed_ref[:, cols] = (resid_ref[:, cols] + gating * values).astype(BF16)
            d_out_ref[0, :, cols] = (upstream * gating).astype(BF16)
            d_out_ref[1, :, cols] = (upstream * values * gating * (1.0 - gating)).astype(BF16)

        by_columns(model, down_step)
        d_up_ref[...] = jnp.zeros_like(d_up_ref)

        def back_step(cols):
            d_squared = across(d_out_ref[0], w_down[cols, :])
            d_pre = (d_squared * 2.0 * positive[:, cols]).astype(BF16)
            d_pre_ref[:, cols] = d_pre
            d_up_ref[...] += across(d_pre, w_up[:, cols])

        by_columns(ff, back_step)

        def gate_back_step(cols):
            d_gate_ref[:, cols] = across(d_out_ref[1], w_gate[cols, :])

        by_columns(model, gate_back_step)
        row = (1.0 - up_mix[...]) * d_up_ref[0:1, :] + (1.0 - gate_mix[...]) * d_gate_ref[0:1, :]
        row_ref[...] = jnp.where(spread(since_ref[0:1, :], model) == 0, 0.0, row)
        if inside:
            away, mine = outs[7:9]

            def turn(r, carry):
                for out, half in ((away, 0), (mine, owners // 2)):
                    at = pl.multiple_of(index_ref[half + r] * block, block)
                    base = pl.multiple_of(r * block, block)
                    out[0, pl.ds(base, block), :] = squared_ref[:, pl.ds(at, block)].T
                return carry

            lax.fori_loop(0, owners // 2, turn, 0)

    low, full, wide = ((tokens, model), BF16), ((tokens, model), F32), ((tokens, ff), BF16)
    half = ((1, ff // 2, tokens), BF16)
    out = pl.pallas_call(
        body,
        grid_spec=pltpu.PrefetchScalarGridSpec(
            num_scalar_prefetch=2,
            grid=(),
            in_specs=[VMEM] * 7 + [HBM] * len(parts),
            out_specs=[VMEM] * (7 + 2 * inside),
            scratch_shapes=[
                pltpu.VMEM((model, ff), BF16),
                pltpu.VMEM((ff, model), BF16),
                pltpu.VMEM((model, model), BF16),
                pltpu.VMEM((tokens, ff), F32),
                pltpu.SemaphoreType.DMA((spans + 2, most)),
            ],
        ),
        out_shape=shapes_of(
            low,
            ((2, tokens, model), BF16),
            wide,
            wide,
            full,
            full,
            ((1, model), F32),
            *[half, half] * inside,
        ),
        cost_estimate=SLIGHT,
        compiler_params=pltpu.CompilerParams(vmem_limit_bytes=60 << 20),
    )(
        offsets,
        stream.blocks,
        up_low,
        gate_low,
        resid,
        slope,
        up_weight,
        gate_weight,
        since,
        *parts,
    )
    if inside:
        return out
    return [*out, *turned_outside([out[2]], [stream])]


def shift_back(z_of, d_of, returned, since_ref, prior, mixes, gain, bias, tokens, cols, put):
    count = len(mixes)

    def norm(z):
        centred, scale = normal(z)
        return centred * scale * gain + bias

    def lost(at):
        total = sum((1.0 - m) * d_of(n, at) for n, m in enumerate(mixes))
        return jnp.where(spread(since_ref[at, :], cols) == 0, 0.0, total)

    steps = tokens // STEP

    def step(i, carry):
        last, sums = carry[0], carry[1:]
        at = pl.ds(pl.multiple_of(i * STEP, STEP), STEP)
        z = z_of(at)
        now = norm(z)
        then = one_later(now, last)
        then = jnp.where(spread(since_ref[at, :], cols) == 0, 0.0, then)
        difference = now - then
        grads = [d_of(n, at) for n in range(count)]
        sums = [s + folded(difference * g) for s, g in zip(sums, grads)]
        ahead = jnp.minimum((i + 1) * STEP, tokens - STEP)
        ahead = lost(pl.ds(pl.multiple_of(ahead, STEP), STEP))[0:1, :]
        ahead = jnp.where(i == steps - 1, returned, ahead)
        d = one_earlier(lost(at), ahead) + sum(m * g for m, g in zip(mixes, grads))
        put(i, at, z, d)
        return (now[STEP - 1 :, :], *sums)

    zero = jnp.zeros((8, cols), F32)
    return lax.fori_loop(0, steps, step, (norm(prior), *[zero] * count))[1:]


def total(folded_sum):
    return jnp.sum(folded_sum, axis=0, keepdims=True)


def middle_back(
    d_up,
    d_gate,
    returned,
    resid,
    prior,
    slope,
    gain,
    bias,
    mixes,
    since,
    until,
    plan,
    recept,
    k,
    v,
    a,
    b,
    rate,
    boost,
):
    tokens, cols = resid.shape
    parts, offsets, copies = listed([plan])
    most = len(copies[0])

    def body(offset_ref, *refs):
        d_up_ref, d_gate_ref, returned_ref, resid_ref, prior_ref, slope_ref = refs[:6]
        gain_ref, bias_ref, up_mix, gate_mix, since_ref, until_ref = refs[6:12]
        recept_ref, k_ref, v_ref, a_ref, b_ref, rate_ref, boost_ref = refs[12:19]
        ins, rest = refs[19 : 19 + len(parts)], refs[19 + len(parts) :]
        d_resid_ref, d_att_ref, d_recept_ref, d_wkv_ref = rest[:4]
        next_a, next_b, end_ref, vec_ref = rest[4:8]
        d_attended, gain_sum, bias_sum, w_ref, sems = rest[8:]
        started = copied(copies[0], ins, offset_ref, w_ref, sems)
        gain, boost = gain_ref[...], boost_ref[...]
        gain_sum[...] = jnp.zeros_like(gain_sum)
        bias_sum[...] = jnp.zeros_like(bias_sum)

        def put(i, at, z, d):
            n, d_z = normal_back(z, d, gain)
            gain_sum[...] += folded(d * n)
            bias_sum[...] += folded(d)
            d_z = slope_ref[at, :].astype(F32) + d_z
            d_resid_ref[at, :] = d_z
            d_att_ref[at, :] = d_z.astype(BF16)

        sums = shift_back(
            lambda at: resid_ref[at, :],
            lambda n, at: (d_up_ref, d_gate_ref)[n][at, :],
            returned_ref[...],
            since_ref,
            prior_ref[...],
            [up_mix[...], gate_mix[...]],
            gain,
            bias_ref[...],
            tokens,
            cols,
            put,
        )
        vec_ref[...] = jnp.zeros_like(vec_ref)
        for n, part in enumerate([gain_sum[...], bias_sum[...], *sums]):
            vec_ref[n : n + 1, :] = total(part)

        wait_all(started)

        def back(at):
            d_attended[:, at] = across(d_att_ref[...], w_ref[at, :])

        by_columns(cols, back)

        def step(i, carry):
            at = pl.ds(pl.multiple_of(i * STEP, STEP), STEP)
            gate, d = recept_ref[at, :], d_attended[at, :]
            bonus = jnp.exp(boost + k_ref[at, :].astype(F32))
            wkv = (a_ref[at, :] + bonus * v_ref[at, :].astype(F32)) / (b_ref[at, :] + bonus)
            low = wkv.astype(BF16).astype(F32)
            d_wkv_ref[at, :] = (d * gate).astype(BF16)
            d_recept_ref[at, :] = (d * low * gate * (1.0 - gate)).astype(BF16)
            return carry

        lax.fori_loop(0, tokens // STEP, step, 0)
        end_ref[...] = jnp.zeros_like(end_ref)
        for first in range(0, cols, 256):
            scan_backward(
                rate_ref,
                boost_ref,
                k_ref,
                v_ref,
                d_wkv_ref,
                a_ref,
                b_ref,
                until_ref,
                next_a,
                next_b,
                end_ref,
                slice(first, first + 256),
            )

    low, full, vec = ((tokens, cols), BF16), ((tokens, cols), F32), ((8, cols), F32)
    return pl.pallas_call(
        body,
        grid_spec=pltpu.PrefetchScalarGridSpec(
            num_scalar_prefetch=1,
            grid=(),
            in_specs=[VMEM] * 19 + [HBM] * len(parts),
            out_specs=[VMEM] * 8,
            scratch_shapes=[
                pltpu.VMEM((tokens, cols), F32),
                pltpu.VMEM((8, cols), F32),
                pltpu.VMEM((8, cols), F32),
                pltpu.VMEM((cols, cols), BF16),
                pltpu.SemaphoreType.DMA((most,)),
            ],
        ),
        out_shape=shapes_of(full, low, low, low, full, full, vec, vec),
        cost_estimate=SLIGHT,
        compiler_params=pltpu.CompilerParams(vmem_limit_bytes=60 << 20),
    )(
        offsets,
        d_up,
        d_gate,
        returned,
        resid,
        prior,
        slope,
        gain,
        bias,
        *mixes,
        since,
        until,
        recept,
        k,
        v,
        a,
        b,
        rate,
        boost,
        *parts,
    )


def recurrence_back(back_a, back_b, heads, gap, k, v, a, b, d_wkv, until, rate, boost):
    tokens, cols = k.shape

    def body(*refs):
        back_a_ref, back_b_ref, heads_ref, gap_ref, k_ref, v_ref, a_ref, b_ref = refs[:8]
        d_ref, until_ref, rate_ref, boost_ref, d_two_ref, vec_ref = refs[8:]
        rate, boost = rate_ref[...], boost_ref[...]
        from_a, from_b = carried(gap_ref, heads_ref, rate)

        def step(i, carry):
            at = pl.ds(pl.multiple_of(i * STEP, STEP), STEP)
            place = i * STEP + lax.broadcasted_iota(jnp.int32, (STEP, cols), 0)
            inside = spread(until_ref[at, :], cols) > tokens
            fade = jnp.exp(-rate * (tokens - 1 - place).astype(F32))
            fade = jnp.where(inside, fade, 0.0)
            next_a = back_a_ref[at, :] + fade * from_a
            next_b = back_b_ref[at, :] + fade * from_b
            a, b = a_ref[at, :], b_ref[at, :]
            key, value = k_ref[at, :].astype(F32), v_ref[at, :].astype(F32)
            lift, bonus = jnp.exp(key), jnp.exp(boost + key)
            ratio = bonus / (b + bonus)
            wkv = (a + bonus * value) / (b + bonus)
            ratio = ratio * d_ref[at, :].astype(F32)
            gap_value = ratio * (value - wkv)
            d_key = gap_value + lift * (value * next_a + next_b)
            d_two_ref[0, at, :] = d_key.astype(BF16)
            d_two_ref[1, at, :] = (ratio + lift * next_a).astype(BF16)
            return carry[0] + folded(next_a * a + next_b * b), carry[1] + folded(gap_value)

        zero = jnp.zeros((8, cols), F32)
        decay, first = lax.fori_loop(0, tokens // STEP, step, (zero, zero))
        vec_ref[...] = jnp.zeros_like(vec_ref)
        vec_ref[0:1, :] = -rate * jnp.exp(-rate) * total(decay)
        vec_ref[1:2, :] = total(first)

    return pl.pallas_call(
        body,
        in_specs=[VMEM] * 12,
        out_specs=[VMEM] * 2,
        out_shape=shapes_of(((2, tokens, cols), BF16), ((8, cols), F32)),
        cost_estimate=SLIGHT,
        compiler_params=pltpu.CompilerParams(vmem_limit_bytes=60 << 20),
    )(back_a, back_b, heads, gap, k, v, a, b, d_wkv, until, rate, boost)


def entry_back(d_kv, d_recept, plans, track, prior, gain, bias, mixes, since):
    tokens, cols = track.shape
    parts, offsets, copies = listed(plans)
    most = max(len(c) for c in copies)

    def body(offset_ref, d_kv_ref, d_recept_ref, track_ref, prior_ref, gain_ref, bias_ref, *refs):
        mix_refs, since_ref = refs[:3], refs[3]
        ins, rest = refs[4 : 4 + len(parts)], refs[4 + len(parts) :]
        d_ref, row_ref, vec_ref = rest[:3]
        grads, weights, sems = rest[3:6], rest[6:9], rest[9]
        started = [
            copied(copies[n], ins, offset_ref, w, sems.at[n]) for n, w in enumerate(weights)
        ]
        lows = (d_kv_ref.at[0], d_kv_ref.at[1], d_recept_ref)
        for copies_of, low, weight, out in zip(started, lows, weights, grads):
            wait_all(copies_of)

            def one(at, low=low, weight=weight, out=out):
                out[:, at] = across(low[...], weight[at, :])

            by_columns(cols, one)

        mixes = [m[...] for m in mix_refs]

        def put(i, at, z, d):
            d_ref[at, :] = d

        sums = shift_back(
            lambda at: track_ref[at, :].astype(F32),
            lambda n, at: grads[n][at, :],
            jnp.zeros((1, cols), F32),
            since_ref,
            prior_ref[...].astype(F32),
            mixes,
            gain_ref[...],
            bias_ref[...],
            tokens,
            cols,
            put,
        )
        row = sum((1.0 - m) * g[0:1, :] for m, g in zip(mixes, grads))
        row_ref[...] = jnp.where(spread(since_ref[0:1, :], cols) == 0, 0.0, row)
        vec_ref[...] = jnp.zeros_like(vec_ref)
        for n, part in enumerate(sums):
            vec_ref[n : n + 1, :] = total(part)

    full = ((tokens, cols), F32)
    return pl.pallas_call(
        body,
        grid_spec=pltpu.PrefetchScalarGridSpec(
            num_scalar_prefetch=1,
            grid=(),
            in_specs=[VMEM] * 10 + [HBM] * len(parts),
            out_specs=[VMEM] * 3,
            scratch_shapes=[pltpu.VMEM((tokens, cols), F32)] * 3
            + [pltpu.VMEM((cols, cols), BF16)] * 3
            + [pltpu.SemaphoreType.DMA((3, most))],
        ),
        out_shape=shapes_of(full, ((1, cols), F32), ((8, cols), F32)),
        cost_estimate=SLIGHT,
        compiler_params=pltpu.CompilerParams(vmem_limit_bytes=60 << 20),
    )(offsets, d_kv, d_recept, track, prior, gain, bias, *mixes, since, *parts)


def first_norm_back(d_normed, returned, track, d_resid, gain):
    tokens, cols = track.shape

    def body(d_ref, returned_ref, track_ref, d_resid_ref, gain_ref, out_ref, vec_ref):
        gain = gain_ref[...]

        def step(i, carry):
            at = pl.ds(pl.multiple_of(i * STEP, STEP), STEP)
            place = i * STEP + lax.broadcasted_iota(jnp.int32, (STEP, cols), 0)
            d = d_ref[at, :] + jnp.where(place == tokens - 1, returned_ref[...], 0.0)
            n, d_z = normal_back(track_ref[at, :].astype(F32), d, gain)
            out_ref[at, :] = (d_resid_ref[at, :] + d_z).astype(BF16)
            return carry[0] + folded(d * n), carry[1] + folded(d)

        zero = jnp.zeros((8, cols), F32)
        gain_sum, bias_sum = lax.fori_loop(0, tokens // STEP, step, (zero, zero))
        vec_ref[...] = jnp.zeros_like(vec_ref)
        vec_ref[0:1, :] = total(gain_sum)
        vec_ref[1:2, :] = total(bias_sum)

    return pl.pallas_call(
        body,
        in_specs=[VMEM] * 5,
        out_specs=[VMEM] * 2,
        out_shape=shapes_of(((tokens, cols), BF16), ((8, cols), F32)),
        cost_estimate=SLIGHT,
        compiler_params=pltpu.CompilerParams(vmem_limit_bytes=60 << 20),
    )(d_normed, returned, track, d_resid, gain)


class Line:
    def __init__(self):
        self.last = None

    def hold(self, value):
        return value if self.last is None else after(value, self.last)

    def mark(self, value):
        self.last = value
        return value

    def pass_on(self, value):
        return self.mark(self.hold(value))


class Stream:
    def __init__(self, names):
        seq_bits = lax.axis_size("seq").bit_length() - 1
        fsdp_bits = lax.axis_size("fsdp").bit_length() - 1
        links = {"c": ("fsdp", 0), "x": ("fsdp", 1), "y": ("seq", 0)}
        links.update({f"z{i}": ("seq", i + 1) for i in range(seq_bits - 1)})
        for i in range(seq_bits - 1):
            if f"z{i}" not in names:
                names = [*names, f"z{i}"]
        self.links = [links[name] for name in names]
        places = [bit + (fsdp_bits if axis == "seq" else 0) for axis, bit in self.links]
        count = len(places)
        owners = 1 << count
        self.masks = [
            sum((1 - ((r >> (count - 1 - p)) & 1)) << place for p, place in enumerate(places))
            for r in range(owners)
        ]
        me = lax.axis_index("seq") * lax.axis_size("fsdp") + lax.axis_index("fsdp")
        self.blocks = jnp.array(self.masks, jnp.int32) ^ me.astype(jnp.int32)


def products(pairs, columns=None):
    pairs = [[x if isinstance(x, tuple) else (x, None) for x in p] for p in pairs]
    rows, tokens = pairs[0][0][0].shape[-2:]
    wide = 512
    counts = [p[2][0].shape[-1] // wide for p in pairs]
    skip = 0
    if columns is not None:
        skip, counts = columns.start // wide, [(columns.stop - columns.start) // wide]
    firsts = [sum(counts[:n]) for n in range(len(counts))]
    total = sum(counts)

    def body(*refs):
        send, keep = refs[-2:]
        for n in range(len(pairs)):
            left_a, left_b, right_a, right_b = refs[4 * n : 4 * n + 4]

            def one(left_a=left_a, left_b=left_b, right_a=right_a, right_b=right_b):
                value = jnp.dot(left_a[...], right_a[...], preferred_element_type=F32)
                value = value + jnp.dot(left_b[...], right_b[...], preferred_element_type=F32)
                send[...] = value[: rows // 2].astype(BF16)
                keep[...] = value[rows // 2 :].astype(BF16)

            if len(pairs) == 1:
                one()
            else:
                i = pl.program_id(0)
                pl.when((i >= firsts[n]) & (i < firsts[n] + counts[n]))(one)

    def spec(lead, block, index):
        if lead is None:
            return pl.BlockSpec(block, index)
        return pl.BlockSpec((None, *block), lambda i: (lead, *index(i)))

    specs = []
    for n, p in enumerate(pairs):
        for q, (_, lead) in enumerate(p):
            if q < 2:
                specs.append(spec(lead, (rows, tokens), lambda i: (0, 0)))
            else:
                specs.append(
                    spec(
                        lead,
                        (tokens, wide),
                        lambda i, n=n: (0, skip + jnp.clip(i - firsts[n], 0, counts[n] - 1)),
                    )
                )
    out = pl.BlockSpec((rows // 2, wide), lambda i: (0, i))
    shape = jax.ShapeDtypeStruct((rows // 2, total * wide), BF16)
    return pl.pallas_call(
        body,
        grid=(total,),
        in_specs=specs,
        out_specs=[out, out],
        out_shape=[shape, shape],
        cost_estimate=SLIGHT,
        compiler_params=pltpu.CompilerParams(vmem_limit_bytes=60 << 20),
    )(*[x for p in pairs for x, _ in p])


class Sum:
    def __init__(self, line, stream, pairs, columns=None):
        self.line, self.links = line, list(stream.links[1:])
        held = pairs[0][2]
        held = (line.hold(held[0]), held[1]) if isinstance(held, tuple) else line.hold(held)
        pairs[0] = (*pairs[0][:2], held, pairs[0][3])
        send, keep = products(pairs, columns)
        line.mark(send)
        self.parts = [keep]
        self.got = flipped(send, *self.links.pop(0))

    def take(self):
        self.got = self.line.pass_on(self.got)

    def step(self):
        self.parts.append(self.line.hold(self.got))
        half = self.parts[0].shape[0] // 2
        if self.links:
            send = sum(p[:half].astype(F32) for p in self.parts).astype(BF16)
            self.line.mark(send)
            self.got = flipped(send, *self.links.pop(0))
            self.parts = [p[half:] for p in self.parts]

    def total(self):
        self.parts.append(self.line.hold(self.got))
        return sum(p.astype(F32) for p in self.parts)


def on_device(
    incoming_symbols,
    downstream_slope,
    sequence_extents,
    mixer_lookup_map,
    mixer_payload_map,
    mixer_accepting_map,
    mixer_emitted_map,
    feedforward_lookup_map,
    feedforward_payload_map,
    feedforward_accepting_map,
    prime_normalize_gain,
    prime_normalize_bias,
    later_normalize_gain,
    later_normalize_bias,
    mixer_lookup_shiftmix,
    mixer_payload_shiftmix,
    mixer_accepting_shiftmix,
    feedforward_lookup_shiftmix,
    feedforward_accepting_shiftmix,
    channel_shrink_rate,
    newest_boost,
):
    track, slope = incoming_symbols[0], downstream_slope[0]
    tokens, model = track.shape
    seq_count, fsdp_count = lax.axis_size("seq"), lax.axis_size("fsdp")
    seq_number, fsdp_number = lax.axis_index("seq"), lax.axis_index("fsdp")
    here = {
        "z0": seq_number // 2 % 2,
        "y": seq_number % 2,
        "x": fsdp_number // 2,
        "c": fsdp_number % 2,
    }
    gain_one, bias_one, gain_two, bias_two, mix_key, mix_value, mix_recept, mix_up, mix_gate = [
        v[None, :]
        for v in (
            prime_normalize_gain,
            prime_normalize_bias,
            later_normalize_gain,
            later_normalize_bias,
            mixer_lookup_shiftmix,
            mixer_payload_shiftmix,
            mixer_accepting_shiftmix,
            feedforward_lookup_shiftmix,
            feedforward_accepting_shiftmix,
        )
    ]
    boost = newest_boost[None, :]
    line = Line()
    by_x = Stream(["c", "x", "y", "z0"])
    by_yx = Stream(["c", "y", "x", "z0"])
    by_zy = Stream(["c", "z0", "y", "x"])
    by_p = Stream(["c", "z0", "y", "x"])
    by_q = Stream(["c", "x", "y", "z0"])

    rows = mixer_lookup_map.shape[0]
    down_rows = feedforward_payload_map.shape[0]
    down_half = down_rows // 2
    pairs = [[i, i + 1] for i in range(0, fsdp_count, 2)]

    def by_chip(weight):
        return lax.all_gather(weight, "fsdp", axis=0, tiled=True, axis_index_groups=pairs)

    accepting_chip, emitted_chip, gate_chip, up_chip, down_chip = [
        by_chip(w)
        for w in (
            mixer_accepting_map,
            mixer_emitted_map,
            feedforward_accepting_map,
            feedforward_lookup_map,
            feedforward_payload_map,
        )
    ]

    def shard_rows(shard, size=rows):
        return (fsdp_number ^ shard) * size

    def chip_rows(size=rows):
        return here["x"] * 2 * size

    half, part = rows // 2, rows // 4
    near_y, far_y = here["y"] * half, (1 - here["y"]) * half
    quarters = [
        (b * 2 + a) * part
        for b in (here["y"], 1 - here["y"])
        for a in (here["z0"], 1 - here["z0"])
    ]
    near_z, far_z = here["z0"] * down_half, (1 - here["z0"]) * down_half
    every = slice(0, model)
    ff = feedforward_lookup_map.shape[1]
    blocks = [slice(n, n + model) for n in range(0, ff, model)]

    own = (mixer_lookup_map, mixer_payload_map)
    away_mix = line.mark(packed([(w, near_y, half, every) for w in own]))
    got_mix = flipped(away_mix, *LINKS["x"])
    away_more = packed(
        [
            (w, near_y, half, every)
            for w in line.hold(
                (mixer_accepting_map, mixer_emitted_map, feedforward_accepting_map)
            )
        ]
        + [(feedforward_lookup_map, quarters[0], part, b) for b in blocks]
    )
    got_more = flipped(line.mark(away_more), *LINKS["x"])
    prior_track = passed_along(line.hold(track[-1:]), "seq", 1)
    cores = [flipped(w, *LINKS["c"]) for w in line.hold(own)]

    group_positions = jnp.arange(tokens * seq_count, dtype=jnp.int32)
    group_flags = token_starts(line.hold(sequence_extents)[0], group_positions)
    chunk_flags = group_flags.reshape(seq_count, tokens)
    local_flags = lax.dynamic_index_in_dim(chunk_flags, seq_number, 0, keepdims=False)
    chunk_has = jnp.any(chunk_flags, axis=1)
    chunk_first = chunk_flags[:, 0]
    places = jnp.arange(tokens, dtype=jnp.int32)
    later = places[None, :] > places[:, None]
    marked = local_flags[None, :]
    last_start = jnp.max(jnp.where(marked & ~later, places[None, :], -FAR), axis=1)
    next_start = jnp.min(jnp.where(marked & later, places[None, :], FAR), axis=1)
    since = jnp.broadcast_to((places - last_start)[:, None], (tokens, 128))
    until = jnp.broadcast_to((next_start - 1 - places)[:, None], (tokens, 128))
    order = jnp.arange(seq_count, dtype=jnp.int32)
    between = (order[None, :] > order[:, None]) & (order[None, :] < seq_number)
    reaches = (order < seq_number) & ~jnp.any(between & chunk_has[None, :], axis=1)
    gap = jnp.where(reaches, ((seq_number - 1 - order) * tokens).astype(F32), NEVER)
    gap = jnp.broadcast_to(gap[:, None], (seq_count, 128))
    above = order[None, :] > seq_number
    blocked = chunk_first[None, :] & (order[None, :] <= order[:, None])
    blocked = blocked | (chunk_has[None, :] & (order[None, :] < order[:, None]))
    comes = (order > seq_number) & ~jnp.any(blocked & above, axis=1)
    gap_back = jnp.where(comes, ((order - 1 - seq_number) * tokens).astype(F32), NEVER)
    gap_back = jnp.broadcast_to(gap_back[:, None], (seq_count, 128))
    rate = jnp.exp(channel_shrink_rate)[None, :]
    line.mark((since, until, gap, gap_back, rate))

    away_down = line.mark(
        packed([(line.hold(feedforward_payload_map), near_z, down_half, every)])
    )

    got_mix = line.pass_on(got_mix)
    other_mix = flipped(got_mix, *LINKS["y"])
    (key_low, value_low, recept_low), mixer_away, mixer_mine = norm_and_mix(
        track,
        line.hold(prior_track),
        gain_one,
        bias_one,
        (mix_key, mix_value, mix_recept),
        since,
        [],
        [(0, by_q), (1, by_q), (2, by_p)],
    )
    line.mark(key_low)
    cores = line.pass_on(cores)
    other_mix = line.pass_on(other_mix)
    cross_mix = flipped(line.hold(got_mix), *LINKS["c"])
    cross_other_mix = flipped(other_mix, *LINKS["c"])

    def halves(parts, w, size, near, far):
        window = slice(w * size, (w + 1) * size)
        return [
            Piece(p, shard_rows(2 + n // 2, 2 * size) + (near, far)[n % 2], (), window)
            for n, p in enumerate(parts)
        ]

    plans_kv = [
        [
            Piece(own[w], shard_rows(0)),
            Piece(cores[w], shard_rows(1)),
            *halves((got_mix, other_mix, cross_mix, cross_other_mix), w, half, near_y, far_y),
        ]
        for w in range(2)
    ]
    k, v, part_a, part_b, ends = keys_and_values(
        line.hold(key_low), value_low, plans_kv, rate, since
    )
    line.mark(ends)
    all_ends = gathered_ends(ends[:2])
    mixer_other = flipped(line.hold(mixer_away), *LINKS["c"])
    got_down = flipped(away_down, *LINKS["x"])
    got_more = line.pass_on(got_more)
    got_rest = line.mark(got_more[: 3 * half])
    other_rest = flipped(got_rest, *LINKS["y"])
    got_up = line.mark(line.hold(got_more)[3 * half :])
    next_up = flipped(got_up, *LINKS["z0"])
    all_ends = line.pass_on(all_ends)
    mixer_other = line.pass_on(mixer_other)
    pair_up = line.mark(jnp.stack([got_up, line.hold(next_up)]))
    far_up = flipped(pair_up, *LINKS["y"])
    got_down = line.pass_on(got_down)
    other_down = flipped(got_down, *LINKS["z0"])
    other_rest = line.pass_on(other_rest)
    cross_rest = flipped(line.hold(got_rest), *LINKS["c"])
    cross_other_rest = flipped(other_rest, *LINKS["c"])
    plan_r, plan_e, plan_gate = [
        [
            Piece(chip, chip_rows()),
            *halves((got_rest, other_rest, cross_rest, cross_other_rest), w, half, near_y, far_y),
        ]
        for w, chip in enumerate((accepting_chip, emitted_chip, gate_chip))
    ]
    recept, attended, resid, state_a, state_b, last_row = attend(
        line.hold(recept_low),
        k,
        v,
        part_a,
        part_b,
        all_ends,
        gap,
        rate,
        boost,
        since,
        track,
        [plan_r, plan_e],
    )

    prior_resid = passed_along(line.mark(last_row), "seq", 1)
    prior_resid = line.hold(prior_resid)
    (up_low, gate_low), channel_away, channel_mine = norm_and_mix(
        resid,
        prior_resid,
        gain_two,
        bias_two,
        (mix_up, mix_gate),
        since,
        [attended],
        [(0, by_p), (2, by_p), (1, by_yx), (1, by_zy)],
    )
    line.mark(channel_away)
    far_up = line.pass_on(far_up)
    cross_up = flipped(line.hold(pair_up), *LINKS["c"])
    cross_far_up = flipped(far_up, *LINKS["c"])
    cross_down = flipped(line.hold(got_down), *LINKS["c"])
    other_down = line.pass_on(other_down)
    cross_other_down = flipped(other_down, *LINKS["c"])
    plan_up = [Piece(up_chip, chip_rows())]
    for shard, first, pair in ((2, 0, pair_up), (2, 2, far_up), (3, 0, cross_up), (3, 2, cross_far_up)):
        for n in range(2):
            for q, block in enumerate(blocks):
                plan_up.append(
                    Piece(
                        pair,
                        shard_rows(shard) + quarters[first + n],
                        (n,),
                        slice(q * part, (q + 1) * part),
                        block.start,
                    )
                )
    plan_down = [
        Piece(down_chip, chip_rows(down_rows)),
        *halves(
            (got_down, other_down, cross_down, cross_other_down), 0, down_half, near_z, far_z
        ),
    ]
    mixed, d_out, _, d_pre_up, d_up_in, d_gate_in, d_row, squared_away, squared_mine = (
        channel_mix(
            *line.hold((up_low, gate_low)),
            resid,
            slope,
            mix_up,
            mix_gate,
            since,
            [plan_up, plan_down, plan_gate],
            by_x,
        )
    )
    returned = passed_along(line.mark(d_row), "seq", -1)
    squared_other = flipped(squared_away, *LINKS["c"])
    d_out_other = flipped(d_out, *LINKS["c"])
    squared_other, d_out_other, returned = line.pass_on((squared_other, d_out_other, returned))
    channel_other = flipped(line.hold(channel_away), *LINKS["c"])
    d_pre_up_other = flipped(line.hold(d_pre_up), *LINKS["c"])
    sum_down = Sum(
        line, by_x, [((squared_mine, 0), (squared_other, 0), (d_out, 0), (d_out_other, 0))]
    )
    half_ff = ff // 2
    sum_up = [
        Sum(
            line,
            stream,
            [((channel_mine, 2 + n), (channel_other, 2 + n), d_pre_up, d_pre_up_other)],
            slice(n * half_ff, (n + 1) * half_ff),
        )
        for n, stream in enumerate((by_yx, by_zy))
    ]

    d_resid, d_att, d_recept, d_wkv, back_a, back_b, heads, vec_two = middle_back(
        line.hold(d_up_in),
        d_gate_in,
        returned,
        resid,
        prior_resid,
        slope,
        gain_two,
        bias_two,
        (mix_up, mix_gate),
        since,
        until,
        plan_e,
        recept,
        k,
        v,
        state_a,
        state_b,
        rate,
        boost,
    )
    line.mark(heads)
    all_heads = gathered_ends(heads[:2])
    d_att_other = flipped(d_att, *LINKS["c"])
    d_recept_other = flipped(d_recept, *LINKS["c"])
    sum_p = Sum(
        line,
        by_p,
        [
            ((channel_mine, 1), (channel_other, 1), (d_out, 1), (d_out_other, 1)),
            ((channel_mine, 0), (channel_other, 0), d_att, d_att_other),
            ((mixer_mine, 2), (mixer_other, 2), d_recept, d_recept_other),
        ],
    )
    sum_up[0].take()
    sum_up[1].take()
    d_kv, vec_state = recurrence_back(
        back_a,
        back_b,
        line.hold(all_heads),
        gap_back,
        k,
        v,
        state_a,
        state_b,
        d_wkv,
        until,
        rate,
        boost,
    )
    line.mark(vec_state)
    d_kv_other = flipped(d_kv, "fsdp", 0)
    d_normed, d_first_row, vec_one = entry_back(
        line.hold(d_kv),
        d_recept,
        [*plans_kv, plan_r],
        track,
        prior_track,
        gain_one,
        bias_one,
        (mix_key, mix_value, mix_recept),
        since,
    )
    returned_first = passed_along(line.mark(d_first_row), "seq", -1)
    sum_up[0].step()
    sum_down.step()
    sum_q = Sum(
        line,
        by_q,
        [
            ((mixer_mine, n), (mixer_other, n), (d_kv, n), (d_kv_other, n))
            for n in range(2)
        ],
    )
    sum_up[1].step()
    sum_up[0].step()
    sum_p.step()
    tokens_grad, vec_first = first_norm_back(
        d_normed, line.hold(returned_first), track, d_resid, gain_one
    )
    line.mark(vec_first)

    small = jnp.concatenate(
        [vec_first[:2], vec_two[:2], vec_one[:3], vec_two[2:4], vec_state[:2]], axis=0
    )
    owners = seq_count * fsdp_count
    share = model // owners
    small = small.reshape(-1, owners, share).transpose(1, 0, 2).reshape(owners, -1)
    line.mark(small)
    small = lax.all_to_all(small, BOTH, split_axis=0, concat_axis=0, tiled=True)
    sum_down.step()
    sum_up[1].step()
    sum_q.step()
    sum_up[0].step()
    sum_p.step()
    sum_down.step()
    sum_q.step()
    sum_up[1].step()
    sum_p.step()
    sum_q.step()
    sums = [sum_p, sum_down, *sum_up, sum_q]
    while any(s.links for s in sums):
        for s in sums:
            if s.links:
                s.step()
    grad_up = jnp.concatenate([s.total() for s in sum_up], axis=1)
    grad_down = sum_down.total()
    grad_gate, grad_output, grad_recept = jnp.split(sum_p.total(), 3, axis=1)
    grad_key, grad_value = jnp.split(sum_q.total(), 2, axis=1)
    small = jnp.sum(line.hold(small), axis=0).reshape(-1, share)
    large = (grad_key, grad_value, grad_recept, grad_output, grad_up, grad_down, grad_gate)
    return (mixed[None], tokens_grad[None], *large, *[small[i] for i in range(11)])


def solution(mesh):
    rows = P("fsdp", None)
    tokens = P("fsdp", "seq", None)
    return jax.shard_map(
        on_device,
        mesh=mesh,
        in_specs=(tokens, tokens, *[rows] * 8, *[P()] * 11),
        out_specs=(tokens, tokens, *[P(BOTH, None)] * 7, *[P(BOTH)] * 11),
        check_vma=False,
    )
```

time: 621 us -> 349 us (0.56)
  waiting for transfers between devices: 274 us -> 61.5 us
  Pallas kernels: 11.2 us -> 126 us
  starting transfers between devices: 136 us -> 61 us
  matrix products: 62 us -> 0 us
  other arithmetic: 67.5 us -> 35.7 us
  blocking collectives: 0 us -> 18.2 us
  local copies, waits for them, and re-layouts: 46.5 us -> 29.6 us
    all_gather x7 -> x5, waiting for transfers between devices: 179 us -> 0.02 us  [by_chip(): lax.all_gather(weight, 'fsdp', axis=0, tiled=True, axis_index_groups=pairs)]
    pallas_call x2 -> x17, Pallas kernels: 11.2 us -> 126 us  [the longest x5 27.2 us: products(): pl.pallas_call(body, grid=(total,), in_specs=specs, out_specs=[out, out],...]
    ppermute x42 -> x0, starting transfers between devices: 90.5 us -> none  [the longest x21 71.6 us: line_sum(): lax.ppermute(sent_up.astype(BF16), 'seq', [(2 * z + y, 2 * z + 2 + y) for...]
    dot_general x21 -> x0, matrix products: 62 us -> none  [the longest x1 8.34 us: on_device(): jnp.dot(squared.T, d_vals, preferred_element_type=F32)]
    ppermute x42 -> x0, waiting for transfers between devices: 42.1 us -> none  [the longest x21 22.3 us: line_sum(): lax.ppermute(sent_up.astype(BF16), 'seq', [(2 * z + y, 2 * z + 2 + y) for...]
    add x32 -> x5, other arithmetic: 41.2 us -> 6.71 us  [total(): return sum((p.astype(F32) for p in self.parts))]
    ppermute x21 -> x46, starting transfers between devices: 16.6 us -> 41.8 us  [flipped(): return lax.ppermute(value, axis, [(i, i ^ 1 << bit) for i in range(count)])]
    convert_element_type x28 -> x0, local copies, waits for them, and re-layouts: 22 us -> none  [the longest x21 21.6 us: scattered_sum(): got = flipped(away.astype(BF16), axis, bit)]
  transfers between devices with their start and end apart: 77 -> 57, of which waited for: 30 -> 14; matrix products, arithmetic and copies ran while one was open for 22% -> 15% of each run, Pallas kernels for 2% -> 29%
where the time goes in v2:
time: 349 us; the launch traced here: 346 us
  Pallas kernels  126 us (36%)
  waiting for transfers between devices  61.5 us (18%)
  starting transfers between devices  61 us (17%)
  other arithmetic  35.7 us (10%)
  local copies, waits for them, and re-layouts  29.6 us (8%)
  blocking collectives  18.2 us (5%)
  between operations  14.6 us (4%)
    ppermute x46, waiting for transfers between devices, flipped(): return lax.ppermute(value, axis, [(i, i ^ 1 << bit) for i in range(count)])  46.8 us
    ppermute x46, starting transfers between devices, flipped(): return lax.ppermute(value, axis, [(i, i ^ 1 << bit) for i in range(count)])  41.8 us
    pallas_call x5, Pallas kernels, products(): pl.pallas_call(body, grid=(total,), in_specs=specs, out_specs=[out, out],...  27.2 us
    pallas_call x1, Pallas kernels, channel_mix(): pl.pallas_call(body, grid_spec=pltpu.PrefetchScalarGridSpec(num_scalar_pr...  26.1 us
    convert_element_type x15, other arithmetic, step(): send = sum((p[:half].astype(F32) for p in self.parts)).astype(BF16)  24 us
    all_to_all x1, blocking collectives, gathered_ends(): lax.all_to_all(copies, 'seq', split_axis=0, concat_axis=0, tiled=True)  18.2 us
    pallas_call x1, Pallas kernels, middle_back(): pl.pallas_call(body, grid_spec=pltpu.PrefetchScalarGridSpec(num_scalar_pr...  14 us
    pallas_call x2, Pallas kernels, norm_and_mix(): pl.pallas_call(body, in_specs=[SMEM] + [VMEM] * (5 + count + more), out_s...  11.3 us
  transfers between devices with their start and end apart: 57, of which 14 were waited for; matrix products, arithmetic and copies ran while one was open for 15% of the time, Pallas kernels for 29%

profile of v2, /device:TPU:0, one launch (start us, length us, event | category | flops | bytes accessed | tf_op | source)
XLA Modules:
  0.0 346.4 jit_solution(15278968446407985967)
XLA Ops:
  20.9 3.9 %collective-permute-start = (bf16[1,1024]{1,0:T(2,128)(2,1)S(1)}, bf16[1,1024]{1,0:T(2,128)(2,1)S(1)}, u32[]{:S(2)}, u32[]{:S(2)}) collective-permute-start(bf16[1,1024]{1,0:T(2,128)(2,1)S(1)} %slice_bitcast_fusion), channel_id=1, source_target_pairs={{0,4},{4,8},{8,12},{12,16},{16,20},{20,24},{24,28},{1,5},{5,9},{9,... | collective-permute-start | bytes 6152 | tf_op jit(solution)/shard_map/ppermute | solution.py:37
  35.5 5.5 %shard_map.404 = (bf16[256,1024]{1,0:T(8,128)(2,1)}, bf16[256,1024]{1,0:T(8,128)(2,1)}, bf16[256,1024]{1,0:T(8,128)(2,1)}, bf16[3,512,256]{2,1,0:T(8,128)(2,1)}, bf16[3,512,256]{2,1,0:T(8,128)(2,1)}) custom-call(s32[3,32]{1,0:T(4,128)} %pad_add_fusion.1.refs_0_, bf16[256,1024]{1,0:T(8,128)(2,1)} %bitcast.61, bf16[1,1024]{1,0:T(2,128)(2,1)} %copy-done.32, ...), custom_call_target="tpu_custom_call" | custom-call | flops 1 | bytes 1 | tf_op jit(solution)/shard_map/pallas_call | solution.py:346
  41.0 5.2 %collective-permute-done.3.refs_3_.refs_7_ = bf16[256,1024]{1,0:T(8,128)(2,1)S(1)} collective-permute-done((bf16[256,1024]{1,0:T(8,128)(2,1)S(1)}, bf16[256,1024]{1,0:T(8,128)(2,1)S(1)}, u32[]{:S(2)}, u32[]{:S(2)}) %collective-permute-start.3) | collective-permute-done | bytes 524320 | tf_op jit(solution)/shard_map/ppermute | solution.py:31
  49.8 9.4 %shard_map.405 = (bf16[256,1024]{1,0:T(8,128)(2,1)}, bf16[256,1024]{1,0:T(8,128)(2,1)}, f32[256,1024]{1,0:T(8,128)}, f32[256,1024]{1,0:T(8,128)}, f32[8,1024]{1,0:T(8,128)}) custom-call(s32[12]{0:T(128)} %stack.111.offset_ref, bf16[256,1024]{1,0:T(8,128)(2,1)} %get-tuple-element.156.key_ref, bf16[256,1024]{1,0:T(8,128)(2,1)} %get-tuple-element.157.value_ref, ...), custom_call_target="tpu_custom_call" | custom-call | flops 1 | bytes 1 | tf_op jit(solution)/shard_map/pallas_call | solution.py:386
  65.9 18.2 %all_to_all.23.refs_5_ = f32[8,2,1024]{2,1,0:T(2,128)} all-to-all(f32[8,2,1024]{2,1,0:T(2,128)S(1)} %broadcast_in_dim.126), channel_id=1, replica_groups=mesh['seq'=8,'fsdp'=4] {'seq'}, dimensions={0} | all-to-all | bytes 131072 | tf_op jit(solution)/shard_map/all_to_all | solution.py:49
  91.4 8.9 %shard_map.406 = (f32[256,1024]{1,0:T(8,128)}, bf16[256,1024]{1,0:T(8,128)(2,1)}, f32[256,1024]{1,0:T(8,128)}, f32[256,1024]{1,0:T(8,128)}, f32[256,1024]{1,0:T(8,128)}, /*index=5*/f32[1,1024]{1,0:T(1,128)}) custom-call(s32[10]{0:T(128)} %stack.101.offset_ref, bf16[256,1024]{1,0:T(8,128)(2,1)} %get-tuple-element.169.refs_0_, ...), custom_call_target="tpu_custom_call" | custom-call | flops 1 | bytes 1 | tf_op jit(solution)/shard_map/pallas_call | solution.py:456
  103.3 5.5 %collective-permute-done.14.refs_2_.refs_4_ = f32[1,1024]{1,0:T(1,128)S(1)} collective-permute-done((f32[1,1024]{1,0:T(1,128)}, f32[1,1024]{1,0:T(1,128)S(1)}, u32[]{:S(2)}, u32[]{:S(2)}) %collective-permute-start.14) | collective-permute-done | bytes 4128 | tf_op jit(solution)/shard_map/ppermute | solution.py:37
  109.5 5.8 %shard_map.407 = (bf16[256,1024]{1,0:T(8,128)(2,1)}, bf16[256,1024]{1,0:T(8,128)(2,1)}, bf16[4,512,256]{2,1,0:T(8,128)(2,1)}, bf16[4,512,256]{2,1,0:T(8,128)(2,1)}) custom-call(s32[4,32]{1,0:T(4,128)} %pad_add_fusion.refs_0_, f32[256,1024]{1,0:T(8,128)} %get-tuple-element.175.refs_1_.resid_ref.refs_3_, f32[1,1024]{1,0:T(1,128)} %copy-done.33, ...), custom_call_target="tpu_custom_call" | custom-call | flops 1 | bytes 1 | tf_op jit(solution)/shard_map/pallas_call | solution.py:346
  123.7 26.1 %shard_map.408 = (bf16[256,1024]{1,0:T(8,128)(2,1)}, bf16[2,256,1024]{2,1,0:T(8,128)(2,1)}, bf16[256,4096]{1,0:T(8,128)(2,1)}, bf16[256,4096]{1,0:T(8,128)(2,1)}...) custom-call(s32[43]{0:T(128)} %stack.96.offset_ref, ...), custom_call_target="tpu_custom_call" | custom-call | flops 1 | bytes 1 | tf_op jit(solution)/shard_map/pallas_call | solution.py:574
  151.9 4.7 %collective-permute-done.23.refs_2_ = f32[1,1024]{1,0:T(1,128)S(1)} collective-permute-done((f32[1,1024]{1,0:T(1,128)}, f32[1,1024]{1,0:T(1,128)S(1)}, u32[]{:S(2)}, u32[]{:S(2)}) %collective-permute-start.23) | collective-permute-done | bytes 4128 | tf_op jit(solution)/shard_map/ppermute | solution.py:37
  158.2 5.4 %shard_map.409 = (bf16[1024,1024]{1,0:T(8,128)(2,1)}, bf16[1024,1024]{1,0:T(8,128)(2,1)}) custom-call(bf16[1,2048,256]{2,1,0:T(8,128)(2,1)} %get-tuple-element.199.refs_0_, bf16[1,2048,256]{2,1,0:T(8,128)(2,1)} %copy-done.25, bf16[2,256,1024]{2,1,0:T(8,128)(2,1)} %get-tuple-element.215.refs_2_, bf16[2,256,1024]{2,1,0:T(8,128)(2,1)} %copy-done.9), custom_call_target="tpu_custom_call" | custom-call | flops 1 | bytes 1 | tf_op jit(solution)/shard_map/pallas_call | solution.py:1020
  166.5 4.6 %shard_map.410 = (bf16[256,2048]{1,0:T(8,128)(2,1)}, bf16[256,2048]{1,0:T(8,128)(2,1)}) custom-call(bf16[4,512,256]{2,1,0:T(8,128)(2,1)} %get-tuple-element.190.refs_0_.refs_4_, bf16[4,512,256]{2,1,0:T(8,128)(2,1)} %copy-done.1, bf16[256,4096]{1,0:T(8,128)(2,1)} %get-tuple-element.205.refs_2_, bf16[256,4096]{1,0:T(8,128)(2,1)} %copy-done.5), custom_call_target="tpu_custom_call" | custom-call | flops 1 | bytes 1 | tf_op jit(solution)/shard_map/pallas_call | solution.py:1020
  174.1 4.7 %shard_map.411 = (bf16[256,2048]{1,0:T(8,128)(2,1)}, bf16[256,2048]{1,0:T(8,128)(2,1)}) custom-call(bf16[4,512,256]{2,1,0:T(8,128)(2,1)} %get-tuple-element.190.refs_0_.refs_4_, bf16[4,512,256]{2,1,0:T(8,128)(2,1)} %copy-done.1, bf16[256,4096]{1,0:T(8,128)(2,1)} %get-tuple-element.205.refs_2_, bf16[256,4096]{1,0:T(8,128)(2,1)} %copy-done.5), custom_call_target="tpu_custom_call" | custom-call | flops 1 | bytes 1 | tf_op jit(solution)/shard_map/pallas_call | solution.py:1020
  179.9 14.0 %shard_map.412 = (f32[256,1024]{1,0:T(8,128)}, bf16[256,1024]{1,0:T(8,128)(2,1)}, bf16[256,1024]{1,0:T(8,128)(2,1)}, bf16[256,1024]{1,0:T(8,128)(2,1)}, f32[256,...) custom-call(s32[5]{0:T(128)} %stack.232.offset_ref, ...), custom_call_target="tpu_custom_call" | custom-call | flops 1 | bytes 1 | tf_op jit(solution)/shard_map/pallas_call | solution.py:755
  195.9 4.0 %all-to-all-start.1 = ((f32[8,2,1024]{2,1,0:T(2,128)}), f32[8,2,1024]{2,1,0:T(2,128)S(1)}, u32[]{:S(2)}, u32[]{:S(2)}) async-start(f32[8,2,1024]{2,1,0:T(2,128)} %broadcast_in_dim.133), calls=%async_computation.1 | async-start | bytes 131072 | tf_op jit(solution)/shard_map/all_to_all | solution.py:49
  200.9 7.2 %shard_map.413 = (bf16[256,3072]{1,0:T(8,128)(2,1)}, bf16[256,3072]{1,0:T(8,128)(2,1)}) custom-call(bf16[4,512,256]{2,1,0:T(8,128)(2,1)} %get-tuple-element.190.refs_0_.refs_4_, bf16[4,512,256]{2,1,0:T(8,128)(2,1)} %copy-done.1, bf16[2,256,1024]{2,1,0:T(8,128)(2,1)} %get-tuple-element.215.refs_2_, bf16[2,256,1024]{2,1,0:T(8,128)(2,1)} %copy-done.9, ...), custom_call_target="tpu_custom_call" | custom-call | flops 1 | bytes 1 | tf_op jit(solution)/shard_map/pallas_call | solution.py:1020
  208.9 5.2 %shard_map.414 = (bf16[2,256,1024]{2,1,0:T(8,128)(2,1)}, f32[8,1024]{1,0:T(8,128)}) custom-call(f32[256,1024]{1,0:T(8,128)} %get-tuple-element.212.refs_0_, f32[256,1024]{1,0:T(8,128)} %get-tuple-element.213.refs_1_, f32[8,2,1024]{2,1,0:T(2,128)} %copy-done.29, f32[8,128]{1,0:T(8,128)} %broadcast_in_dim.119.refs_3_, ...), custom_call_target="tpu_custom_call" | custom-call | flops 1 | bytes 1 | tf_op jit(solution)/shard_map/pallas_call | solution.py:832
  216.8 10.7 %shard_map.415 = (f32[256,1024]{1,0:T(8,128)}, f32[1,1024]{1,0:T(1,128)}, f32[8,1024]{1,0:T(8,128)}) custom-call(s32[17]{0:T(128)} %stack.115.offset_ref, bf16[2,256,1024]{2,1,0:T(8,128)(2,1)} %get-tuple-element.233.d_kv_ref.refs_2_.refs_6_, bf16[256,1024]{1,0:T(8,128)(2,1)} %get-tuple-element.218.refs_10_.d_recept_ref, bf16[256,1024]{1,0:T(8,128)(2,1)} %bitcast.63, ...), custom_call_target="tpu_custom_call" | custom-call | flops 1 | bytes 1 | tf_op jit(solution)/shard_map/pallas_call | solution.py:889
  237.0 5.2 %shard_map.416 = (bf16[256,2048]{1,0:T(8,128)(2,1)}, bf16[256,2048]{1,0:T(8,128)(2,1)}) custom-call(bf16[3,512,256]{2,1,0:T(8,128)(2,1)} %get-tuple-element.217.refs_8_.refs_0_.refs_4_, bf16[3,512,256]{2,1,0:T(8,128)(2,1)} %collective-permute-done.11.refs_9_.refs_1_.refs_5_, bf16[2,256,1024]{2,1,0:T(8,128)(2,1)} %get-tuple-element.233.d_kv_ref.refs_2_.refs_6_, ...), custom_call_target="tpu_custom_call" | custom-call | flops 1 | bytes 1 | tf_op jit(solution)/shard_map/pallas_call | solution.py:1020
  250.2 8.6 %collective-permute-done.37 = bf16[512,1024]{1,0:T(8,128)(2,1)} collective-permute-done((bf16[512,1024]{1,0:T(8,128)(2,1)}, bf16[512,1024]{1,0:T(8,128)(2,1)}, u32[]{:S(2)}, u32[]{:S(2)}) %collective-permute-start.37) | collective-permute-done | bytes 1048608 | tf_op jit(solution)/shard_map/ppermute | solution.py:31
  261.6 4.8 %shard_map.417 = (bf16[256,1024]{1,0:T(8,128)(2,1)}, f32[8,1024]{1,0:T(8,128)}) custom-call(f32[256,1024]{1,0:T(8,128)} %get-tuple-element.225.d_ref, f32[1,1024]{1,0:T(1,128)} %copy-done.37, bf16[256,1024]{1,0:T(8,128)(2,1)} %bitcast.64, f32[256,1024]{1,0:T(8,128)} %get-tuple-element.239.d_resid_ref, f32[1,1024]{1,0:T(1,128)} %bitcast.79), custom_call_target="tpu_custom_call" | custom-call | flops 1 | bytes 1 | tf_op jit(solution)/shard_map/pallas_call | solution.py:926
  270.0 6.0 %all-to-all-start.2 = ((f32[32,1,352]{2,1,0:T(1,128)}), f32[32,1,352]{2,1,0:T(1,128)S(1)}, u32[]{:S(2)}, u32[]{:S(2)}) async-start(f32[32,1,352]{2,1,0:T(1,128)} %all_to_all.19), calls=%async_computation.2 | async-start | bytes 98304 | tf_op jit(solution)/shard_map/all_to_all | solution.py:1433
  289.8 10.8 %collective-permute-done.40 = bf16[128,3072]{1,0:T(8,128)(2,1)} collective-permute-done((bf16[128,3072]{1,0:T(8,128)(2,1)}, bf16[128,3072]{1,0:T(8,128)(2,1)}, u32[]{:S(2)}, u32[]{:S(2)}) %collective-permute-start.40) | collective-permute-done | bytes 786464 | tf_op jit(solution)/shard_map/ppermute | solution.py:31
  317.7 9.1 %collective-permute-done.42 = bf16[64,2048]{1,0:T(8,128)(2,1)S(1)} collective-permute-done((bf16[64,2048]{1,0:T(8,128)(2,1)S(1)}, bf16[64,2048]{1,0:T(8,128)(2,1)S(1)}, u32[]{:S(2)}, u32[]{:S(2)}) %collective-permute-start.42) | collective-permute-done | bytes 262176 | tf_op jit(solution)/shard_map/ppermute | solution.py:31
  (275 shorter events, 138.1 us)
Async XLA Ops:
  7.2 81.0 %all-gather.6.cloned.1.call-start = ((), (), s32[]{:S(2)}) async-start(), calls=%async_computation.3 | async-start | bytes 1572864 | tf_op jit(solution)/shard_map/all_gather | solution.py:1120
  7.9 80.3 %all-gather.8.cloned.1.call-start = ((), (), s32[]{:S(2)}) async-start(), calls=%async_computation.4 | async-start | bytes 1572864 | tf_op jit(solution)/shard_map/all_gather | solution.py:1120
  8.7 108.4 %all-gather.14.cloned.1.call-start = ((), (), s32[]{:S(2)}) async-start(), calls=%async_computation.7 | async-start | bytes 1572864 | tf_op jit(solution)/shard_map/all_gather | solution.py:1120
  9.4 107.6 %all-gather.10.cloned.1.call-start = ((), (), s32[]{:S(2)}) async-start(), calls=%async_computation.5 | async-start | bytes 6291456 | tf_op jit(solution)/shard_map/all_gather | solution.py:1120
  10.0 107.0 %all-gather.12.cloned.1.call-start = ((), (), s32[]{:S(2)}) async-start(), calls=%async_computation.6 | async-start | bytes 6291456 | tf_op jit(solution)/shard_map/all_gather | solution.py:1120
  20.0 39.2 %collective-permute-start.2 = (bf16[640,1024]{1,0:T(8,128)(2,1)}, bf16[640,1024]{1,0:T(8,128)(2,1)}, u32[]{:S(2)}, u32[]{:S(2)}) collective-permute-start(bf16[640,1024]{1,0:T(8,128)(2,1)} %shard_map.402), channel_id=1, source_target_pairs={{0,2},{1,3},{2,0},{3,1},{4,6},{5,7},{6,4},{7,5},{8,10},{9,11},{10,... | collective-permute-start | bytes 3932168 | tf_op jit(solution)/shard_map/ppermute | solution.py:31
  46.6 40.0 %collective-permute-start.9 = (bf16[512,1024]{1,0:T(8,128)(2,1)}, bf16[512,1024]{1,0:T(8,128)(2,1)}, u32[]{:S(2)}, u32[]{:S(2)}) collective-permute-start(bf16[512,1024]{1,0:T(8,128)(2,1)} %shard_map.403), channel_id=1, source_target_pairs={{0,2},{1,3},{2,0},{3,1},{4,6},{5,7},{6,4},{7,5},{8,10},{9,11},{10,... | collective-permute-start | bytes 3145736 | tf_op jit(solution)/shard_map/ppermute | solution.py:31
  59.2 24.9 %collective-permute-start.11 = (bf16[3,512,256]{2,1,0:T(8,128)(2,1)}, bf16[3,512,256]{2,1,0:T(8,128)(2,1)}, u32[]{:S(2)}, u32[]{:S(2)}) collective-permute-start(bf16[3,512,256]{2,1,0:T(8,128)(2,1)} %get-tuple-element.163), channel_id=1, source_target_pairs={{0,1},{1,0},{2,3},{3,2},{4,5},{5,4},{6,7},{7,6},{8,9},{9,8},{10,11... | collective-permute-start | bytes 2359304 | tf_op jit(solution)/shard_map/ppermute | solution.py:31
  85.1 30.2 %collective-permute-start.16 = (bf16[2,256,1024]{2,1,0:T(8,128)(2,1)}, bf16[2,256,1024]{2,1,0:T(8,128)(2,1)}, u32[]{:S(2)}, u32[]{:S(2)}) collective-permute-start(bf16[2,256,1024]{2,1,0:T(8,128)(2,1)} %pad_maximum_fusion.refs_4_), channel_id=1, source_target_pairs={{0,4},{4,0},{8,12},{12,8},{16,20},{20,16},{24,28},{28,24},{1,5},{5... | collective-permute-start | bytes 3145736 | tf_op jit(solution)/shard_map/ppermute | solution.py:31
  86.6 28.7 %collective-permute-start.15 = (bf16[512,1024]{1,0:T(8,128)(2,1)}, bf16[512,1024]{1,0:T(8,128)(2,1)}, u32[]{:S(2)}, u32[]{:S(2)}) collective-permute-start(bf16[512,1024]{1,0:T(8,128)(2,1)} %collective-permute-done.9.refs_9_), channel_id=1, source_target_pairs={{0,8},{4,12},{8,0},{12,4},{16,24},{20,28},{24,16},{28,20},{1,9},{5... | collective-permute-start | bytes 3145736 | tf_op jit(solution)/shard_map/ppermute | solution.py:31
  163.6 66.2 %collective-permute-start.33 = (bf16[1024,1024]{1,0:T(8,128)(2,1)}, bf16[1024,1024]{1,0:T(8,128)(2,1)}, u32[]{:S(2)}, u32[]{:S(2)}) collective-permute-start(bf16[1024,1024]{1,0:T(8,128)(2,1)} %get-tuple-element.201), channel_id=1, source_target_pairs={{0,2},{1,3},{2,0},{3,1},{4,6},{5,7},{6,4},{7,5},{8,10},{9,11},{10,... | collective-permute-start | bytes 6291464 | tf_op jit(solution)/shard_map/ppermute | solution.py:31
  171.1 37.0 %collective-permute-start.27 = (bf16[256,2048]{1,0:T(8,128)(2,1)}, bf16[256,2048]{1,0:T(8,128)(2,1)S(1)}, u32[]{:S(2)}, u32[]{:S(2)}) collective-permute-start(bf16[256,2048]{1,0:T(8,128)(2,1)} %get-tuple-element.204), channel_id=1, source_target_pairs={{0,4},{4,0},{8,12},{12,8},{16,20},{20,16},{24,28},{28,24},{1,5},{5... | collective-permute-start | bytes 3145736 | tf_op jit(solution)/shard_map/ppermute | solution.py:31
  178.8 29.4 %collective-permute-start.26 = (bf16[256,2048]{1,0:T(8,128)(2,1)}, bf16[256,2048]{1,0:T(8,128)(2,1)S(1)}, u32[]{:S(2)}, u32[]{:S(2)}) collective-permute-start(bf16[256,2048]{1,0:T(8,128)(2,1)} %get-tuple-element.206), channel_id=1, source_target_pairs={{0,8},{4,12},{8,0},{12,4},{16,24},{20,28},{24,16},{28,20},{1,9},{5... | collective-permute-start | bytes 3145736 | tf_op jit(solution)/shard_map/ppermute | solution.py:31
  214.8 44.0 %collective-permute-start.31 = (bf16[256,3072]{1,0:T(8,128)(2,1)}, bf16[256,3072]{1,0:T(8,128)(2,1)}, u32[]{:S(2)}, u32[]{:S(2)}) collective-permute-start(bf16[256,3072]{1,0:T(8,128)(2,1)} %get-tuple-element.219), channel_id=1, source_target_pairs={{0,8},{4,12},{8,0},{12,4},{16,24},{20,28},{24,16},{28,20},{1,9},{5... | collective-permute-start | bytes 4718600 | tf_op jit(solution)/shard_map/ppermute | solution.py:31
  232.5 26.4 %collective-permute-start.37 = (bf16[512,1024]{1,0:T(8,128)(2,1)}, bf16[512,1024]{1,0:T(8,128)(2,1)}, u32[]{:S(2)}, u32[]{:S(2)}) collective-permute-start(bf16[512,1024]{1,0:T(8,128)(2,1)} %add_convert_fusion), channel_id=1, source_target_pairs={{0,4},{4,0},{8,12},{12,8},{16,20},{20,16},{24,28},{28,24},{1,5},{5... | collective-permute-start | bytes 3145736 | tf_op jit(solution)/shard_map/ppermute | solution.py:31
  233.9 27.1 %collective-permute-start.30 = (f32[1,1024]{1,0:T(1,128)S(1)}, f32[1,1024]{1,0:T(1,128)S(1)}, u32[]{:S(2)}, u32[]{:S(2)}) collective-permute-start(f32[1,1024]{1,0:T(1,128)S(1)} %copy-done.40), channel_id=1, source_target_pairs={{4,0},{8,4},{12,8},{16,12},{20,16},{24,20},{28,24},{5,1},{9,5},{13... | collective-permute-start | bytes 12296 | tf_op jit(solution)/shard_map/ppermute | solution.py:37
  242.2 42.8 %collective-permute-start.35 = (bf16[256,2048]{1,0:T(8,128)(2,1)}, bf16[256,2048]{1,0:T(8,128)(2,1)}, u32[]{:S(2)}, u32[]{:S(2)}) collective-permute-start(bf16[256,2048]{1,0:T(8,128)(2,1)} %get-tuple-element.234), channel_id=1, source_target_pairs={{0,2},{1,3},{2,0},{3,1},{4,6},{5,7},{6,4},{7,5},{8,10},{9,11},{10,... | collective-permute-start | bytes 3145736 | tf_op jit(solution)/shard_map/ppermute | solution.py:31
  245.6 37.6 %collective-permute-start.36 = (bf16[128,2048]{1,0:T(8,128)(2,1)}, bf16[128,2048]{1,0:T(8,128)(2,1)}, u32[]{:S(2)}, u32[]{:S(2)}) collective-permute-start(bf16[128,2048]{1,0:T(8,128)(2,1)} %add_convert_fusion.4), channel_id=1, source_target_pairs={{0,4},{4,0},{8,12},{12,8},{16,20},{20,16},{24,28},{28,24},{1,5},{5... | collective-permute-start | bytes 1572872 | tf_op jit(solution)/shard_map/ppermute | solution.py:31
  258.8 28.4 %collective-permute-start.41 = (bf16[64,2048]{1,0:T(8,128)(2,1)}, bf16[64,2048]{1,0:T(8,128)(2,1)}, u32[]{:S(2)}, u32[]{:S(2)}) collective-permute-start(bf16[64,2048]{1,0:T(8,128)(2,1)} %add_convert_fusion.10), channel_id=1, source_target_pairs={{0,8},{4,12},{8,0},{12,4},{16,24},{20,28},{24,16},{28,20},{1,9},{5... | collective-permute-start | bytes 786440 | tf_op jit(solution)/shard_map/ppermute | solution.py:31
  278.3 25.1 %collective-permute-start.39 = (bf16[256,1024]{1,0:T(8,128)(2,1)}, bf16[256,1024]{1,0:T(8,128)(2,1)}, u32[]{:S(2)}, u32[]{:S(2)}) collective-permute-start(bf16[256,1024]{1,0:T(8,128)(2,1)} %add_convert_fusion.3), channel_id=1, source_target_pairs={{0,8},{4,12},{8,0},{12,4},{16,24},{20,28},{24,16},{28,20},{1,9},{5... | collective-permute-start | bytes 1572872 | tf_op jit(solution)/shard_map/ppermute | solution.py:31
  284.5 28.0 %collective-permute-start.44 = (bf16[64,2048]{1,0:T(8,128)(2,1)S(1)}, bf16[64,2048]{1,0:T(8,128)(2,1)S(1)}, u32[]{:S(2)}, u32[]{:S(2)}) collective-permute-start(bf16[64,2048]{1,0:T(8,128)(2,1)S(1)} %add_convert_fusion.9), channel_id=1, source_target_pairs={{0,2},{1,3},{2,0},{3,1},{4,6},{5,7},{6,4},{7,5},{8,10},{9,11},{10,... | collective-permute-start | bytes 786440 | tf_op jit(solution)/shard_map/ppermute | solution.py:31
  286.3 24.4 %collective-permute-start.38 = (bf16[128,2048]{1,0:T(8,128)(2,1)S(1)}, bf16[128,2048]{1,0:T(8,128)(2,1)S(1)}, u32[]{:S(2)}, u32[]{:S(2)}) collective-permute-start(bf16[128,2048]{1,0:T(8,128)(2,1)S(1)} %add_convert_fusion.2), channel_id=1, source_target_pairs={{0,4},{4,0},{8,12},{12,8},{16,20},{20,16},{24,28},{28,24},{1,5},{5... | collective-permute-start | bytes 1572872 | tf_op jit(solution)/shard_map/ppermute | solution.py:31
  288.4 41.3 %collective-permute-start.47 = (bf16[32,2048]{1,0:T(8,128)(2,1)S(1)}, bf16[32,2048]{1,0:T(8,128)(2,1)S(1)}, u32[]{:S(2)}, u32[]{:S(2)}) collective-permute-start(bf16[32,2048]{1,0:T(8,128)(2,1)S(1)} %add_convert_fusion.14), channel_id=1, source_target_pairs={{0,16},{4,20},{8,24},{12,28},{16,0},{20,4},{24,8},{28,12},{1,17},{... | collective-permute-start | bytes 393224 | tf_op jit(solution)/shard_map/ppermute | solution.py:31
  304.7 29.6 %collective-permute-start.49 = (bf16[128,1024]{1,0:T(8,128)(2,1)S(1)}, bf16[128,1024]{1,0:T(8,128)(2,1)S(1)}, u32[]{:S(2)}, u32[]{:S(2)}) collective-permute-start(bf16[128,1024]{1,0:T(8,128)(2,1)S(1)} %add_convert_fusion.8), channel_id=1, source_target_pairs={{0,16},{4,20},{8,24},{12,28},{16,0},{20,4},{24,8},{28,12},{1,17},{... | collective-permute-start | bytes 786440 | tf_op jit(solution)/shard_map/ppermute | solution.py:31
  (77 other events, 673.0 us)
Sparse Core Ops, SparseCore 0:
  9.6 11.7 all-gather.5
  22.9 10.2 all-gather.7
  34.7 10.2 all-gather.13
  46.3 15.5 all-gather.9
  63.3 15.2 all-gather.11

commit v3 on v2

v3 whole, which is shorter than its diff:
```python
from functools import partial

import jax
import jax.numpy as jnp
from jax import lax
from jax.experimental import pallas as pl
from jax.experimental.pallas import tpu as pltpu
from jax.sharding import PartitionSpec as P

norm_eps = 1e-05
F32 = jnp.float32
BF16 = jnp.bfloat16
FAR = 1 << 20
SLIGHT = pl.CostEstimate(flops=1, bytes_accessed=1, transcendentals=0)
NEVER = 1e30
BOTH = ("seq", "fsdp")
LINKS = {"c": ("fsdp", 0), "x": ("fsdp", 1), "y": ("seq", 0), "z0": ("seq", 1)}
VMEM = pl.BlockSpec(memory_space=pltpu.VMEM)
SMEM = pl.BlockSpec(memory_space=pltpu.SMEM)
HBM = pl.BlockSpec(memory_space=pl.ANY)
WIDE = 512
STEP = 64


def after(value, *others):
    return lax.optimization_barrier((value, others))[0]


def flipped(value, axis, bit):
    count = lax.axis_size(axis)
    return lax.ppermute(value, axis, [(i, i ^ (1 << bit)) for i in range(count)])


def passed_along(value, axis, steps):
    count = lax.axis_size(axis)
    initial, last = (max(0, -steps), min(count, count - steps))
    return lax.ppermute(value, axis, [(source, source + steps) for source in range(initial, last)])


def token_starts(sequence_extents, positions):
    begins = jnp.cumsum(sequence_extents, axis=-1) - sequence_extents
    start_marks = (begins[..., :, None] == positions) & (sequence_extents[..., :, None] > 0)
    return jnp.any(start_marks, axis=-2)


def gathered_ends(copies):
    return lax.all_to_all(copies, "seq", split_axis=0, concat_axis=0, tiled=True)


def across(left, right):
    return lax.dot_general(left, right, (((1,), (1,)), ((), ())), preferred_element_type=F32)


def spread(mark, cols):
    return jnp.tile(mark, (1, cols // 128))


def normal(z):
    centred = z - jnp.mean(z, axis=-1, keepdims=True)
    return centred, lax.rsqrt(jnp.mean(centred * centred, axis=-1, keepdims=True) + norm_eps)


def normal_back(z, d, gain):
    centred, scale = normal(z)
    n = centred * scale
    e = d * gain
    inner = e - jnp.mean(e, axis=-1, keepdims=True) - n * jnp.mean(e * n, axis=-1, keepdims=True)
    return n, scale * inner


def one_later(block, previous):
    place = lax.broadcasted_iota(jnp.int32, block.shape, 0)
    return jnp.where(place == 0, previous, pltpu.roll(block, 1, 0))


def one_earlier(block, following):
    rows = block.shape[0]
    place = lax.broadcasted_iota(jnp.int32, block.shape, 0)
    return jnp.where(place == rows - 1, following, pltpu.roll(block, rows - 1, 0))


def folded(block):
    return sum(block[n : n + 8] for n in range(0, block.shape[0], 8))


def turn_blocks(stream, n, source, whole, away, mine):
    order = stream.order()
    owners = len(order)
    block = source.shape[1] // owners
    whole[...] = source[...].T
    for r in range(owners):
        base = pl.multiple_of(order[r] * block, block)
        out, at = (away, r) if r < owners // 2 else (mine, r - owners // 2)
        out[n, at * block : (at + 1) * block, :] = whole[pl.ds(base, block), :]


def turns_in_kernel(rows, streams):
    return (rows // len(streams[0].masks)) % 16 == 0


def turned_outside(acts, streams):
    rows = acts[0].shape[1]
    out = []
    for act, stream in zip(acts, streams):
        block = rows // len(stream.masks)
        blocks = jnp.stack(stream.order())
        index = blocks[:, None] * block + jnp.arange(block)[None, :]
        out.append(jnp.take(act.T, index.reshape(-1), axis=0))
    out = jnp.stack(out)
    return out[:, : rows // 2], out[:, rows // 2 :]


class Piece:
    def __init__(self, part, offset, lead=(), rows=None, column=None):
        self.part, self.offset, self.lead = part, offset, lead
        self.rows, self.column = rows, column


def listed(plans):
    parts, copies = [], []
    for plan in plans:
        copies.append([])
        for piece in plan:
            known = [n for n, p in enumerate(parts) if p is piece.part]
            if not known:
                parts.append(piece.part)
                known = [len(parts) - 1]
            copies[-1].append((known[0], piece))
    return parts, copies


def copied(copies, ins, whole, sems, columns=None):
    started = []
    for n, (part, piece) in enumerate(copies):
        source = ins[part].at[piece.lead] if piece.lead else ins[part]
        if piece.rows is not None:
            source = source.at[piece.rows, :]
        base = pl.multiple_of(piece.offset(), 16)
        target = pl.ds(base, source.shape[0])
        if piece.column is not None:
            taken = slice(piece.column, piece.column + source.shape[1])
            if columns is not None and taken.start != columns.start:
                continue
        elif columns is not None:
            taken = columns
            source = source.at[:, columns]
        else:
            taken = slice(0, source.shape[1])
        copy = pltpu.make_async_copy(source, whole.at[target, taken], sems.at[n])
        copy.start()
        started.append(copy)
    return started


def packed(entries):
    parts, places = [], []
    for array, _, _, _ in entries:
        known = [n for n, p in enumerate(parts) if p is array]
        if not known:
            parts.append(array)
            known = [len(parts) - 1]
        places.append(known[0])
    wide = entries[0][3].stop - entries[0][3].start
    total_rows = sum(e[2] for e in entries)

    def body(*refs):
        ins, out, sems = refs[: len(parts)], refs[-2], refs[-1]
        started, at = [], 0
        for n, (_, offset, rows, columns) in enumerate(entries):
            copy = pltpu.make_async_copy(
                ins[places[n]].at[pl.ds(pl.multiple_of(offset(), 16), rows), columns],
                out.at[at : at + rows, :],
                sems.at[n],
            )
            copy.start()
            started.append(copy)
            at += rows
        wait_all(started)

    return pl.pallas_call(
        body,
        in_specs=[HBM] * len(parts),
        out_specs=VMEM,
        scratch_shapes=[pltpu.SemaphoreType.DMA((len(entries),))],
        out_shape=jax.ShapeDtypeStruct((total_rows, wide), BF16),
        cost_estimate=SLIGHT,
        compiler_params=pltpu.CompilerParams(vmem_limit_bytes=60 << 20),
    )(*parts)


def wait_all(copies):
    for copy in copies:
        copy.wait()


def by_columns(count, body, wide=WIDE):
    def step(j, carry):
        body(pl.ds(pl.multiple_of(j * wide, wide), wide))
        return carry

    lax.fori_loop(0, count // wide, step, 0)


class Late:
    def __init__(self, source, ref, sem):
        self.copy, self.ref, self.waited = pltpu.make_async_copy(source, ref, sem), ref, False

    def get(self):
        if not self.waited:
            self.copy.wait()
            self.waited = True
        return self.ref


class Early:
    def __init__(self, ref, out, sem):
        self.copy, self.ref, self.sent = pltpu.make_async_copy(ref, out, sem), ref, False

    def send(self):
        self.copy.start()
        self.sent = True


def streamed(body, scalars, ins, outs, scratch=()):
    lates = [a for a, how in ins if how == "late"]
    earlies = [o for o in outs if o[2] == "early"]

    def wrapped(*refs):
        refs = list(refs)

        def pop(count):
            taken, refs[:] = refs[:count], refs[count:]
            return taken

        scalar_refs, in_refs, out_refs = pop(len(scalars)), pop(len(ins)), pop(len(outs))
        late_refs, early_refs = pop(len(lates)), pop(len(earlies))
        late_sems, early_sems = pop(1)[0], pop(1)[0]
        given, made, n = [], [], 0
        for (_, how), ref in zip(ins, in_refs):
            if how == "late":
                given.append(Late(ref, late_refs[n], late_sems.at[n]))
                n += 1
            else:
                given.append(ref)
        n = 0
        for (_, _, how), ref in zip(outs, out_refs):
            if how == "early":
                made.append(Early(early_refs[n], ref, early_sems.at[n]))
                n += 1
            else:
                made.append(ref)
        body(scalar_refs, given, made, *refs)
        for out in made:
            if isinstance(out, Early):
                if not out.sent:
                    out.send()
        for out in made:
            if isinstance(out, Early):
                out.copy.wait()

    return pl.pallas_call(
        wrapped,
        grid_spec=pltpu.PrefetchScalarGridSpec(
            num_scalar_prefetch=len(scalars),
            grid=(),
            in_specs=[VMEM if how == "now" else HBM for _, how in ins],
            out_specs=[VMEM if how == "now" else HBM for _, _, how in outs],
            scratch_shapes=[pltpu.VMEM(a.shape, a.dtype) for a in lates]
            + [pltpu.VMEM(shape, dtype) for shape, dtype, _ in earlies]
            + [
                pltpu.SemaphoreType.DMA((max(1, len(lates)),)),
                pltpu.SemaphoreType.DMA((max(1, len(earlies)),)),
            ]
            + list(scratch),
        ),
        out_shape=[jax.ShapeDtypeStruct(shape, dtype) for shape, dtype, _ in outs],
        cost_estimate=SLIGHT,
        compiler_params=pltpu.CompilerParams(vmem_limit_bytes=60 << 20),
    )(*scalars, *[a for a, _ in ins])


def start_copies(copies):
    for copy in copies:
        copy.start()


def start_all(*lates):
    for late in lates:
        late.copy.start()


def shapes_of(*pairs):
    return [jax.ShapeDtypeStruct(shape, dtype) for shape, dtype in pairs]


def scan_forward(rate_ref, k_ref, v_ref, since_ref, a_ref, b_ref, end_ref, cols):
    rows, wide = k_ref.shape[0], cols.stop - cols.start
    place = lax.broadcasted_iota(jnp.int32, (8, wide), 0)
    rate = rate_ref[:, cols]
    fades = [jnp.exp(-rate * float(d)) for d in (1, 2, 4)]
    carry_fade = jnp.exp(-rate * (place + 1).astype(F32))

    def step(i, state):
        base = pl.multiple_of(i * 16, 16)
        k = k_ref[pl.ds(base, 16), cols].astype(F32)
        v = v_ref[pl.ds(base, 16), cols].astype(F32)
        for h in range(2):
            at = pl.multiple_of(base + 8 * h, 8)
            part = slice(8 * h, 8 * h + 8)
            since = spread(since_ref[pl.ds(at, 8), :], wide)
            near = jnp.minimum(since, place)
            lift = jnp.exp(k[part])
            new = []
            for run, last, ref in zip((lift * v[part], lift), state, (a_ref, b_ref)):
                for d, fade in zip((1, 2, 4), fades):
                    run = run + jnp.where(near >= d, fade * pltpu.roll(run, d, 0), 0.0)
                run = run + jnp.where(since > place, carry_fade * last, 0.0)
                before = one_later(run, last)
                ref[pl.ds(at, 8), cols] = jnp.where(since >= 1, before, 0.0)
                new.append(run[7:8, :])
            state = tuple(new)
        return state

    zero = jnp.zeros((1, wide), F32)
    sa, sb = lax.fori_loop(0, rows // 16, step, (zero, zero))
    for n in range(end_ref.shape[0]):
        end_ref[n, 0:1, cols] = sa
        end_ref[n, 1:2, cols] = sb


def scan_backward(
    rate_ref,
    boost_ref,
    k_ref,
    v_ref,
    d_ref,
    a_in_ref,
    b_in_ref,
    until_ref,
    a_ref,
    b_ref,
    end_ref,
    cols,
):
    rows, wide = k_ref.shape[0], cols.stop - cols.start
    place = lax.broadcasted_iota(jnp.int32, (8, wide), 0)
    rate = rate_ref[:, cols]
    fades = [jnp.exp(-rate * float(d)) for d in (1, 2, 4)]
    carry_fade = jnp.exp(-rate * (8 - place).astype(F32))

    def step(j, state):
        base = pl.multiple_of((rows // 16 - 1 - j) * 16, 16)
        k = k_ref[pl.ds(base, 16), cols].astype(F32)
        v = v_ref[pl.ds(base, 16), cols].astype(F32)
        d = d_ref[pl.ds(base, 16), cols].astype(F32)
        for h in (1, 0):
            at = pl.multiple_of(base + 8 * h, 8)
            part = slice(8 * h, 8 * h + 8)
            until = spread(until_ref[pl.ds(at, 8), :], wide)
            near = jnp.minimum(until, 7 - place)
            bonus = jnp.exp(boost_ref[:, cols] + k[part])
            inverse = 1.0 / (b_in_ref[pl.ds(at, 8), cols] + bonus)
            wkv = (a_in_ref[pl.ds(at, 8), cols] + bonus * v[part]) * inverse
            first = d[part] * inverse
            new = []
            for run, last, ref in zip((first, -first * wkv), state, (a_ref, b_ref)):
                for q, fade in zip((1, 2, 4), fades):
                    run = run + jnp.where(near >= q, fade * pltpu.roll(run, 8 - q, 0), 0.0)
                run = run + jnp.where(until >= 8 - place, carry_fade * last, 0.0)
                ref[pl.ds(at, 8), cols] = jnp.where(until >= 1, one_earlier(run, last), 0.0)
                new.append(run[0:1, :])
            state = tuple(new)
        return state

    zero = jnp.zeros((1, wide), F32)
    sa, sb = lax.fori_loop(0, rows // 16, step, (zero, zero))
    for n in range(end_ref.shape[0]):
        end_ref[n, 0:1, cols] = sa
        end_ref[n, 1:2, cols] = sb


def carried(gap_ref, ends_ref, rate):
    cols = rate.shape[1]
    a = b = jnp.zeros((1, cols), F32)
    for j in range(gap_ref.shape[0]):
        weigh = jnp.exp(-rate * spread(gap_ref[j : j + 1, :], cols))
        a = a + weigh * ends_ref[j, 0:1, :]
        b = b + weigh * ends_ref[j, 1:2, :]
    return a, b


def norm_and_mix(track, prior, gain, bias, weights, since, others, turns):
    tokens, cols = track.shape
    count, more = len(weights), len(others)
    streams = [stream for _, stream in turns]
    inside = bool(turns) and turns_in_kernel(cols, streams)

    def body(*refs):
        track_ref, prior_ref, gain_ref, bias_ref, since_ref = refs[:5]
        mix_refs, other_refs = refs[5 : 5 + count], refs[5 + count : 5 + count + more]
        outs = refs[5 + count + more :]
        mixed, rest = outs[:count], outs[count:]
        gain, bias = gain_ref[...], bias_ref[...]

        def norm(z):
            centred, scale = normal(z)
            return centred * scale * gain + bias

        def step(i, last):
            at = pl.ds(pl.multiple_of(i * STEP, STEP), STEP)
            now = norm(track_ref[at, :].astype(F32))
            then = one_later(now, last)
            then = jnp.where(spread(since_ref[at, :], cols) == 0, 0.0, then)
            for out, mix_ref in zip(mixed, mix_refs):
                weight = mix_ref[...]
                out[at, :] = (now * weight + then * (1.0 - weight)).astype(BF16)
            return now[STEP - 1 :, :]

        lax.fori_loop(0, tokens // STEP, step, norm(prior_ref[...].astype(F32)))
        if inside:
            away, mine, whole = rest
            sources = [*other_refs, *mixed]
            for n, (which, _) in enumerate(turns):
                turn_blocks(streams[n], n, sources[which], whole, away, mine)

    low = ((tokens, cols), BF16)
    half = ((len(streams), cols // 2, tokens), BF16)
    out = pl.pallas_call(
        body,
        in_specs=[VMEM] * (5 + count + more),
        out_specs=[VMEM] * (count + 2 * inside),
        out_shape=shapes_of(*[low] * count, *[half, half] * inside),
        scratch_shapes=[pltpu.VMEM((cols, tokens), BF16)] * inside,
        cost_estimate=SLIGHT,
        compiler_params=pltpu.CompilerParams(vmem_limit_bytes=60 << 20),
    )(track, prior, gain, bias, since, *weights, *others)
    if inside:
        return out[:count], out[count], out[count + 1]
    if not turns:
        return out
    sources = [*others, *out]
    return out, *turned_outside([sources[which] for which, _ in turns], streams)


def keys_and_values(key_low, value_low, plans, rate, since):
    tokens, cols = key_low.shape
    parts, copies = listed(plans)
    most = max(len(c) for c in copies)

    def body(scalars, ins, outs, w_k, w_v, sems):
        key_ref, value, rate_ref, since_ref = ins[:4]
        k, v, a, b, end_ref = outs
        started = [
            copied(copies[n], ins[4:], w, sems.at[n])
            for n, w in enumerate((w_k, w_v))
        ]
        start_all(value)
        for n, (low, w, out) in enumerate(((key_ref, w_k, k), (value, w_v, v))):
            wait_all(started[n])
            low = low.get() if n else low

            def one(at, low=low, w=w, out=out):
                value = jnp.dot(low[...], w[:, at], preferred_element_type=F32)
                out.ref[:, at] = value.astype(BF16)

            by_columns(cols, one)
            out.send()
        scan_forward(
            rate_ref, k.ref, v.ref, since_ref, a.ref, b.ref, end_ref, slice(0, cols)
        )

    low, full = ((tokens, cols), BF16, "early"), ((tokens, cols), F32, "early")
    return streamed(
        body,
        [],
        [(key_low, "now"), (value_low, "late"), (rate, "now"), (since, "now")]
        + [(p, "raw") for p in parts],
        [low, low, full, full, ((lax.axis_size("seq"), 2, cols), F32, "now")],
        [
            pltpu.VMEM((cols, cols), BF16),
            pltpu.VMEM((cols, cols), BF16),
            pltpu.SemaphoreType.DMA((2, most)),
        ],
    )


def attend(recept_low, k, v, part_a, part_b, ends, gap, rate, boost, since, track, plans):
    tokens, cols = recept_low.shape
    parts, copies = listed(plans)
    most = max(len(c) for c in copies)

    def body(scalars, ins, outs, w_r, w_e, sems):
        low_ref, k, v, part_a, part_b, ends_ref, gap_ref = ins[:7]
        rate_ref, boost_ref, since_ref, track = ins[7:11]
        recept, att, resid, a_out, b_out, last_ref = outs
        started = [copied(copies[0], ins[11:], w_r, sems.at[0])]
        start_all(k, v, part_a, part_b)
        started.append(copied(copies[1], ins[11:], w_e, sems.at[1]))
        start_all(track)
        rate, boost = rate_ref[...], boost_ref[...]
        enter_a, enter_b = carried(gap_ref, ends_ref, rate)
        wait_all(started[0])

        def gate(at):
            pre = jnp.dot(low_ref[...], w_r[:, at], preferred_element_type=F32)
            recept.ref[:, at] = jax.nn.sigmoid(pre)

        by_columns(cols, gate)
        recept.send()
        k_ref, v_ref, pa_ref, pb_ref = k.get(), v.get(), part_a.get(), part_b.get()

        def step(i, carry):
            at = pl.ds(pl.multiple_of(i * STEP, STEP), STEP)
            place = i * STEP + lax.broadcasted_iota(jnp.int32, (STEP, cols), 0)
            inside = spread(since_ref[at, :], cols) > place
            fade = jnp.where(inside, jnp.exp(-rate * place.astype(F32)), 0.0)
            a = pa_ref[at, :] + fade * enter_a
            b = pb_ref[at, :] + fade * enter_b
            a_out.ref[at, :] = a
            b_out.ref[at, :] = b
            bonus = jnp.exp(boost + k_ref[at, :].astype(F32))
            wkv = (a + bonus * v_ref[at, :].astype(F32)) / (b + bonus)
            low = wkv.astype(BF16).astype(F32)
            att.ref[at, :] = (recept.ref[at, :] * low).astype(BF16)
            return carry

        lax.fori_loop(0, tokens // STEP, step, 0)
        a_out.send()
        b_out.send()
        att.send()
        wait_all(started[1])
        track_ref = track.get()

        def emit(at):
            out = jnp.dot(att.ref[...], w_e[:, at], preferred_element_type=F32)
            resid.ref[:, at] = track_ref[:, at].astype(F32) + out

        by_columns(cols, emit)
        resid.send()
        last_ref[...] = resid.ref[tokens - 1 :, :]

    low, full = ((tokens, cols), BF16, "early"), ((tokens, cols), F32, "early")
    return streamed(
        body,
        [],
        [
            (recept_low, "now"),
            (k, "late"),
            (v, "late"),
            (part_a, "late"),
            (part_b, "late"),
            (ends, "now"),
            (gap, "now"),
            (rate, "now"),
            (boost, "now"),
            (since, "now"),
            (track, "late"),
        ]
        + [(p, "raw") for p in parts],
        [full, low, full, full, full, ((1, cols), F32, "now")],
        [
            pltpu.VMEM((cols, cols), BF16),
            pltpu.VMEM((cols, cols), BF16),
            pltpu.SemaphoreType.DMA((2, most)),
        ],
    )


def channel_mix(up_low, gate_low, resid, slope, up_weight, gate_weight, since, plans, stream):
    tokens, model = up_low.shape
    ff = plans[0][0].part.shape[-1]
    parts, copies = listed(plans)
    most = max(len(c) for c in copies)
    spans = 4
    span = ff // spans
    owners = len(stream.masks)
    block = ff // owners
    inside = block % 128 == 0

    def body(scalars, ins, outs, w_up, w_down, w_gate, positive, d_up, gating, *rest):
        order = stream.order()
        up_ref, gate_ref, resid, slope, up_mix, gate_mix, since_ref = ins[:7]
        mixed, d_out, d_pre, d_up_out, d_gate, row_ref = outs[:6]
        squared, sems = rest if inside else (outs[6].ref, rest[0])
        gate_copies = copied(copies[2], ins[7:], w_gate, sems.at[spans + 1])
        up_copies = [
            copied(
                copies[0], ins[7:], w_up, sems.at[n], slice(n * span, (n + 1) * span)
            )
            for n in range(spans)
        ]
        down_copies = copied(copies[1], ins[7:], w_down, sems.at[spans])
        start_all(resid, slope)
        wait_all(gate_copies)

        def gate_step(cols):
            gate = jnp.dot(gate_ref[...], w_gate[:, cols], preferred_element_type=F32)
            gating[:, cols] = jax.nn.sigmoid(gate)

        by_columns(model, gate_step)

        def up_step(j, carry):
            cols = pl.ds(pl.multiple_of(j * WIDE, WIDE), WIDE)
            pre = jnp.dot(up_ref[...], w_up[:, cols], preferred_element_type=F32)
            pre = jnp.maximum(pre, 0.0)
            positive[:, cols] = pre
            squared[:, cols] = (pre * pre).astype(BF16)
            return carry

        for n in range(spans):
            wait_all(up_copies[n])
            lax.fori_loop(n * span // WIDE, (n + 1) * span // WIDE, up_step, 0)
        if inside:
            away, mine = outs[6:8]

            for r in range(owners):
                out, base = (away, r) if r < owners // 2 else (mine, r - owners // 2)
                at = pl.multiple_of(order[r] * block, block)
                out.ref[0, base * block : (base + 1) * block, :] = squared[:, pl.ds(at, block)].T
            away.send()
            mine.send()
        wait_all(down_copies)
        resid_ref, slope_ref = resid.get(), slope.get()

        def down_step(cols):
            values = jnp.dot(squared[...], w_down[:, cols], preferred_element_type=F32)
            gate = gating[:, cols]
            upstream = slope_ref[:, cols].astype(F32)
            mixed.ref[:, cols] = (resid_ref[:, cols] + gate * values).astype(BF16)
            d_out.ref[0, :, cols] = (upstream * gate).astype(BF16)
            d_out.ref[1, :, cols] = (upstream * values * gate * (1.0 - gate)).astype(BF16)

        by_columns(model, down_step)
        d_out.send()
        mixed.send()

        def gate_back_step(cols):
            gating[:, cols] = across(d_out.ref[1], w_gate[cols, :])

        by_columns(model, gate_back_step)
        d_gate.ref[...] = gating[...].astype(BF16)
        d_gate.send()

        def back_step(cols):
            d_squared = across(d_out.ref[0], w_down[cols, :])
            value = (d_squared * 2.0 * positive[:, cols]).astype(BF16)
            d_pre.ref[:, cols] = value
            d_up[...] += across(value, w_up[:, cols])

        d_up[...] = jnp.zeros_like(d_up)
        by_columns(ff, back_step, 1024)
        d_pre.send()
        d_up_out.ref[...] = d_up[...].astype(BF16)
        d_up_out.send()
        row = (1.0 - up_mix[...]) * d_up[0:1, :] + (1.0 - gate_mix[...]) * gating[0:1, :]
        row_ref[...] = jnp.where(spread(since_ref[0:1, :], model) == 0, 0.0, row)

    low = ((tokens, model), BF16, "early")
    half = ((1, ff // 2, tokens), BF16, "early")
    wide = ((tokens, ff), BF16, "early")
    out = streamed(
        body,
        [],
        [
            (up_low, "now"),
            (gate_low, "now"),
            (resid, "late"),
            (slope, "late"),
            (up_weight, "now"),
            (gate_weight, "now"),
            (since, "now"),
        ]
        + [(p, "raw") for p in parts],
        [
            low,
            ((2, tokens, model), BF16, "early"),
            wide,
            low,
            low,
            ((1, model), F32, "now"),
            *([half, half] if inside else [wide]),
        ],
        [
            pltpu.VMEM((model, ff), BF16),
            pltpu.VMEM((ff, model), BF16),
            pltpu.VMEM((model, model), BF16),
            pltpu.VMEM((tokens, ff), F32),
            pltpu.VMEM((tokens, model), F32),
            pltpu.VMEM((tokens, model), F32),
            *[pltpu.VMEM((tokens, ff), BF16)] * inside,
            pltpu.SemaphoreType.DMA((spans + 2, most)),
        ],
    )
    if inside:
        return out
    return [*out[:6], *turned_outside([out[6]], [stream])]


def shift_back(z_of, d_of, returned, since_ref, prior, mixes, gain, bias, tokens, cols, put):
    count = len(mixes)

    def norm(z):
        centred, scale = normal(z)
        return centred * scale * gain + bias

    gone = [1.0 - m for m in mixes]

    def lost(at, rows):
        total = sum(g * d_of(n, at)[rows] for n, g in enumerate(gone))
        return jnp.where(spread(since_ref[at, :][rows], cols) == 0, 0.0, total)

    steps = tokens // STEP

    def step(i, carry):
        last, sums = carry[0], carry[1:]
        at = pl.ds(pl.multiple_of(i * STEP, STEP), STEP)
        z = z_of(at)
        now = norm(z)
        then = one_later(now, last)
        then = jnp.where(spread(since_ref[at, :], cols) == 0, 0.0, then)
        difference = now - then
        grads = [d_of(n, at) for n in range(count)]
        sums = [s + folded(difference * g) for s, g in zip(sums, grads)]
        ahead = jnp.minimum((i + 1) * STEP, tokens - STEP)
        ahead = lost(pl.ds(pl.multiple_of(ahead, STEP), 16), slice(0, 1))
        ahead = jnp.where(i == steps - 1, returned, ahead)
        d = one_earlier(lost(at, slice(None)), ahead) + sum(m * g for m, g in zip(mixes, grads))
        put(i, at, z, d)
        return (now[STEP - 1 :, :], *sums)

    zero = jnp.zeros((8, cols), F32)
    return lax.fori_loop(0, steps, step, (norm(prior), *[zero] * count))[1:]


def total(folded_sum):
    return jnp.sum(folded_sum, axis=0, keepdims=True)


def middle_back(
    d_up,
    d_gate,
    returned,
    resid,
    prior,
    slope,
    gain,
    bias,
    mixes,
    since,
    until,
    plan,
    recept,
    k,
    v,
    a,
    b,
    rate,
    boost,
):
    tokens, cols = resid.shape
    parts, copies = listed([plan])
    most = len(copies[0])

    def body(scalars, ins, outs, d_attended, gain_sum, bias_sum, w_ref, sems):
        d_up_ref, d_gate_ref, returned_ref, resid_ref, prior_ref, slope_ref = ins[:6]
        gain_ref, bias_ref, up_mix, gate_mix, since_ref, until_ref = ins[6:12]
        recept, k, v, a, b, rate_ref, boost_ref = ins[12:19]
        d_resid, d_att, d_recept, d_wkv, next_a, next_b, end_ref, vec_ref = outs
        started = copied(copies[0], ins[19:], w_ref, sems)
        start_all(recept, k, v, a, b)
        gain, boost = gain_ref[...], boost_ref[...]
        gain_sum[...] = jnp.zeros_like(gain_sum)
        bias_sum[...] = jnp.zeros_like(bias_sum)

        def put(i, at, z, d):
            n, d_z = normal_back(z, d, gain)
            gain_sum[...] += folded(d * n)
            bias_sum[...] += folded(d)
            d_z = slope_ref[at, :].astype(F32) + d_z
            d_resid.ref[at, :] = d_z
            d_att.ref[at, :] = d_z.astype(BF16)

        sums = shift_back(
            lambda at: resid_ref[at, :],
            lambda n, at: (d_up_ref, d_gate_ref)[n][at, :].astype(F32),
            returned_ref[...],
            since_ref,
            prior_ref[...],
            [up_mix[...], gate_mix[...]],
            gain,
            bias_ref[...],
            tokens,
            cols,
            put,
        )
        d_att.send()
        d_resid.send()
        vec_ref[...] = jnp.zeros_like(vec_ref)
        for n, part in enumerate([gain_sum[...], bias_sum[...], *sums]):
            vec_ref[n : n + 1, :] = total(part)
        wait_all(started)

        def back(at):
            d_attended[:, at] = across(d_att.ref[...], w_ref[at, :])

        by_columns(cols, back)
        recept_ref, k_ref, v_ref, a_ref, b_ref = [x.get() for x in (recept, k, v, a, b)]

        def step(i, carry):
            at = pl.ds(pl.multiple_of(i * STEP, STEP), STEP)
            gate, d = recept_ref[at, :], d_attended[at, :]
            bonus = jnp.exp(boost + k_ref[at, :].astype(F32))
            wkv = (a_ref[at, :] + bonus * v_ref[at, :].astype(F32)) / (b_ref[at, :] + bonus)
            low = wkv.astype(BF16).astype(F32)
            d_wkv.ref[at, :] = (d * gate).astype(BF16)
            d_recept.ref[at, :] = (d * low * gate * (1.0 - gate)).astype(BF16)
            return carry

        lax.fori_loop(0, tokens // STEP, step, 0)
        d_recept.send()
        d_wkv.send()
        scan_backward(
            rate_ref,
            boost_ref,
            k_ref,
            v_ref,
            d_wkv.ref,
            a_ref,
            b_ref,
            until_ref,
            next_a.ref,
            next_b.ref,
            end_ref,
            slice(0, cols),
        )

    low, full = ((tokens, cols), BF16, "early"), ((tokens, cols), F32, "early")
    vec = ((8, cols), F32, "now")
    return streamed(
        body,
        [],
        [
            (x, "now")
            for x in (d_up, d_gate, returned, resid, prior, slope, gain, bias, *mixes, since, until)
        ]
        + [(x, "late") for x in (recept, k, v, a, b)]
        + [(rate, "now"), (boost, "now")]
        + [(p, "raw") for p in parts],
        [
            full,
            low,
            low,
            low,
            full,
            full,
            ((lax.axis_size("seq"), 2, cols), F32, "now"),
            vec,
        ],
        [
            pltpu.VMEM((tokens, cols), F32),
            pltpu.VMEM((8, cols), F32),
            pltpu.VMEM((8, cols), F32),
            pltpu.VMEM((cols, cols), BF16),
            pltpu.SemaphoreType.DMA((most,)),
        ],
    )


def recurrence_back(back_a, back_b, heads, gap, k, v, a, b, d_wkv, until, rate, boost):
    tokens, cols = k.shape

    def body(*refs):
        back_a_ref, back_b_ref, heads_ref, gap_ref, k_ref, v_ref, a_ref, b_ref = refs[:8]
        d_ref, until_ref, rate_ref, boost_ref, d_key_ref, d_value_ref, vec_ref = refs[8:]
        rate, boost = rate_ref[...], boost_ref[...]
        from_a, from_b = carried(gap_ref, heads_ref, rate)

        def step(i, carry):
            at = pl.ds(pl.multiple_of(i * STEP, STEP), STEP)
            place = i * STEP + lax.broadcasted_iota(jnp.int32, (STEP, cols), 0)
            inside = spread(until_ref[at, :], cols) > tokens
            fade = jnp.exp(-rate * (tokens - 1 - place).astype(F32))
            fade = jnp.where(inside, fade, 0.0)
            next_a = back_a_ref[at, :] + fade * from_a
            next_b = back_b_ref[at, :] + fade * from_b
            a, b = a_ref[at, :], b_ref[at, :]
            key, value = k_ref[at, :].astype(F32), v_ref[at, :].astype(F32)
            lift, bonus = jnp.exp(key), jnp.exp(boost + key)
            ratio = bonus / (b + bonus)
            wkv = (a + bonus * value) / (b + bonus)
            ratio = ratio * d_ref[at, :].astype(F32)
            gap_value = ratio * (value - wkv)
            d_key = gap_value + lift * (value * next_a + next_b)
            d_key_ref[at, :] = d_key.astype(BF16)
            d_value_ref[at, :] = (ratio + lift * next_a).astype(BF16)
            return carry[0] + folded(next_a * a + next_b * b), carry[1] + folded(gap_value)

        zero = jnp.zeros((8, cols), F32)
        decay, first = lax.fori_loop(0, tokens // STEP, step, (zero, zero))
        vec_ref[...] = jnp.zeros_like(vec_ref)
        vec_ref[0:1, :] = -rate * jnp.exp(-rate) * total(decay)
        vec_ref[1:2, :] = total(first)

    return pl.pallas_call(
        body,
        in_specs=[VMEM] * 12,
        out_specs=[VMEM] * 3,
        out_shape=shapes_of(((tokens, cols), BF16), ((tokens, cols), BF16), ((8, cols), F32)),
        cost_estimate=SLIGHT,
        compiler_params=pltpu.CompilerParams(vmem_limit_bytes=60 << 20),
    )(back_a, back_b, heads, gap, k, v, a, b, d_wkv, until, rate, boost)


def entry_back(d_key, d_value, d_recept, plans, track, prior, gain, bias, mixes, since):
    tokens, cols = track.shape
    parts, copies = listed(plans)
    most = max(len(c) for c in copies)

    def body(*refs):
        lows, (track_ref, prior_ref, gain_ref, bias_ref) = refs[:3], refs[3:7]
        mix_refs, since_ref = refs[7:10], refs[10]
        ins, rest = refs[11 : 11 + len(parts)], refs[11 + len(parts) :]
        d_ref, row_ref, vec_ref = rest[:3]
        grads, weights, sems = rest[3:6], rest[6:9], rest[9]
        started = [
            copied(copies[n], ins, w, sems.at[n]) for n, w in enumerate(weights)
        ]
        for copies_of, low, weight, out in zip(started, lows, weights, grads):
            wait_all(copies_of)

            def one(at, low=low, weight=weight, out=out):
                out[:, at] = across(low[...], weight[at, :])

            by_columns(cols, one)

        mixes = [m[...] for m in mix_refs]

        def put(i, at, z, d):
            d_ref[at, :] = d

        sums = shift_back(
            lambda at: track_ref[at, :].astype(F32),
            lambda n, at: grads[n][at, :],
            jnp.zeros((1, cols), F32),
            since_ref,
            prior_ref[...].astype(F32),
            mixes,
            gain_ref[...],
            bias_ref[...],
            tokens,
            cols,
            put,
        )
        row = sum((1.0 - m) * g[0:1, :] for m, g in zip(mixes, grads))
        row_ref[...] = jnp.where(spread(since_ref[0:1, :], cols) == 0, 0.0, row)
        vec_ref[...] = jnp.zeros_like(vec_ref)
        for n, part in enumerate(sums):
            vec_ref[n : n + 1, :] = total(part)

    full = ((tokens, cols), F32)
    return pl.pallas_call(
        body,
        in_specs=[VMEM] * 11 + [HBM] * len(parts),
        out_specs=[VMEM] * 3,
        scratch_shapes=[pltpu.VMEM((tokens, cols), F32)] * 3
        + [pltpu.VMEM((cols, cols), BF16)] * 3
        + [pltpu.SemaphoreType.DMA((3, most))],
        out_shape=shapes_of(full, ((1, cols), F32), ((8, cols), F32)),
        cost_estimate=SLIGHT,
        compiler_params=pltpu.CompilerParams(vmem_limit_bytes=60 << 20),
    )(d_key, d_value, d_recept, track, prior, gain, bias, *mixes, since, *parts)


def first_norm_back(d_normed, returned, track, d_resid, gain):
    tokens, cols = track.shape

    def body(d_ref, returned_ref, track_ref, d_resid_ref, gain_ref, out_ref, vec_ref):
        gain = gain_ref[...]

        def step(i, carry):
            at = pl.ds(pl.multiple_of(i * STEP, STEP), STEP)
            place = i * STEP + lax.broadcasted_iota(jnp.int32, (STEP, cols), 0)
            d = d_ref[at, :] + jnp.where(place == tokens - 1, returned_ref[...], 0.0)
            n, d_z = normal_back(track_ref[at, :].astype(F32), d, gain)
            out_ref[at, :] = (d_resid_ref[at, :] + d_z).astype(BF16)
            return carry[0] + folded(d * n), carry[1] + folded(d)

        zero = jnp.zeros((8, cols), F32)
        gain_sum, bias_sum = lax.fori_loop(0, tokens // STEP, step, (zero, zero))
        vec_ref[...] = jnp.zeros_like(vec_ref)
        vec_ref[0:1, :] = total(gain_sum)
        vec_ref[1:2, :] = total(bias_sum)

    return pl.pallas_call(
        body,
        in_specs=[VMEM] * 5,
        out_specs=[VMEM] * 2,
        out_shape=shapes_of(((tokens, cols), BF16), ((8, cols), F32)),
        cost_estimate=SLIGHT,
        compiler_params=pltpu.CompilerParams(vmem_limit_bytes=60 << 20),
    )(d_normed, returned, track, d_resid, gain)


class Line:
    def __init__(self):
        self.last = None

    def hold(self, value):
        return value if self.last is None else after(value, self.last)

    def mark(self, value):
        self.last = value
        return value

    def pass_on(self, value):
        return self.mark(self.hold(value))


class Stream:
    def __init__(self, names):
        seq_bits = lax.axis_size("seq").bit_length() - 1
        fsdp_bits = lax.axis_size("fsdp").bit_length() - 1
        links = {"c": ("fsdp", 0), "x": ("fsdp", 1), "y": ("seq", 0)}
        links.update({f"z{i}": ("seq", i + 1) for i in range(seq_bits - 1)})
        for i in range(seq_bits - 1):
            if f"z{i}" not in names:
                names = [*names, f"z{i}"]
        self.links = [links[name] for name in names]
        places = [bit + (fsdp_bits if axis == "seq" else 0) for axis, bit in self.links]
        count = len(places)
        owners = 1 << count
        self.masks = [
            sum((1 - ((r >> (count - 1 - p)) & 1)) << place for p, place in enumerate(places))
            for r in range(owners)
        ]
        self.fsdp_count = lax.axis_size("fsdp")

    def order(self):
        me = lax.axis_index("seq") * self.fsdp_count + lax.axis_index("fsdp")
        return [me ^ mask for mask in self.masks]


def products(pairs, columns=None):
    pairs = [[x if isinstance(x, tuple) else (x, None) for x in p] for p in pairs]
    rows, tokens = pairs[0][0][0].shape[-2:]
    apart = columns is not None
    columns = columns or [slice(0, p[2][0].shape[-1]) for p in pairs]
    span = 1024
    tasks = [
        (n, slice(c, c + span))
        for n, window in enumerate(columns)
        for c in range(window.start, window.stop, span)
    ]
    places, widths = [], [0]
    for t, (n, _) in enumerate(tasks):
        if apart and t and tasks[t - 1][0] != n:
            widths.append(0)
        places.append((len(widths) - 1, widths[-1]))
        widths[-1] += span
    arrays, numbers = [], []
    for p in pairs:
        for array, _ in p:
            known = [n for n, other in enumerate(arrays) if other is array]
            if not known:
                arrays.append(array)
                known = [len(arrays) - 1]
            numbers.append(known[0])

    def body(scalars, ins, outs, lefts, rights, left_sems, right_sems, send, keep, out_sems):
        def source(n, q):
            ref = ins[numbers[4 * n + q]]
            lead = pairs[n][q][1]
            return ref if lead is None else ref.at[lead]

        coming, loaded = [], {}
        for t, (n, cols) in enumerate(tasks):
            if n not in loaded:
                loaded[n] = [
                    pltpu.make_async_copy(source(n, q), lefts.at[n, q], left_sems.at[n, q])
                    for q in range(2)
                ]
                start_copies(loaded[n])
            coming.append(
                [
                    pltpu.make_async_copy(
                        source(n, 2 + q).at[:, cols], rights.at[t, q], right_sems.at[t, q]
                    )
                    for q in range(2)
                ]
            )
            start_copies(coming[-1])
        going, seen = [], set()
        for t, (n, _) in enumerate(tasks):
            if n not in seen:
                wait_all(loaded[n])
                seen.add(n)
            wait_all(coming[t])
            for c in range(0, span, WIDE):
                at = slice(c, c + WIDE)
                value = jnp.dot(lefts[n, 0], rights[t, 0, :, at], preferred_element_type=F32)
                value = value + jnp.dot(
                    lefts[n, 1], rights[t, 1, :, at], preferred_element_type=F32
                )
                send[t, :, at] = value[: rows // 2].astype(BF16)
                keep[t, :, at] = value[rows // 2 :].astype(BF16)
            which, first = places[t]
            out_cols = slice(first, first + span)
            for q, (ref, out) in enumerate(((send, outs[2 * which]), (keep, outs[2 * which + 1]))):
                copy = pltpu.make_async_copy(ref.at[t], out.at[:, out_cols], out_sems.at[t, q])
                copy.start()
                going.append(copy)
        wait_all(going)

    count = len(tasks)
    return streamed(
        body,
        [],
        [(a, "raw") for a in arrays],
        [((rows // 2, width), BF16, "raw") for width in widths for _ in range(2)],
        [
            pltpu.VMEM((len(pairs), 2, rows, tokens), BF16),
            pltpu.VMEM((count, 2, tokens, span), BF16),
            pltpu.SemaphoreType.DMA((len(pairs), 2)),
            pltpu.SemaphoreType.DMA((count, 2)),
            pltpu.VMEM((count, rows // 2, span), BF16),
            pltpu.VMEM((count, rows // 2, span), BF16),
            pltpu.SemaphoreType.DMA((count, 2)),
        ],
    )


def added(groups, dtype):
    out = []
    for parts, _, rows in groups:
        out.append(sum(a[first : first + rows].astype(F32) for a, first in parts).astype(dtype))
    return jnp.concatenate(out, axis=1)


def added_by_kernel(groups, dtype):
    rows = groups[0][2]
    if rows % 16:
        return added(groups, dtype)
    entries = [(a, first, g) for g, (parts, _, _) in enumerate(groups) for a, first in parts]
    widths = [cols for _, cols, _ in groups]

    def body(scalars, ins, outs, sems, *held):
        coming = []
        for n, (_, first, g) in enumerate(entries):
            coming.append(
                pltpu.make_async_copy(ins[n].at[first : first + rows, :], held[n], sems.at[n])
            )
        start_copies(coming)
        wait_all(coming)
        at = 0
        for g, width in enumerate(widths):
            mine = [held[n] for n, entry in enumerate(entries) if entry[2] == g]

            def one(i, carry, mine=mine, at=at, width=width):
                part = pl.ds(pl.multiple_of(i * 16, 16), 16)
                value = sum(ref[part, :].astype(F32) for ref in mine)
                outs[0].ref[part, at : at + width] = value.astype(dtype)
                return carry

            lax.fori_loop(0, rows // 16, one, 0)
            at += width

    return streamed(
        body,
        [],
        [(a, "raw") for a, _, _ in entries],
        [((rows, sum(widths)), dtype, "early")],
        [pltpu.SemaphoreType.DMA((len(entries),))]
        + [pltpu.VMEM((rows, widths[g]), BF16) for _, _, g in entries],
    )[0]


class Sum:
    def __init__(self, line, stream, pairs, ready=None, wait=False):
        self.line, self.links = line, list(stream.links[1:])
        if ready is None:
            held = pairs[0][2]
            held = (line.hold(held[0]), held[1]) if isinstance(held, tuple) else line.hold(held)
            pairs[0] = (*pairs[0][:2], held, pairs[0][3])
            ready = line.mark(products(pairs))
        send, keep = ready
        self.rows, self.cols = keep.shape
        self.parts = [(keep, 0)]
        self.send = send
        if not wait:
            self.go()

    def go(self):
        self.got = flipped(self.send, *self.links.pop(0))

    def take(self):
        self.got = self.line.pass_on(self.got)

    def group(self):
        self.parts.append((self.line.hold(self.got), 0))
        if not self.links:
            return self.parts, self.cols, self.rows
        self.rows //= 2
        group = (self.parts, self.cols, self.rows)
        self.parts = [(a, first + self.rows) for a, first in self.parts]
        return group

    def step(self, add=None):
        step_together([self], add or added)

    def total(self):
        group = self.group()
        return added([group], F32)


def step_together(sums, add=added):
    groups = [s.group() for s in sums]
    links = [s.links.pop(0) for s in sums]
    send = add(groups, BF16)
    sums[0].line.mark(send)
    got = flipped(send, *links[0])
    at = 0
    for s in sums:
        s.got = got if len(sums) == 1 else got[:, at : at + s.cols]
        at += s.cols


def on_device(
    incoming_symbols,
    downstream_slope,
    sequence_extents,
    mixer_lookup_map,
    mixer_payload_map,
    mixer_accepting_map,
    mixer_emitted_map,
    feedforward_lookup_map,
    feedforward_payload_map,
    feedforward_accepting_map,
    prime_normalize_gain,
    prime_normalize_bias,
    later_normalize_gain,
    later_normalize_bias,
    mixer_lookup_shiftmix,
    mixer_payload_shiftmix,
    mixer_accepting_shiftmix,
    feedforward_lookup_shiftmix,
    feedforward_accepting_shiftmix,
    channel_shrink_rate,
    newest_boost,
):
    track, slope = incoming_symbols[0], downstream_slope[0]
    tokens, model = track.shape
    seq_count, fsdp_count = lax.axis_size("seq"), lax.axis_size("fsdp")
    seq_number = lax.axis_index("seq")
    gain_one, bias_one, gain_two, bias_two, mix_key, mix_value, mix_recept, mix_up, mix_gate = [
        v[None, :]
        for v in (
            prime_normalize_gain,
            prime_normalize_bias,
            later_normalize_gain,
            later_normalize_bias,
            mixer_lookup_shiftmix,
            mixer_payload_shiftmix,
            mixer_accepting_shiftmix,
            feedforward_lookup_shiftmix,
            feedforward_accepting_shiftmix,
        )
    ]
    boost = newest_boost[None, :]
    line = Line()
    by_x = Stream(["c", "x", "z0", "y"])
    by_yx = Stream(["c", "y", "x", "z0"])
    by_zx = Stream(["c", "z0", "x", "y"])
    by_p = Stream(["c", "y", "z0", "x"])
    by_q = Stream(["c", "x", "y", "z0"])

    rows = mixer_lookup_map.shape[0]
    down_rows = feedforward_payload_map.shape[0]
    down_half = down_rows // 2
    pairs = [[i, i + 1] for i in range(0, fsdp_count, 2)]

    def by_chip(weight):
        return lax.all_gather(weight, "fsdp", axis=0, tiled=True, axis_index_groups=pairs)

    def bit(name):
        axis, number = LINKS[name]
        return (lax.axis_index(axis) >> number) & 1

    def shard_rows(shard, size=rows, shift=None):
        def offset():
            base = (lax.axis_index("fsdp") ^ shard) * size
            return base if shift is None else base + shift()

        return offset

    def chip_rows(size=rows):
        return lambda: bit("x") * 2 * size

    half, part = rows // 2, rows // 4

    def near_y():
        return bit("y") * half

    def far_y():
        return (1 - bit("y")) * half

    quarters = [
        lambda i=i, j=j: ((bit("y") ^ i) * 2 + (bit("z0") ^ j)) * part
        for i in range(2)
        for j in range(2)
    ]

    def near_z():
        return bit("z0") * down_half

    def far_z():
        return (1 - bit("z0")) * down_half

    every = slice(0, model)
    ff = feedforward_lookup_map.shape[1]
    blocks = [slice(n, n + model) for n in range(0, ff, model)]

    own = (mixer_lookup_map, mixer_payload_map)
    away_mix = line.mark(packed([(w, near_y, half, every) for w in own]))
    got_mix = flipped(away_mix, *LINKS["x"])
    (
        lookup_chip,
        payload_chip,
        accepting_chip,
        emitted_chip,
        gate_chip,
        up_chip,
        down_chip,
    ) = [
        by_chip(line.hold(w))
        for w in (
            mixer_lookup_map,
            mixer_payload_map,
            mixer_accepting_map,
            mixer_emitted_map,
            feedforward_accepting_map,
            feedforward_lookup_map,
            feedforward_payload_map,
        )
    ]

    away_more = packed(
        [
            (w, near_y, half, every)
            for w in line.hold(
                (mixer_accepting_map, mixer_emitted_map, feedforward_accepting_map)
            )
        ]
        + [(feedforward_lookup_map, quarters[0], part, b) for b in blocks]
    )
    got_more = flipped(line.mark(away_more), *LINKS["x"])
    prior_track = line.pass_on(passed_along(line.hold(track[-1:]), "seq", 1))

    group_positions = jnp.arange(tokens * seq_count, dtype=jnp.int32)
    group_flags = token_starts(line.hold(sequence_extents)[0], group_positions)
    chunk_flags = group_flags.reshape(seq_count, tokens)
    local_flags = lax.dynamic_index_in_dim(chunk_flags, seq_number, 0, keepdims=False)
    chunk_has = jnp.any(chunk_flags, axis=1)
    chunk_first = chunk_flags[:, 0]
    places = jnp.arange(tokens, dtype=jnp.int32)
    later = places[None, :] > places[:, None]
    marked = local_flags[None, :]
    last_start = jnp.max(jnp.where(marked & ~later, places[None, :], -FAR), axis=1)
    next_start = jnp.min(jnp.where(marked & later, places[None, :], FAR), axis=1)
    since = jnp.broadcast_to((places - last_start)[:, None], (tokens, 128))
    until = jnp.broadcast_to((next_start - 1 - places)[:, None], (tokens, 128))
    order = jnp.arange(seq_count, dtype=jnp.int32)
    between = (order[None, :] > order[:, None]) & (order[None, :] < seq_number)
    reaches = (order < seq_number) & ~jnp.any(between & chunk_has[None, :], axis=1)
    gap = jnp.where(reaches, ((seq_number - 1 - order) * tokens).astype(F32), NEVER)
    gap = jnp.broadcast_to(gap[:, None], (seq_count, 128))
    above = order[None, :] > seq_number
    blocked = chunk_first[None, :] & (order[None, :] <= order[:, None])
    blocked = blocked | (chunk_has[None, :] & (order[None, :] < order[:, None]))
    comes = (order > seq_number) & ~jnp.any(blocked & above, axis=1)
    gap_back = jnp.where(comes, ((order - 1 - seq_number) * tokens).astype(F32), NEVER)
    gap_back = jnp.broadcast_to(gap_back[:, None], (seq_count, 128))
    rate = jnp.exp(channel_shrink_rate)[None, :]
    line.mark((since, until, gap, gap_back, rate))

    away_down = line.mark(
        packed([(line.hold(feedforward_payload_map), near_z, down_half, every)])
    )

    got_mix = line.pass_on(got_mix)
    other_mix = flipped(got_mix, *LINKS["y"])
    key_low, value_low, recept_low = norm_and_mix(
        track,
        line.hold(prior_track),
        gain_one,
        bias_one,
        (mix_key, mix_value, mix_recept),
        since,
        [],
        [],
    )
    line.mark(key_low)
    other_mix = line.pass_on(other_mix)
    cross_mix = flipped(line.hold(got_mix), *LINKS["c"])
    cross_other_mix = flipped(other_mix, *LINKS["c"])

    def halves(parts, w, size, near, far):
        window = slice(w * size, (w + 1) * size)
        return [
            Piece(p, shard_rows(2 + n // 2, 2 * size, (near, far)[n % 2]), (), window)
            for n, p in enumerate(parts)
        ]

    plans_kv = [
        [
            Piece((lookup_chip, payload_chip)[w], chip_rows()),
            *halves((got_mix, other_mix, cross_mix, cross_other_mix), w, half, near_y, far_y),
        ]
        for w in range(2)
    ]
    got_down = flipped(away_down, *LINKS["x"])
    k, v, part_a, part_b, ends = keys_and_values(
        line.hold(key_low), value_low, plans_kv, rate, since
    )
    line.mark(ends)
    all_ends = gathered_ends(ends)
    got_more = line.pass_on(got_more)
    got_rest = line.mark(got_more[: 3 * half])
    other_rest = flipped(got_rest, *LINKS["y"])
    got_up = line.mark(line.hold(got_more)[3 * half :])
    next_up = flipped(got_up, *LINKS["z0"])
    pair_up = line.mark(jnp.stack([got_up, line.hold(next_up)]))
    far_up = flipped(pair_up, *LINKS["y"])
    all_ends = line.pass_on(all_ends)
    got_down = line.pass_on(got_down)
    other_down = flipped(got_down, *LINKS["z0"])
    other_rest = line.pass_on(other_rest)
    cross_rest = flipped(line.hold(got_rest), *LINKS["c"])
    cross_other_rest = flipped(other_rest, *LINKS["c"])
    plan_r, plan_e, plan_gate = [
        [
            Piece(chip, chip_rows()),
            *halves((got_rest, other_rest, cross_rest, cross_other_rest), w, half, near_y, far_y),
        ]
        for w, chip in enumerate((accepting_chip, emitted_chip, gate_chip))
    ]
    recept, attended, resid, state_a, state_b, last_row = attend(
        line.hold(recept_low),
        k,
        v,
        part_a,
        part_b,
        all_ends,
        gap,
        rate,
        boost,
        since,
        track,
        [plan_r, plan_e],
    )

    prior_resid = passed_along(line.mark(last_row), "seq", 1)
    prior_resid = line.hold(prior_resid)
    (up_low, gate_low), channel_away, channel_mine = norm_and_mix(
        resid,
        prior_resid,
        gain_two,
        bias_two,
        (mix_up, mix_gate),
        since,
        [attended, key_low, value_low, recept_low],
        [(0, by_p), (5, by_p), (4, by_yx), (4, by_zx), (1, by_q), (2, by_q), (3, by_p)],
    )
    line.mark(channel_away)
    cross_up = flipped(line.hold(pair_up), *LINKS["c"])
    cross_down = flipped(line.hold(got_down), *LINKS["c"])
    far_up = line.pass_on(far_up)
    cross_far_up = flipped(far_up, *LINKS["c"])
    other_down = line.pass_on(other_down)
    cross_other_down = flipped(other_down, *LINKS["c"])
    plan_up = [Piece(up_chip, chip_rows())]
    for shard, first, pair in ((2, 0, pair_up), (2, 2, far_up), (3, 0, cross_up), (3, 2, cross_far_up)):
        for n in range(2):
            for q, block in enumerate(blocks):
                plan_up.append(
                    Piece(
                        pair,
                        shard_rows(shard, shift=quarters[first + n]),
                        (n,),
                        slice(q * part, (q + 1) * part),
                        block.start,
                    )
                )
    plan_down = [
        Piece(down_chip, chip_rows(down_rows)),
        *halves(
            (got_down, other_down, cross_down, cross_other_down), 0, down_half, near_z, far_z
        ),
    ]
    mixed, d_out, d_pre_up, d_up_in, d_gate_in, d_row, squared_away, squared_mine = (
        channel_mix(
            *line.hold((up_low, gate_low)),
            resid,
            slope,
            mix_up,
            mix_gate,
            since,
            [plan_up, plan_down, plan_gate],
            by_x,
        )
    )
    returned = passed_along(line.mark(d_row), "seq", -1)
    squared_other = flipped(squared_away, *LINKS["c"])
    d_out_other = flipped(d_out, *LINKS["c"])
    squared_other, d_out_other = line.pass_on((squared_other, d_out_other))
    channel_other = flipped(line.hold(channel_away), *LINKS["c"])
    d_pre_up_other = flipped(line.hold(d_pre_up), *LINKS["c"])
    sum_down = Sum(
        line, by_x, [((squared_mine, 0), (squared_other, 0), (d_out, 0), (d_out_other, 0))]
    )
    returned = line.pass_on(returned)
    half_ff = ff // 2
    up_keep = products(
        [
            ((channel_mine, 2 + n), (channel_other, 2 + n), line.hold(d_pre_up), d_pre_up_other)
            for n in range(2)
        ],
        [slice(n * half_ff, (n + 1) * half_ff) for n in range(2)],
    )
    line.mark(up_keep)
    sum_up = [
        Sum(line, stream, None, ready=up_keep[2 * n : 2 * n + 2])
        for n, stream in enumerate((by_yx, by_zx))
    ]

    d_resid, d_att, d_recept, d_wkv, back_a, back_b, heads, vec_two = middle_back(
        line.hold(d_up_in),
        d_gate_in,
        returned,
        resid,
        prior_resid,
        slope,
        gain_two,
        bias_two,
        (mix_up, mix_gate),
        since,
        until,
        plan_e,
        recept,
        k,
        v,
        state_a,
        state_b,
        rate,
        boost,
    )
    line.mark(heads)
    all_heads = gathered_ends(heads)
    d_att_other = flipped(d_att, *LINKS["c"])
    d_recept_other = flipped(d_recept, *LINKS["c"])
    sum_p = Sum(
        line,
        by_p,
        [
            ((channel_mine, 1), (channel_other, 1), (d_out, 1), (d_out_other, 1)),
            ((channel_mine, 0), (channel_other, 0), d_att, d_att_other),
            ((channel_mine, 6), (channel_other, 6), d_recept, d_recept_other),
        ],
        wait=True,
    )
    all_heads = line.pass_on(all_heads)
    sum_p.send = line.pass_on(sum_p.send)
    sum_p.go()
    sum_up[0].take()
    sum_up[1].take()
    d_key, d_value, vec_state = recurrence_back(
        line.hold(back_a),
        back_b,
        all_heads,
        gap_back,
        k,
        v,
        state_a,
        state_b,
        d_wkv,
        until,
        rate,
        boost,
    )
    line.mark(vec_state)
    sum_down.step(added_by_kernel)
    step_together(sum_up, added_by_kernel)
    d_key_other = flipped(line.hold(d_key), *LINKS["c"])
    d_value_other = flipped(d_value, *LINKS["c"])
    d_normed, d_first_row, vec_one = entry_back(
        line.hold(d_key),
        d_value,
        d_recept,
        [*plans_kv, plan_r],
        track,
        prior_track,
        gain_one,
        bias_one,
        (mix_key, mix_value, mix_recept),
        since,
    )
    returned_first = passed_along(line.mark(d_first_row), "seq", -1)
    sum_q = Sum(
        line,
        by_q,
        [
            ((channel_mine, 4), (channel_other, 4), d_key, d_key_other),
            ((channel_mine, 5), (channel_other, 5), d_value, d_value_other),
        ],
    )
    sum_p.step(added_by_kernel)
    sum_down.step(added_by_kernel)
    returned_first = line.pass_on(returned_first)
    sum_up[1].step(added_by_kernel)
    sum_up[0].step(added_by_kernel)
    tokens_grad, vec_first = first_norm_back(
        line.hold(d_normed), returned_first, track, d_resid, gain_one
    )
    line.mark(vec_first)
    sum_q.take()
    sum_q.step(added_by_kernel)
    sum_p.step(added_by_kernel)

    small = jnp.concatenate(
        [vec_first[:2], vec_two[:2], vec_one[:3], vec_two[2:4], vec_state[:2]], axis=0
    )
    owners = seq_count * fsdp_count
    share = model // owners
    small = small.reshape(-1, owners, share).transpose(1, 0, 2).reshape(owners, -1)
    line.mark(small)
    small = lax.all_to_all(small, BOTH, split_axis=0, concat_axis=0, tiled=True)
    step_together(sum_up)
    sums = [sum_down, sum_q, sum_p, *sum_up]
    while any(s.links for s in sums):
        for s in sums:
            if s.links:
                s.step()
    grad_up = jnp.concatenate([s.total() for s in sum_up], axis=1)
    grad_down = sum_down.total()
    grad_gate, grad_output, grad_recept = jnp.split(sum_p.total(), 3, axis=1)
    grad_key, grad_value = jnp.split(sum_q.total(), 2, axis=1)
    small = jnp.sum(line.hold(small), axis=0).reshape(-1, share)
    large = (grad_key, grad_value, grad_recept, grad_output, grad_up, grad_down, grad_gate)
    return (mixed[None], tokens_grad[None], *large, *[small[i] for i in range(11)])


def solution(mesh):
    rows = P("fsdp", None)
    tokens = P("fsdp", "seq", None)
    return jax.shard_map(
        on_device,
        mesh=mesh,
        in_specs=(tokens, tokens, *[rows] * 8, *[P()] * 11),
        out_specs=(tokens, tokens, *[P(BOTH, None)] * 7, *[P(BOTH)] * 11),
        check_vma=False,
    )
```

time: 349 us -> 322 us (0.923)
  blocking collectives: 18.2 us -> 0 us
  other arithmetic: 35.7 us -> 17.6 us
  waiting for transfers between devices: 61.5 us -> 78.9 us
  local copies, waits for them, and re-layouts: 29.6 us -> 21.7 us
  starting transfers between devices: 61 us -> 65.4 us
  Pallas kernels: 126 us -> 122 us
    all_to_all x1 -> x0, blocking collectives: 18.2 us -> none  [gathered_ends(): lax.all_to_all(copies, 'seq', split_axis=0, concat_axis=0, tiled=True)]
    convert_element_type x15 -> x6, other arithmetic: 24 us -> 7.32 us  [added(): sum((a[first:first + rows].astype(F32) for a, first in parts)).astype(dtype)]
    all_to_all x1 -> x2, waiting for transfers between devices: 0.01 us -> 11.5 us  [gathered_ends(): lax.all_to_all(copies, 'seq', split_axis=0, concat_axis=0, tiled=True)]
    ppermute x46 -> x42, waiting for transfers between devices: 46.8 us -> 53 us  [flipped(): return lax.ppermute(value, axis, [(i, i ^ 1 << bit) for i in range(count)])]
    all_to_all x1 -> x2, starting transfers between devices: 4.03 us -> 9.11 us  [gathered_ends(): lax.all_to_all(copies, 'seq', split_axis=0, concat_axis=0, tiled=True)]
    another operation x6 -> x0, local copies, waits for them, and re-layouts: 3.66 us -> none  [the longest x5 3.06 us: listed(): return (parts, jnp.stack(offsets).astype(jnp.int32), copies)]
    pallas_call x16 -> x23, Pallas kernels: 121 us -> 118 us  [the longest x16 85.8 us: streamed(): pl.pallas_call(wrapped, grid_spec=pltpu.PrefetchScalarGridSpec(num_scalar...]
    ppermute x46 -> x42, starting transfers between devices: 41.8 us -> 39.9 us  [flipped(): return lax.ppermute(value, axis, [(i, i ^ 1 << bit) for i in range(count)])]
  transfers between devices with their start and end apart: 57 -> 56, of which waited for: 14 -> 23; matrix products, arithmetic and copies ran while one was open for 15% -> 9% of each run, Pallas kernels for 29% -> 30%
where the time goes in v3:
time: 322 us; the launch traced here: 321 us
  Pallas kernels  122 us (38%)
  waiting for transfers between devices  78.9 us (25%)
  starting transfers between devices  65.4 us (20%)
  local copies, waits for them, and re-layouts  21.7 us (7%)
  other arithmetic  17.6 us (5%)
  between operations  14.9 us (5%)
    pallas_call x16, Pallas kernels, streamed(): pl.pallas_call(wrapped, grid_spec=pltpu.PrefetchScalarGridSpec(num_scalar...  85.8 us
    ppermute x42, waiting for transfers between devices, flipped(): return lax.ppermute(value, axis, [(i, i ^ 1 << bit) for i in range(count)])  53 us
    ppermute x42, starting transfers between devices, flipped(): return lax.ppermute(value, axis, [(i, i ^ 1 << bit) for i in range(count)])  39.9 us
    all_to_all x2, waiting for transfers between devices, gathered_ends(): lax.all_to_all(copies, 'seq', split_axis=0, concat_axis=0, tiled=True)  11.5 us
    ppermute x4, starting transfers between devices, passed_along(): lax.ppermute(value, axis, [(source, source + steps) for source in range(i...  11.4 us
    pallas_call x2, Pallas kernels, norm_and_mix(): pl.pallas_call(body, in_specs=[VMEM] * (5 + count + more), out_specs=[VME...  10.9 us
    pallas_call x1, Pallas kernels, entry_back(): pl.pallas_call(body, in_specs=[VMEM] * 11 + [HBM] * len(parts), out_specs...  9.56 us
    unnamed x101, local copies, waits for them, and re-layouts  9.48 us
  transfers between devices with their start and end apart: 56, of which 23 were waited for; matrix products, arithmetic and copies ran while one was open for 9% of the time, Pallas kernels for 30%

profile of v3, /device:TPU:0, one launch (start us, length us, event | category | flops | bytes accessed | tf_op | source)
XLA Modules:
  0.0 320.5 jit_solution(5063078213867938124)
XLA Ops:
  18.6 3.9 %collective-permute-start = (bf16[1,1024]{1,0:T(2,128)(2,1)S(1)}, bf16[1,1024]{1,0:T(2,128)(2,1)S(1)}, u32[]{:S(2)}, u32[]{:S(2)}) collective-permute-start(bf16[1,1024]{1,0:T(2,128)(2,1)S(1)} %slice_bitcast_fusion), channel_id=1, source_target_pairs={{0,4},{4,8},{8,12},{12,16},{16,20},{20,24},{24,28},{1,5},{5,9},{9,... | collective-permute-start | bytes 6152 | tf_op jit(solution)/shard_map/ppermute | solution.py:37
  36.0 6.7 %collective-permute-done.3.refs_6_.refs_13_ = bf16[256,1024]{1,0:T(8,128)(2,1)S(1)} collective-permute-done((bf16[256,1024]{1,0:T(8,128)(2,1)S(1)}, bf16[256,1024]{1,0:T(8,128)(2,1)S(1)}, u32[]{:S(2)}, u32[]{:S(2)}) %collective-permute-start.3) | collective-permute-done | bytes 524320 | tf_op jit(solution)/shard_map/ppermute | solution.py:31
  47.0 8.3 %shard_map.360 = (bf16[256,1024]{1,0:T(8,128)(2,1)}, bf16[256,1024]{1,0:T(8,128)(2,1)}, f32[256,1024]{1,0:T(8,128)}, f32[256,1024]{1,0:T(8,128)}, f32[8,2,1024]{2,1,0:T(2,128)}) custom-call(bf16[256,1024]{1,0:T(8,128)(2,1)} %get-tuple-element.157.refs_0_.refs_8_, bf16[256,1024]{1,0:T(8,128)(2,1)} %get-tuple-element.158.refs_1_.refs_9_, f32[1,1024]{1,0:T(1,128)} %bitcast.41, ...), custom_call_target="tpu_custom_call" | custom-call | flops 1 | bytes 1 | tf_op jit(solution)/shard_map/pallas_call | solution.py:261
  60.2 3.9 %all-to-all-start = ((f32[8,2,1024]{2,1,0:T(2,128)}), f32[8,2,1024]{2,1,0:T(2,128)S(1)}, u32[]{:S(2)}, u32[]{:S(2)}) async-start(f32[8,2,1024]{2,1,0:T(2,128)} %get-tuple-element.162), calls=%async_computation | async-start | bytes 131072 | tf_op jit(solution)/shard_map/all_to_all | solution.py:47
  64.1 6.4 %collective-permute-done.8 = bf16[256,1024]{1,0:T(8,128)(2,1)S(1)} collective-permute-done((bf16[256,1024]{1,0:T(8,128)(2,1)S(1)}, bf16[256,1024]{1,0:T(8,128)(2,1)S(1)}, u32[]{:S(2)}, u32[]{:S(2)}) %collective-permute-start.8) | collective-permute-done | bytes 524320 | tf_op jit(solution)/shard_map/ppermute | solution.py:31
  73.0 6.8 %all-to-all-done.refs_5_ = f32[8,2,1024]{2,1,0:T(2,128)S(1)} async-done(((f32[8,2,1024]{2,1,0:T(2,128)}), f32[8,2,1024]{2,1,0:T(2,128)S(1)}, u32[]{:S(2)}, u32[]{:S(2)}) %all-to-all-start) | async-done | bytes 65568 | tf_op jit(solution)/shard_map/all_to_all | solution.py:47
  84.6 7.6 %shard_map.361 = (f32[256,1024]{1,0:T(8,128)}, bf16[256,1024]{1,0:T(8,128)(2,1)}, f32[256,1024]{1,0:T(8,128)}, f32[256,1024]{1,0:T(8,128)}, f32[256,1024]{1,0:T(8,128)}, /*index=5*/f32[1,1024]{1,0:T(1,128)}) custom-call(bf16[256,1024]{1,0:T(8,128)(2,1)} %get-tuple-element.169.refs_0_.refs_10_, bf16[256,1024]{1,0:T(8,128)(2,1)} %get-tuple-element.170.refs_1_.refs_13_.refs_4_, ...), custom_call_target="tpu_custom_call" | custom-call | flops 1 | bytes 1 | tf_op jit(solution)/shard_map/pallas_call | solution.py:261
  92.2 4.7 %collective-permute-start.11 = (f32[1,1024]{1,0:T(1,128)}, f32[1,1024]{1,0:T(1,128)S(1)}, u32[]{:S(2)}, u32[]{:S(2)}) collective-permute-start(f32[1,1024]{1,0:T(1,128)} %get-tuple-element.178), channel_id=1, source_target_pairs={{0,4},{4,8},{8,12},{12,16},{16,20},{20,24},{24,28},{1,5},{5,9},{9,... | collective-permute-start | bytes 12296 | tf_op jit(solution)/shard_map/ppermute | solution.py:37
  99.6 7.1 %shard_map.362 = (bf16[256,1024]{1,0:T(8,128)(2,1)}, bf16[256,1024]{1,0:T(8,128)(2,1)}, bf16[7,512,256]{2,1,0:T(8,128)(2,1)}, bf16[7,512,256]{2,1,0:T(8,128)(2,1)}) custom-call(f32[256,1024]{1,0:T(8,128)} %get-tuple-element.177.refs_0_.refs_2_.refs_3_, f32[1,1024]{1,0:T(1,128)} %copy-done.42, f32[1,1024]{1,0:T(1,128)} %bitcast.57, f32[1,1024]{1,0:T(1,128)} %bitcast.59, ...), custom_call_target="tpu_custom_call" | custom-call | flops 1 | bytes 1 | tf_op jit(solution)/shard_map/pallas_call | solution.py:428
  107.7 4.8 %collective-permute-done.17.refs_16_ = bf16[512,1024]{1,0:T(8,128)(2,1)S(1)} collective-permute-done((bf16[512,1024]{1,0:T(8,128)(2,1)}, bf16[512,1024]{1,0:T(8,128)(2,1)S(1)}, u32[]{:S(2)}, u32[]{:S(2)}) %collective-permute-start.17) | collective-permute-done | bytes 1048608 | tf_op jit(solution)/shard_map/ppermute | solution.py:31
  115.1 20.3 %shard_map.363 = (bf16[256,1024]{1,0:T(8,128)(2,1)}, bf16[2,256,1024]{2,1,0:T(8,128)(2,1)}, bf16[256,4096]{1,0:T(8,128)(2,1)}, bf16[256,1024]{1,0:T(8,128)(2,1)}...) custom-call(bf16[256,1024]{1,0:T(8,128)(2,1)} %get-tuple-element.186, ...), custom_call_target="tpu_custom_call" | custom-call | flops 1 | bytes 1 | tf_op jit(solution)/shard_map/pallas_call | solution.py:261
  140.8 5.9 %shard_map.364 = (bf16[1024,1024]{1,0:T(8,128)(2,1)}, bf16[1024,1024]{1,0:T(8,128)(2,1)}) custom-call(bf16[1,2048,256]{2,1,0:T(8,128)(2,1)} %get-tuple-element.203.refs_0_, bf16[1,2048,256]{2,1,0:T(8,128)(2,1)} %copy-done.20, bf16[2,256,1024]{2,1,0:T(8,128)(2,1)} %get-tuple-element.221.refs_2_, bf16[2,256,1024]{2,1,0:T(8,128)(2,1)} %copy-done.7), custom_call_target="tpu_custom_call" | custom-call | flops 1 | bytes 1 | tf_op jit(solution)/shard_map/pallas_call | solution.py:261
  149.8 5.6 %collective-permute-done.21.refs_2_ = f32[1,1024]{1,0:T(1,128)S(1)} collective-permute-done((f32[1,1024]{1,0:T(1,128)S(1)}, f32[1,1024]{1,0:T(1,128)S(1)}, u32[]{:S(2)}, u32[]{:S(2)}) %collective-permute-start.21) | collective-permute-done | bytes 4128 | tf_op jit(solution)/shard_map/ppermute | solution.py:37
  156.7 5.9 %shard_map.365 = (bf16[256,2048]{1,0:T(8,128)(2,1)}, bf16[256,2048]{1,0:T(8,128)(2,1)}, bf16[256,2048]{1,0:T(8,128)(2,1)}, bf16[256,2048]{1,0:T(8,128)(2,1)}) custom-call(bf16[7,512,256]{2,1,0:T(8,128)(2,1)} %get-tuple-element.195.refs_0_, bf16[7,512,256]{2,1,0:T(8,128)(2,1)} %copy-done.1, bf16[256,4096]{1,0:T(8,128)(2,1)} %get-tuple-element.209.refs_2_.refs_4_, ...), custom_call_target="tpu_custom_call" | custom-call | flops 1 | bytes 1 | tf_op jit(solution)/shard_map/pallas_call | solution.py:261
  166.5 10.0 %shard_map.366 = (f32[256,1024]{1,0:T(8,128)}, bf16[256,1024]{1,0:T(8,128)(2,1)}, bf16[256,1024]{1,0:T(8,128)(2,1)}, bf16[256,1024]{1,0:T(8,128)(2,1)}, f32[256,...) custom-call(bf16[256,1024]{1,0:T(8,128)(2,1)} %get-tuple-element.214.refs_0_, ...), custom_call_target="tpu_custom_call" | custom-call | flops 1 | bytes 1 | tf_op jit(solution)/shard_map/pallas_call | solution.py:261
  177.1 5.2 %all-to-all-start.1 = ((f32[8,2,1024]{2,1,0:T(2,128)}), f32[8,2,1024]{2,1,0:T(2,128)S(1)}, u32[]{:S(2)}, u32[]{:S(2)}) async-start(f32[8,2,1024]{2,1,0:T(2,128)} %get-tuple-element.220), calls=%async_computation.1 | async-start | bytes 131072 | tf_op jit(solution)/shard_map/all_to_all | solution.py:47
  184.0 4.7 %shard_map.367 = (bf16[256,3072]{1,0:T(8,128)(2,1)}, bf16[256,3072]{1,0:T(8,128)(2,1)}) custom-call(bf16[7,512,256]{2,1,0:T(8,128)(2,1)} %get-tuple-element.195.refs_0_, bf16[7,512,256]{2,1,0:T(8,128)(2,1)} %copy-done.1, bf16[2,256,1024]{2,1,0:T(8,128)(2,1)} %get-tuple-element.221.refs_2_, bf16[2,256,1024]{2,1,0:T(8,128)(2,1)} %copy-done.7, ...), custom_call_target="tpu_custom_call" | custom-call | flops 1 | bytes 1 | tf_op jit(solution)/shard_map/pallas_call | solution.py:261
  188.6 4.6 %all-to-all-done.1.refs_2_ = f32[8,2,1024]{2,1,0:T(2,128)S(1)} async-done(((f32[8,2,1024]{2,1,0:T(2,128)}), f32[8,2,1024]{2,1,0:T(2,128)S(1)}, u32[]{:S(2)}, u32[]{:S(2)}) %all-to-all-start.1) | async-done | bytes 65568 | tf_op jit(solution)/shard_map/all_to_all | solution.py:47
  194.1 5.5 %shard_map.368 = (bf16[256,1024]{1,0:T(8,128)(2,1)}, bf16[256,1024]{1,0:T(8,128)(2,1)}, f32[8,1024]{1,0:T(8,128)}) custom-call(f32[256,1024]{1,0:T(8,128)} %get-tuple-element.230.refs_0_, f32[256,1024]{1,0:T(8,128)} %get-tuple-element.231.refs_1_, f32[8,2,1024]{2,1,0:T(2,128)} %copy-done.34, f32[8,128]{1,0:T(8,128)} %broadcast_in_dim.107.refs_3_, ...), custom_call_target="tpu_custom_call" | custom-call | flops 1 | bytes 1 | tf_op jit(solution)/shard_map/pallas_call | solution.py:904
  208.3 9.6 %shard_map.371 = (f32[256,1024]{1,0:T(8,128)}, f32[1,1024]{1,0:T(1,128)}, f32[8,1024]{1,0:T(8,128)}) custom-call(bf16[256,1024]{1,0:T(8,128)(2,1)} %get-tuple-element.242.refs_0_.refs_2_, bf16[256,1024]{1,0:T(8,128)(2,1)} %get-tuple-element.239.refs_1_.refs_4_, bf16[256,1024]{1,0:T(8,128)(2,1)} %get-tuple-element.223.refs_6_.refs_2_, ...), custom_call_target="tpu_custom_call" | custom-call | flops 1 | bytes 1 | tf_op jit(solution)/shard_map/pallas_call | solution.py:961
  219.2 3.8 %shard_map.372 = (bf16[256,2048]{1,0:T(8,128)(2,1)}, bf16[256,2048]{1,0:T(8,128)(2,1)}) custom-call(bf16[7,512,256]{2,1,0:T(8,128)(2,1)} %get-tuple-element.195.refs_0_, bf16[7,512,256]{2,1,0:T(8,128)(2,1)} %copy-done.1, bf16[256,1024]{1,0:T(8,128)(2,1)} %get-tuple-element.242.refs_0_.refs_2_, bf16[256,1024]{1,0:T(8,128)(2,1)} %collective-permute-done.32.refs_3_, ...), custom_call_target="tpu_custom_call" | custom-call | flops 1 | bytes 1 | tf_op jit(solution)/shard_map/pallas_call | solution.py:261
  223.1 5.2 %collective-permute-done.28 = bf16[128,4096]{1,0:T(8,128)(2,1)} collective-permute-done((bf16[128,4096]{1,0:T(8,128)(2,1)}, bf16[128,4096]{1,0:T(8,128)(2,1)}, u32[]{:S(2)}, u32[]{:S(2)}) %collective-permute-start.28) | collective-permute-done | bytes 1048608 | tf_op jit(solution)/shard_map/ppermute | solution.py:31
  254.8 4.6 %all-to-all-start.2 = ((f32[32,1,352]{2,1,0:T(1,128)}), f32[32,1,352]{2,1,0:T(1,128)S(1)}, u32[]{:S(2)}, u32[]{:S(2)}) async-start(f32[32,1,352]{2,1,0:T(1,128)} %all_to_all.19), calls=%async_computation.2 | async-start | bytes 98304 | tf_op jit(solution)/shard_map/all_to_all | solution.py:1635
  283.1 5.9 %collective-permute-done.35 = bf16[128,2048]{1,0:T(8,128)(2,1)S(1)} collective-permute-done((bf16[128,2048]{1,0:T(8,128)(2,1)}, bf16[128,2048]{1,0:T(8,128)(2,1)S(1)}, u32[]{:S(2)}, u32[]{:S(2)}) %collective-permute-start.35) | collective-permute-done | bytes 524320 | tf_op jit(solution)/shard_map/ppermute | solution.py:31
  (270 shorter events, 148.5 us)
Async XLA Ops:
  7.2 37.6 %all-gather.8.cloned.1.call-start = ((), (), s32[]{:S(2)}) async-start(), calls=%async_computation.3 | async-start | bytes 1572864 | tf_op jit(solution)/shard_map/all_gather | solution.py:1282
  9.1 35.6 %all-gather.10.cloned.1.call-start = ((), (), s32[]{:S(2)}) async-start(), calls=%async_computation.4 | async-start | bytes 1572864 | tf_op jit(solution)/shard_map/all_gather | solution.py:1282
  9.9 70.6 %all-gather.12.cloned.1.call-start = ((), (), s32[]{:S(2)}) async-start(), calls=%async_computation.5 | async-start | bytes 1572864 | tf_op jit(solution)/shard_map/all_gather | solution.py:1282
  10.6 69.8 %all-gather.14.cloned.1.call-start = ((), (), s32[]{:S(2)}) async-start(), calls=%async_computation.6 | async-start | bytes 1572864 | tf_op jit(solution)/shard_map/all_gather | solution.py:1282
  11.2 96.5 %all-gather.20.cloned.1.call-start = ((), (), s32[]{:S(2)}) async-start(), calls=%async_computation.9 | async-start | bytes 1572864 | tf_op jit(solution)/shard_map/all_gather | solution.py:1282
  11.8 96.0 %all-gather.16.cloned.1.call-start = ((), (), s32[]{:S(2)}) async-start(), calls=%async_computation.7 | async-start | bytes 6291456 | tf_op jit(solution)/shard_map/all_gather | solution.py:1282
  12.4 95.4 %all-gather.18.cloned.1.call-start = ((), (), s32[]{:S(2)}) async-start(), calls=%async_computation.8 | async-start | bytes 6291456 | tf_op jit(solution)/shard_map/all_gather | solution.py:1282
  17.8 38.4 %collective-permute-start.2 = (bf16[640,1024]{1,0:T(8,128)(2,1)}, bf16[640,1024]{1,0:T(8,128)(2,1)S(1)}, u32[]{:S(2)}, u32[]{:S(2)}) collective-permute-start(bf16[640,1024]{1,0:T(8,128)(2,1)} %shard_map.357), channel_id=1, source_target_pairs={{0,2},{1,3},{2,0},{3,1},{4,6},{5,7},{6,4},{7,5},{8,10},{9,11},{10,... | collective-permute-start | bytes 3932168 | tf_op jit(solution)/shard_map/ppermute | solution.py:31
  43.3 36.6 %collective-permute-start.7 = (bf16[512,1024]{1,0:T(8,128)(2,1)}, bf16[512,1024]{1,0:T(8,128)(2,1)}, u32[]{:S(2)}, u32[]{:S(2)}) collective-permute-start(bf16[512,1024]{1,0:T(8,128)(2,1)} %shard_map.358), channel_id=1, source_target_pairs={{0,2},{1,3},{2,0},{3,1},{4,6},{5,7},{6,4},{7,5},{8,10},{9,11},{10,... | collective-permute-start | bytes 3145736 | tf_op jit(solution)/shard_map/ppermute | solution.py:31
  58.7 21.3 %collective-permute-start.6 = (bf16[384,1024]{1,0:T(8,128)(2,1)S(1)}, bf16[384,1024]{1,0:T(8,128)(2,1)S(1)}, u32[]{:S(2)}, u32[]{:S(2)}) collective-permute-start(bf16[384,1024]{1,0:T(8,128)(2,1)S(1)} %slice.218.refs_12_.refs_18_.refs_20_), channel_id=1, source_target_pairs={{0,4},{4,0},{8,12},{12,8},{16,20},{20,16},{24,28},{28,24},{1,5},{5... | collective-permute-start | bytes 2359304 | tf_op jit(solution)/shard_map/ppermute | solution.py:31
  60.2 19.7 %all-to-all-start = ((f32[8,2,1024]{2,1,0:T(2,128)}), f32[8,2,1024]{2,1,0:T(2,128)S(1)}, u32[]{:S(2)}, u32[]{:S(2)}) async-start(f32[8,2,1024]{2,1,0:T(2,128)} %get-tuple-element.162), calls=%async_computation | async-start | bytes 131072 | tf_op jit(solution)/shard_map/all_to_all | solution.py:47
  71.6 35.1 %collective-permute-start.13 = (bf16[2,256,1024]{2,1,0:T(8,128)(2,1)}, bf16[2,256,1024]{2,1,0:T(8,128)(2,1)}, u32[]{:S(2)}, u32[]{:S(2)}) collective-permute-start(bf16[2,256,1024]{2,1,0:T(8,128)(2,1)} %pad_maximum_fusion.refs_8_), channel_id=1, source_target_pairs={{0,4},{4,0},{8,12},{12,8},{16,20},{20,16},{24,28},{28,24},{1,5},{5... | collective-permute-start | bytes 3145736 | tf_op jit(solution)/shard_map/ppermute | solution.py:31
  79.9 26.9 %collective-permute-start.12 = (bf16[512,1024]{1,0:T(8,128)(2,1)}, bf16[512,1024]{1,0:T(8,128)(2,1)}, u32[]{:S(2)}, u32[]{:S(2)}) collective-permute-start(bf16[512,1024]{1,0:T(8,128)(2,1)} %collective-permute-done.7.refs_13_), channel_id=1, source_target_pairs={{0,8},{4,12},{8,0},{12,4},{16,24},{20,28},{24,16},{28,20},{1,9},{5... | collective-permute-start | bytes 3145736 | tf_op jit(solution)/shard_map/ppermute | solution.py:31
  146.7 52.9 %collective-permute-start.27 = (bf16[1024,1024]{1,0:T(8,128)(2,1)}, bf16[1024,1024]{1,0:T(8,128)(2,1)}, u32[]{:S(2)}, u32[]{:S(2)}) collective-permute-start(bf16[1024,1024]{1,0:T(8,128)(2,1)} %get-tuple-element.205), channel_id=1, source_target_pairs={{0,2},{1,3},{2,0},{3,1},{4,6},{5,7},{6,4},{7,5},{8,10},{9,11},{10,... | collective-permute-start | bytes 6291464 | tf_op jit(solution)/shard_map/ppermute | solution.py:31
  162.5 31.6 %collective-permute-start.24 = (bf16[256,2048]{1,0:T(8,128)(2,1)}, bf16[256,2048]{1,0:T(8,128)(2,1)S(1)}, u32[]{:S(2)}, u32[]{:S(2)}) collective-permute-start(bf16[256,2048]{1,0:T(8,128)(2,1)} %get-tuple-element.210), channel_id=1, source_target_pairs={{0,4},{4,0},{8,12},{12,8},{16,20},{20,16},{24,28},{28,24},{1,5},{5... | collective-permute-start | bytes 3145736 | tf_op jit(solution)/shard_map/ppermute | solution.py:31
  165.9 28.2 %collective-permute-start.23 = (bf16[256,2048]{1,0:T(8,128)(2,1)}, bf16[256,2048]{1,0:T(8,128)(2,1)}, u32[]{:S(2)}, u32[]{:S(2)}) collective-permute-start(bf16[256,2048]{1,0:T(8,128)(2,1)} %get-tuple-element.212), channel_id=1, source_target_pairs={{0,8},{4,12},{8,0},{12,4},{16,24},{20,28},{24,16},{28,20},{1,9},{5... | collective-permute-start | bytes 3145736 | tf_op jit(solution)/shard_map/ppermute | solution.py:31
  193.3 37.2 %collective-permute-start.31 = (bf16[256,3072]{1,0:T(8,128)(2,1)}, bf16[256,3072]{1,0:T(8,128)(2,1)S(1)}, u32[]{:S(2)}, u32[]{:S(2)}) collective-permute-start(bf16[256,3072]{1,0:T(8,128)(2,1)} %get-tuple-element.227), channel_id=1, source_target_pairs={{0,4},{4,0},{8,12},{12,8},{16,20},{20,16},{24,28},{28,24},{1,5},{5... | collective-permute-start | bytes 4718600 | tf_op jit(solution)/shard_map/ppermute | solution.py:31
  205.6 22.7 %collective-permute-start.28 = (bf16[128,4096]{1,0:T(8,128)(2,1)}, bf16[128,4096]{1,0:T(8,128)(2,1)}, u32[]{:S(2)}, u32[]{:S(2)}) collective-permute-start(bf16[128,4096]{1,0:T(8,128)(2,1)} %shard_map.370), channel_id=1, source_target_pairs={{0,2},{1,3},{2,0},{3,1},{4,6},{5,7},{6,4},{7,5},{8,10},{9,11},{10,... | collective-permute-start | bytes 3145736 | tf_op jit(solution)/shard_map/ppermute | solution.py:31
  206.2 28.1 %collective-permute-start.30 = (bf16[512,1024]{1,0:T(8,128)(2,1)}, bf16[512,1024]{1,0:T(8,128)(2,1)S(1)}, u32[]{:S(2)}, u32[]{:S(2)}) collective-permute-start(bf16[512,1024]{1,0:T(8,128)(2,1)} %shard_map.369), channel_id=1, source_target_pairs={{0,8},{4,12},{8,0},{12,4},{16,24},{20,28},{24,16},{28,20},{1,9},{5... | collective-permute-start | bytes 3145736 | tf_op jit(solution)/shard_map/ppermute | solution.py:31
  217.9 19.8 %collective-permute-start.29 = (f32[1,1024]{1,0:T(1,128)}, f32[1,1024]{1,0:T(1,128)S(1)}, u32[]{:S(2)}, u32[]{:S(2)}) collective-permute-start(f32[1,1024]{1,0:T(1,128)} %get-tuple-element.241), channel_id=1, source_target_pairs={{4,0},{8,4},{12,8},{16,12},{20,16},{24,20},{28,24},{5,1},{9,5},{13... | collective-permute-start | bytes 12296 | tf_op jit(solution)/shard_map/ppermute | solution.py:37
  245.4 23.6 %collective-permute-start.34 = (bf16[256,2048]{1,0:T(8,128)(2,1)}, bf16[256,2048]{1,0:T(8,128)(2,1)S(1)}, u32[]{:S(2)}, u32[]{:S(2)}) collective-permute-start(bf16[256,2048]{1,0:T(8,128)(2,1)} %get-tuple-element.243), channel_id=1, source_target_pairs={{0,2},{1,3},{2,0},{3,1},{4,6},{5,7},{6,4},{7,5},{8,10},{9,11},{10,... | collective-permute-start | bytes 3145736 | tf_op jit(solution)/shard_map/ppermute | solution.py:31
  246.9 33.4 %collective-permute-start.40 = (bf16[128,3072]{1,0:T(8,128)(2,1)}, bf16[128,3072]{1,0:T(8,128)(2,1)}, u32[]{:S(2)}, u32[]{:S(2)}) collective-permute-start(bf16[128,3072]{1,0:T(8,128)(2,1)} %shard_map.373), channel_id=1, source_target_pairs={{0,8},{4,12},{8,0},{12,4},{16,24},{20,28},{24,16},{28,20},{1,9},{5... | collective-permute-start | bytes 2359304 | tf_op jit(solution)/shard_map/ppermute | solution.py:31
  252.8 23.9 %collective-permute-start.36 = (bf16[256,1024]{1,0:T(8,128)(2,1)}, bf16[256,1024]{1,0:T(8,128)(2,1)S(1)}, u32[]{:S(2)}, u32[]{:S(2)}) collective-permute-start(bf16[256,1024]{1,0:T(8,128)(2,1)} %shard_map.374), channel_id=1, source_target_pairs={{0,4},{4,0},{8,12},{12,8},{16,20},{20,16},{24,28},{28,24},{1,5},{5... | collective-permute-start | bytes 1572872 | tf_op jit(solution)/shard_map/ppermute | solution.py:31
  278.9 23.9 %collective-permute-start.45 = (bf16[128,1024]{1,0:T(8,128)(2,1)}, bf16[128,1024]{1,0:T(8,128)(2,1)}, u32[]{:S(2)}, u32[]{:S(2)}) collective-permute-start(bf16[128,1024]{1,0:T(8,128)(2,1)} %add_convert_fusion.1), channel_id=1, source_target_pairs={{0,16},{4,20},{8,24},{12,28},{16,0},{20,4},{24,8},{28,12},{1,17},{... | collective-permute-start | bytes 786440 | tf_op jit(solution)/shard_map/ppermute | solution.py:31
  (82 other events, 643.7 us)
Sparse Core Ops, SparseCore 0:
  9.6 11.7 all-gather.7
  22.9 10.1 all-gather.9
  34.7 11.5 all-gather.11
  47.7 10.2 all-gather.13
  59.3 10.1 all-gather.19
  71.0 15.4 all-gather.15
  88.1 15.2 all-gather.17
